TPU v7x, 32 devices: a whole 2x2x4 slice. The times are simulated.
32 devices in a mesh: dp: 8 (over z, y), mp: 4 (over x, core).
Axes of the slice: x: 2, y: 2, z: 4, core: 2. Of those that a mesh axis runs over, the one named last changes fastest.
Arguments:
- tokens_in: bfloat16 [8192, 768], P('dp'), may hold values from -6 to 6
- first_values: bfloat16 [8192, 768], P('dp', 'mp'), may hold values from -8 to 8
- skip_source: int32 [12], replicated, may hold values from 0 to 12, as said below
- grad_out: bfloat16 [8192, 768], P('dp'), may hold values from -6 to 6
- qkv_weight: float32 [768, 2304], P('dp', 'mp'), may hold values from -0.3125 to 0.3125
- proj_weight: float32 [768, 768], P('mp', 'dp'), may hold values from -0.875 to 0.875
- fc_weight: float32 [768, 3072], P('dp', 'mp'), may hold values from -0.21875 to 0.21875
- down_weight: float32 [3072, 768], P('mp', 'dp'), may hold values from -0.15625 to 0.15625
- norm_params: float32 [4, 768], P(None, 'dp'), may hold values from -0.5 to 1.5, as said below
- qkv_moment: float32 [768, 2304], P('dp', 'mp'), may hold values from -128 to 128
- proj_moment: float32 [768, 768], P('mp', 'dp'), may hold values from -20 to 20
- fc_moment: float32 [768, 3072], P('dp', 'mp'), may hold values from -32 to 32
- down_moment: float32 [3072, 768], P('mp', 'dp'), may hold values from -40 to 40
- norm_moment: float32 [4, 768], P(None, 'dp'), may hold values from -128 to 128
- qkv_second: float32 [768, 2304], P('dp', 'mp'), may hold values from 32.768 to 131.072
- proj_second: float32 [768, 768], P('mp', 'dp'), may hold values from 1.007616 to 4.01408
- fc_second: float32 [768, 3072], P('dp', 'mp'), may hold values from 2.048 to 8.192
- down_second: float32 [3072, 768], P('mp', 'dp'), may hold values from 3.44064 to 13.9264
- norm_second: float32 [4, 768], P(None, 'dp'), may hold values from 32.768 to 131.072
Outputs:
- block_out: bfloat16 [8192, 768], P(('dp', 'mp'))
- input_grad: float32 [8192, 768], P(('dp', 'mp'))
- first_grad: float32 [8192, 768], P('dp', 'mp')
- qkv_weight_out: float32 [768, 2304], P('dp', 'mp')
- qkv_moment_out: float32 [768, 2304], P('dp', 'mp')
- qkv_second_out: float32 [768, 2304], P('dp', 'mp')
- proj_weight_out: float32 [768, 768], P('mp', 'dp')
- proj_moment_out: float32 [768, 768], P('mp', 'dp')
- proj_second_out: float32 [768, 768], P('mp', 'dp')
- fc_weight_out: float32 [768, 3072], P('dp', 'mp')
- fc_moment_out: float32 [768, 3072], P('dp', 'mp')
- fc_second_out: float32 [768, 3072], P('dp', 'mp')
- down_weight_out: float32 [3072, 768], P('mp', 'dp')
- down_moment_out: float32 [3072, 768], P('mp', 'dp')
- down_second_out: float32 [3072, 768], P('mp', 'dp')
- norm_params_out: float32 [4, 768], P(None, 'dp')
- norm_moment_out: float32 [4, 768], P(None, 'dp')
- norm_second_out: float32 [4, 768], P(None, 'dp')
Inputs may be any that keep to these rules, and one draw needn't show every extreme that they name: `skip_source`: exactly 6 entries are below 12, and these are distinct; which heads reuse first-layer values is drawn. `norm_params`: rows 0 and 2 are gains, rows 1 and 3 shifts.
All inputs are finite; a program needn't handle non-finite values.
Results may differ from a plain program's by a relative error of at most 0.012.
The roundings to bfloat16 on the way count: a program that leaves them out, or rounds other values in their place, can miss the bound.
Values may be sent and summed in bfloat16 or wider, within the bound.
No kernel may reach another device: no remote copies, remote signals or barrier semaphores. Data moves between devices by JAX's collectives and lax.ppermute only.
A program may use at most 128 MiB of HBM per device.

v0:
```python
import jax
import jax.numpy as jnp
from jax import lax
from jax.sharding import PartitionSpec as P

H = 12
HD = 64
SEQ = 1024
BLOCK = 512
ADAM_STEP = 5


masked_score = -1e30


def layer_norm(values, gain, shift):
    center = values - jnp.mean(values, axis=-1, keepdims=True)
    spread = jnp.mean(center * center, axis=-1, keepdims=True)
    return center * lax.rsqrt(spread + 1e-05) * gain + shift


def gelu_tanh(values):
    return jax.nn.gelu(values, approximate=True)


def adamw(master, moment, second, grad, rate, weighted):
    moment_new = 0.9 * moment + 0.1 * grad
    second_new = 0.999 * second + 0.001 * grad * grad
    mean_hat = moment_new / (1.0 - 0.9**ADAM_STEP)
    var_hat = second_new / (1.0 - 0.999**ADAM_STEP)
    master_new = master - rate * (mean_hat / (jnp.sqrt(var_hat) + 1e-08) + weighted * master)
    return (master_new, moment_new, second_new)


def own_rows(values):
    width = values.shape[0] // lax.axis_size("mp")
    return lax.dynamic_slice_in_dim(values, lax.axis_index("mp") * width, width, 0)


def row_sum(partial_value):
    return lax.psum(partial_value, "mp")


def scores_of(query_block, keys, start):
    scale = query_block.shape[-1] ** (-0.5)
    raw = jnp.einsum("bhd,shd->hbs", query_block, keys, preferred_element_type=jnp.float32) * scale
    rows = start + lax.broadcasted_iota(jnp.int32, (query_block.shape[0], keys.shape[0]), 0)
    cols = lax.broadcasted_iota(jnp.int32, (query_block.shape[0], keys.shape[0]), 1)
    return jnp.where((cols <= rows)[None], raw, masked_score)


def attend_sequence(group):
    queries, keys, values = group
    contexts = []
    totals = []
    for block in range(queries.shape[0] // BLOCK):
        start = block * BLOCK
        query_block = queries[start : start + BLOCK]
        scores = scores_of(query_block, keys, start)
        peak = jnp.max(scores, axis=-1, keepdims=True)
        weights = jnp.exp(scores - peak)
        total = jnp.sum(weights, axis=-1, keepdims=True)
        probs = (weights / total).astype(jnp.bfloat16)
        context = jnp.einsum("hbs,shd->bhd", probs, values, preferred_element_type=jnp.float32)
        contexts.append(context.astype(jnp.bfloat16))
        totals.append(peak[..., 0] + jnp.log(total[..., 0]))
    return (jnp.concatenate(contexts, 0), jnp.concatenate(totals, 1))


def attend_back(group):
    queries, keys, values, grad_context, log_totals = group
    scale = queries.shape[-1] ** (-0.5)
    grad_queries = []
    grad_keys = jnp.zeros(keys.shape, jnp.float32)
    grad_values = jnp.zeros(values.shape, jnp.float32)
    for block in range(queries.shape[0] // BLOCK):
        start = block * BLOCK
        query_block = queries[start : start + BLOCK]
        grad_block = grad_context[start : start + BLOCK]
        scores = scores_of(query_block, keys, start)
        probs = jnp.exp(scores - log_totals[:, start : start + BLOCK, None])
        rounded = probs.astype(jnp.bfloat16)
        grad_probs = jnp.einsum(
            "bhd,shd->hbs", grad_block, values, preferred_element_type=jnp.float32
        )
        grad_values = grad_values + jnp.einsum(
            "hbs,bhd->shd", rounded, grad_block, preferred_element_type=jnp.float32
        )
        inner = jnp.sum(grad_probs * probs, axis=-1, keepdims=True)
        grad_scores = (probs * (grad_probs - inner)).astype(jnp.bfloat16)
        grad_queries.append(
            jnp.einsum("hbs,shd->bhd", grad_scores, keys, preferred_element_type=jnp.float32)
            * scale
        )
        grad_keys = (
            grad_keys
            + jnp.einsum(
                "hbs,bhd->shd", grad_scores, query_block, preferred_element_type=jnp.float32
            )
            * scale
        )
    return (jnp.concatenate(grad_queries, 0), grad_keys, grad_values)


def local(
    tokens_in,
    first_values,
    skip_source,
    grad_out,
    qkv_weight,
    proj_weight,
    fc_weight,
    down_weight,
    norm_params,
    qkv_moment,
    proj_moment,
    fc_moment,
    down_moment,
    norm_moment,
    qkv_second,
    proj_second,
    fc_second,
    down_second,
    norm_second,
):
    bf16 = jnp.bfloat16
    f32 = jnp.float32
    qkv_full, proj_full, fc_full, down_full, norm_full = (
        lax.all_gather(qkv_weight.astype(bf16), "dp", axis=0, tiled=True),
        lax.all_gather(proj_weight.astype(bf16), "dp", axis=1, tiled=True),
        lax.all_gather(fc_weight.astype(bf16), "dp", axis=0, tiled=True),
        lax.all_gather(down_weight.astype(bf16), "dp", axis=1, tiled=True),
        lax.all_gather(norm_params.astype(bf16), "dp", axis=1, tiled=True),
    )
    norm_vals = norm_full.astype(f32)
    local_heads = qkv_full.shape[1] // (3 * HD)
    sources = lax.dynamic_slice_in_dim(
        skip_source, lax.axis_index("mp") * local_heads, local_heads, 0
    )
    reuse = sources < H
    selector = sources[:, None] == jnp.arange(H, dtype=jnp.int32)[None, :]
    tokens = tokens_in.astype(f32)
    count = tokens.shape[0]
    sequences = count // SEQ
    upstream_rows = grad_out.astype(f32)
    normed_one_full, norm_back_one = jax.vjp(layer_norm, tokens, norm_vals[0], norm_vals[1])
    normed_one = normed_one_full.astype(bf16)
    mixed = (
        jnp.dot(normed_one, qkv_full, preferred_element_type=f32)
        .astype(bf16)
        .reshape(count, local_heads, 3, HD)
    )
    queries = mixed[:, :, 0]
    keys = mixed[:, :, 1]
    fresh = mixed[:, :, 2]
    every_first = lax.all_gather(first_values, "mp", axis=1, tiled=True).reshape(count, H, HD)
    chosen = jnp.einsum(
        "tgd,jg->tjd", every_first, selector.astype(bf16), preferred_element_type=f32
    ).astype(bf16)
    values = jnp.where(reuse[None, :, None], chosen, fresh)
    shape_seq = (sequences, SEQ, local_heads, HD)
    contexts, log_totals = lax.map(
        attend_sequence,
        (queries.reshape(shape_seq), keys.reshape(shape_seq), values.reshape(shape_seq)),
    )
    context = contexts.reshape(count, local_heads * HD)
    middle = tokens + row_sum(jnp.dot(context, proj_full, preferred_element_type=f32))
    normed_two_full, norm_back_two = jax.vjp(layer_norm, middle, norm_vals[2], norm_vals[3])
    normed_two = normed_two_full.astype(bf16)
    pre_act = jnp.dot(normed_two, fc_full, preferred_element_type=f32)
    activated, gelu_back = jax.vjp(gelu_tanh, pre_act)
    hidden = activated.astype(bf16)
    block_rows = (middle + row_sum(jnp.dot(hidden, down_full, preferred_element_type=f32))).astype(
        bf16
    )
    block_out = own_rows(block_rows)
    down_grad = jnp.dot(hidden.T, grad_out, preferred_element_type=f32)
    grad_hidden = jnp.dot(grad_out, down_full.T, preferred_element_type=f32)
    grad_pre = gelu_back(grad_hidden)[0].astype(bf16)
    fc_grad = jnp.dot(normed_two.T, grad_pre, preferred_element_type=f32)
    grad_two = row_sum(jnp.dot(grad_pre, fc_full.T, preferred_element_type=f32))
    grad_middle_norm, gain_two, shift_two = norm_back_two(grad_two)
    late_pair = jnp.stack([gain_two, shift_two])
    grad_middle = upstream_rows + grad_middle_norm
    grad_attn = grad_middle.astype(bf16)
    proj_grad = jnp.dot(context.T, grad_attn, preferred_element_type=f32)
    grad_context = jnp.dot(grad_attn, proj_full.T, preferred_element_type=f32).astype(bf16)
    grad_queries, grad_keys, grad_values = lax.map(
        attend_back,
        (
            queries.reshape(shape_seq),
            keys.reshape(shape_seq),
            values.reshape(shape_seq),
            grad_context.reshape(shape_seq),
            log_totals,
        ),
    )
    grad_queries = grad_queries.reshape(count, local_heads, HD)
    grad_keys = grad_keys.reshape(count, local_heads, HD)
    grad_values = grad_values.reshape(count, local_heads, HD)
    fresh_grad = jnp.where(reuse[None, :, None], 0.0, grad_values)
    reused_grad = jnp.where(reuse[None, :, None], grad_values, 0.0)
    first_part = jnp.einsum(
        "tjd,jg->tgd", reused_grad, selector.astype(f32), precision=lax.Precision.HIGHEST
    ).reshape(count, H * HD)
    grad_mixed = (
        jnp.stack([grad_queries, grad_keys, fresh_grad], axis=2)
        .astype(bf16)
        .reshape(count, local_heads * 3 * HD)
    )
    qkv_grad = jnp.dot(normed_one.T, grad_mixed, preferred_element_type=f32)
    input_part = jnp.dot(grad_mixed, qkv_full.T, preferred_element_type=f32)
    grad_one = lax.psum(input_part, "mp")
    first_grad = lax.psum_scatter(first_part, "mp", scatter_dimension=1, tiled=True)
    grad_tokens_norm, gain_one, shift_one = norm_back_one(grad_one)
    early_pair = jnp.stack([gain_one, shift_one])
    input_rows = grad_middle + grad_tokens_norm
    input_grad = own_rows(input_rows)
    norm_grad = jnp.concatenate([early_pair, late_pair], 0)
    qkv_shard, proj_shard, fc_shard, down_shard, norm_shard = (
        lax.psum_scatter(qkv_grad, "dp", scatter_dimension=0, tiled=True),
        lax.psum_scatter(proj_grad, "dp", scatter_dimension=1, tiled=True),
        lax.psum_scatter(fc_grad, "dp", scatter_dimension=0, tiled=True),
        lax.psum_scatter(down_grad, "dp", scatter_dimension=1, tiled=True),
        lax.psum_scatter(norm_grad, "dp", scatter_dimension=1, tiled=True),
    )
    qkv_new = adamw(qkv_weight, qkv_moment, qkv_second, qkv_shard, 0.06, 0.1)
    proj_new = adamw(proj_weight, proj_moment, proj_second, proj_shard, 0.15, 0.1)
    fc_new = adamw(fc_weight, fc_moment, fc_second, fc_shard, 0.04, 0.1)
    down_new = adamw(down_weight, down_moment, down_second, down_shard, 0.03, 0.1)
    norm_new = adamw(norm_params, norm_moment, norm_second, norm_shard, 0.3, 0.0)
    return (
        block_out,
        input_grad,
        first_grad,
        qkv_new[0],
        qkv_new[1],
        qkv_new[2],
        proj_new[0],
        proj_new[1],
        proj_new[2],
        fc_new[0],
        fc_new[1],
        fc_new[2],
        down_new[0],
        down_new[1],
        down_new[2],
        norm_new[0],
        norm_new[1],
        norm_new[2],
    )


def solution(mesh):
    return jax.shard_map(
        local,
        mesh=mesh,
        in_specs=(
            P("dp", None),
            P("dp", "mp"),
            P(),
            P("dp", None),
            P("dp", "mp"),
            P("mp", "dp"),
            P("dp", "mp"),
            P("mp", "dp"),
            P(None, "dp"),
            P("dp", "mp"),
            P("mp", "dp"),
            P("dp", "mp"),
            P("mp", "dp"),
            P(None, "dp"),
            P("dp", "mp"),
            P("mp", "dp"),
            P("dp", "mp"),
            P("mp", "dp"),
            P(None, "dp"),
        ),
        out_specs=(
            P(("dp", "mp"), None),
            P(("dp", "mp"), None),
            P("dp", "mp"),
            P("dp", "mp"),
            P("dp", "mp"),
            P("dp", "mp"),
            P("mp", "dp"),
            P("mp", "dp"),
            P("mp", "dp"),
            P("dp", "mp"),
            P("dp", "mp"),
            P("dp", "mp"),
            P("mp", "dp"),
            P("mp", "dp"),
            P("mp", "dp"),
            P(None, "dp"),
            P(None, "dp"),
            P(None, "dp"),
        ),
        check_vma=False,
    )
```

profile of v0, /device:TPU:0, one launch (start us, length us, event | category | flops | bytes accessed | tf_op | source)
XLA Modules:
  0.0 742.0 jit_solution(3762727616627558483)
XLA Ops:
  9.5 1.7 convert_reduce_fusion
  11.2 2.0 fusion.20
  13.3 22.3 %all-gather = bf16[8,96,4]{1,2,0:T(4,128)(2,1)S(1)} all-gather(bf16[1,96,4]{1,2,0:T(4,128)(2,1)S(1)} %convert_bitcast_fusion), channel_id=1, replica_groups=mesh['dp'=8,'mp'=4] {'dp'}, dimensions={0}, use_global_device_ids=true | all-gather | bytes 6912 | tf_op jit(solution)/shard_map/all_gather | solution.py:133
  35.7 33.3 %all_gather.20 = bf16[768,576]{1,0:T(8,128)(2,1)S(1)} all-gather(bf16[96,576]{1,0:T(8,128)(2,1)S(1)} %convert_element_type.105), channel_id=1, replica_groups=mesh['dp'=8,'mp'=4] {'dp'}, dimensions={0}, use_global_device_ids=true | all-gather | bytes 995328 | tf_op jit(solution)/shard_map/all_gather | solution.py:129
  69.0 1.4 convolution_convert_fusion
  70.9 31.1 %all_gather.21 = bf16[192,768]{0,1:T(8,128)(2,1)S(1)} all-gather(bf16[192,96]{0,1:T(8,128)(2,1)S(1)} %copy.85), channel_id=1, replica_groups=mesh['dp'=8,'mp'=4] {'dp'}, dimensions={1}, use_global_device_ids=true | all-gather | bytes 331776 | tf_op jit(solution)/shard_map/all_gather | solution.py:130
  102.4 1.4 fusion.93
  103.9 1.5 fusion.1
  105.4 1.1 copy-done
  106.5 1.4 fusion.94
  107.9 2.6 copy-done.1
  110.5 1.5 fusion
  112.1 2.8 fusion.43
  114.9 4.4 fusion.52
  119.4 1.4 fusion.51
  120.9 2.3 fusion.95
  124.2 65.1 %all-reduce.5.cloned.1.call-done = f32[1024,768]{1,0:T(8,128)} async-done(((f32[1024,768]{1,0:T(8,128)}), f32[1024,768]{1,0:T(8,128)}) %all-reduce.5.cloned.1.call-update) | async-done | bytes 3145744 | tf_op jit(solution)/shard_map/psum | solution.py:41
  189.3 2.7 fusion.91
  193.7 1.7 add_convert_fusion
  195.5 3.3 fusion.96
  198.7 1.6 copy-done.62
  200.4 3.2 fusion.82
  203.7 69.2 %reduce-scatter.17.cloned.1.call-done = f32[768,96]{0,1:T(8,128)} async-done(((f32[768,768]{0,1:T(8,128)}), f32[768,96]{0,1:T(8,128)}) %reduce-scatter.17.cloned.1.call-update) | async-done | bytes 294928 | tf_op jit(solution)/shard_map/reduce_scatter | solution.py:224
  272.9 2.4 multiply_subtract_fusion
  275.4 40.8 %all-gather.9.cloned.1.call-done = bf16[768,768]{0,1:T(8,128)(2,1)} async-done(((bf16[768,96]{0,1:T(8,128)(2,1)}), bf16[768,768]{0,1:T(8,128)(2,1)}) %all-gather.9.cloned.1.call-update) | async-done | bytes 1179664 | tf_op jit(solution)/shard_map/all_gather | solution.py:132
  316.1 5.6 fusion.19
  321.7 1.1 copy-done.63
  322.8 3.1 fusion.97
  328.1 6.2 fusion.83
  334.3 58.7 %all-reduce.7.cloned.1.call-done = f32[1024,768]{1,0:T(8,128)} async-done(((f32[1024,768]{1,0:T(8,128)}), f32[1024,768]{1,0:T(8,128)}) %all-reduce.7.cloned.1.call-update) | async-done | bytes 3145744 | tf_op jit(solution)/shard_map/psum | solution.py:41
  393.1 4.0 multiply_reduce_fusion.2
  397.2 1.5 fusion.90
  400.6 0.9 slice-done.4
  401.5 1.3 slice-done.5
  403.0 1.9 multiply_reduce_fusion.1
  405.0 1.4 multiply_convert_fusion.1
  406.4 1.1 fusion.54
  408.2 1.2 fusion.22
  409.3 1.9 multiply_reduce_fusion
  411.3 1.2 fusion.35
  413.4 1.4 multiply_convert_fusion
  414.7 1.1 fusion.53
  416.8 1.0 copy-done.14
  417.8 3.2 fusion.98
  421.1 3.5 convolution_bitcast_fusion.1
  424.9 4.9 fusion.99
  429.9 111.2 %all-reduce.9.cloned.1.call-done = (f32[1024,768]{1,0:T(8,128)}, f32[1024,768]{1,0:T(8,128)}) async-done(((f32[1024,768]{1,0:T(8,128)}, f32[1024,768]{1,0:T(8,128)}), (f32[1024,768]{1,0:T(8,128)}, f32[1024,768]{1,0:T(8,128)})) %all-reduce.9.cloned.1.call-update) | async-done | bytes 6291472 | tf_op jit(solution)/shard_map/psum | solution.py:41
  541.1 3.6 fusion.12
  544.7 0.9 copy.93
  545.8 4.9 fusion.79
  550.7 1.3 select_bitcast_fusion
  552.1 2.4 convolution_bitcast_fusion
  554.5 3.5 copy.90
  558.1 1.1 copy.92
  559.2 0.7 multiply_subtract_fusion.3
  560.7 3.1 fusion.89
  563.9 2.0 fusion.56
  565.9 2.3 dynamic-slice_add_fusion
  568.1 2.2 multiply_subtract_fusion.1
  570.3 54.8 %reduce-scatter.21.cloned.1.call-done = f32[96,4]{1,0:T(8,128)} async-done(((f32[768,4]{1,0:T(8,128)}), f32[96,4]{1,0:T(8,128)}) %reduce-scatter.21.cloned.1.call-update) | async-done | bytes 1552
  625.1 0.9 copy.94
  626.6 68.3 %reduce-scatter.13.cloned.1.call-done = f32[96,576]{1,0:T(8,128)} async-done(((f32[768,576]{1,0:T(8,128)}), f32[96,576]{1,0:T(8,128)}) %reduce-scatter.13.cloned.1.call-update) | async-done | bytes 221200 | tf_op jit(solution)/shard_map/reduce_scatter | solution.py:221
  694.9 1.9 multiply_subtract_fusion.2
  696.8 37.8 %reduce-scatter.11.cloned.1.call-done = f32[1024,192]{0,1:T(8,128)} async-done(((f32[1024,768]{0,1:T(8,128)}), f32[1024,192]{0,1:T(8,128)}) %reduce-scatter.11.cloned.1.call-update) | async-done | bytes 786448 | tf_op jit(solution)/shard_map/reduce_scatter | solution.py:214
  (204 shorter events, 14.0 us)
Async XLA Ops:
  8.0 61.0 %copy-start.2 = (bf16[1024,768]{1,0:T(8,128)(2,1)S(1)}, bf16[1024,768]{1,0:T(8,128)(2,1)}, u32[]{:S(2)}) copy-start(bf16[1024,768]{1,0:T(8,128)(2,1)} %param.19) | copy-start | bytes 4718596
  8.0 27.6 %copy-start.19 = (f32[96,576]{1,0:T(8,128)S(1)}, f32[96,576]{1,0:T(8,128)}, u32[]{:S(2)}) copy-start(f32[96,576]{1,0:T(8,128)} %param.23) | copy-start | bytes 663556
  8.0 104.0 %all-gather.5.cloned.1.call-start = ((), (), s32[]{:S(2)}) async-start(), calls=%async_computation.6 | async-start | bytes 1966080 | tf_op jit(solution)/shard_map/all_gather | solution.py:156
  8.8 180.5 %all-reduce.5.cloned.1.call-start = ((), (), s32[]{:S(2)}) async-start(), calls=%async_computation.7 | async-start | bytes 6291456 | tf_op jit(solution)/shard_map/psum | solution.py:41
  11.2 59.3 %copy-start.29 = (f32[1024]{0:T(1024)}, f32[1024]{0:T(1024)S(1)}, u32[]{:S(2)}) copy-start(f32[1024]{0:T(1024)S(1)} %broadcast_multiply_fusion.1) | copy-start | bytes 12292
  13.2 22.3 %copy-start.39 = (f32[1024]{0:T(1024)}, f32[1024]{0:T(1024)S(1)}, u32[]{:S(2)}) copy-start(f32[1024]{0:T(1024)S(1)} %fusion.20) | copy-start | bytes 12292
  13.3 57.2 %copy-start.37 = (f32[1024]{0:T(1024)}, f32[1024]{0:T(1024)S(1)}, u32[]{:S(2)}) copy-start(f32[1024]{0:T(1024)S(1)} %fusion.71) | copy-start | bytes 12292
  35.7 34.8 %copy-start.35 = (f32[768]{0:T(1024)}, f32[768]{0:T(1024)S(1)}, u32[]{:S(2)}) copy-start(f32[768]{0:T(1024)S(1)} %get-tuple-element.72) | copy-start | bytes 9220
  35.7 34.8 %copy-start.54 = (f32[768]{0:T(1024)}, f32[768]{0:T(1024)S(1)}, u32[]{:S(2)}) copy-start(f32[768]{0:T(1024)S(1)} %get-tuple-element.71) | copy-start | bytes 9220
  35.7 157.5 %copy-start.31 = (f32[768]{0:T(1024)}, f32[768]{0:T(1024)S(1)}, u32[]{:S(2)}) copy-start(f32[768]{0:T(1024)S(1)} %get-tuple-element.69) | copy-start | bytes 9220
  69.0 1.7 copy-start.60
  70.5 34.9 %copy-start.8 = (bf16[1024,576]{0,1:T(8,128)(2,1)}, bf16[1024,576]{0,1:T(8,128)(2,1)S(1)}, u32[]{:S(2)}) copy-start(bf16[1024,576]{0,1:T(8,128)(2,1)S(1)} %convolution_convert_fusion) | copy-start | bytes 3538948
  70.8 41.3 %copy-start.51 = (pred[3]{0:T(512)(128)(4,1)}, pred[3]{0:T(512)(128)(4,1)S(1)}, u32[]{:S(2)}) copy-start(pred[3]{0:T(512)(128)(4,1)S(1)} %get-tuple-element.96) | copy-start | bytes 13
  70.8 41.3 %copy-start.58 = (s32[3]{0:T(128)}, s32[3]{0:T(128)S(1)}, u32[]{:S(2)}) copy-start(s32[3]{0:T(128)S(1)} %get-tuple-element.97) | copy-start | bytes 40
  102.1 18.8 %copy-start.6 = (bf16[192,768]{0,1:T(8,128)(2,1)}, bf16[192,768]{0,1:T(8,128)(2,1)S(1)}, u32[]{:S(2)}) copy-start(bf16[192,768]{0,1:T(8,128)(2,1)S(1)} %all_gather.21) | copy-start | bytes 884740
  103.9 2.6 copy-start
  103.9 11.0 %copy-start.43 = (f32[3,512]{1,0:T(4,128)}, f32[3,512]{1,0:T(4,128)S(1)}, u32[]{:S(2)}) copy-start(f32[3,512]{1,0:T(4,128)S(1)} %get-tuple-element.101) | copy-start | bytes 18436
  106.5 8.4 %copy-start.45 = (f32[3,512]{1,0:T(4,128)}, f32[3,512]{1,0:T(4,128)S(1)}, u32[]{:S(2)}) copy-start(f32[3,512]{1,0:T(4,128)S(1)} %fusion.1) | copy-start | bytes 18436
  107.9 2.6 copy-start.1
  107.9 11.4 %copy-start.46 = (f32[3,512]{1,0:T(4,128)}, f32[3,512]{1,0:T(4,128)S(1)}, u32[]{:S(2)}) copy-start(f32[3,512]{1,0:T(4,128)S(1)} %get-tuple-element.103) | copy-start | bytes 18436
  112.0 7.3 copy-start.47
  112.1 7.3 slice-start.2
  114.9 4.5 copy-start.12
  114.9 4.5 slice-start.3
  120.9 2.4 copy-start.15
  123.2 72.2 %all-gather.7.cloned.1.call-start = ((), (), s32[]{:S(2)}) async-start(), calls=%async_computation.8 | async-start | bytes 1327104 | tf_op jit(solution)/shard_map/all_gather | solution.py:131
  124.0 148.9 %reduce-scatter.17.cloned.1.call-start = ((), (), s32[]{:S(2)}) async-start(), calls=%async_computation.14 | async-start | bytes 2654208 | tf_op jit(solution)/shard_map/reduce_scatter | solution.py:224
  195.5 4.9 copy-start.10
  198.7 1.6 copy-start.62
  203.6 112.5 %all-gather.9.cloned.1.call-start = ((), (), s32[]{:S(2)}) async-start(), calls=%async_computation.9 | async-start | bytes 1327104 | tf_op jit(solution)/shard_map/all_gather | solution.py:132
  275.3 117.8 %all-reduce.7.cloned.1.call-start = ((), (), s32[]{:S(2)}) async-start(), calls=%async_computation.10 | async-start | bytes 6291456 | tf_op jit(solution)/shard_map/psum | solution.py:41
  316.1 6.7 copy-start.61
  326.0 215.1 %all-reduce.9.cloned.1.call-start = ((), (), s32[]{:S(2)}) async-start(), calls=%async_computation.17 | async-start | bytes 12582912 | tf_op jit(solution)/shard_map/psum | solution.py:41
  393.1 4.0 copy-start.42
  393.1 4.1 copy-start.4
  393.1 4.1 copy-start.26
  393.1 4.1 copy-start.32
  393.1 4.1 copy-start.34
  398.7 2.8 slice-start.4
  398.7 4.1 slice-start.5
  399.9 5.1 copy-start.3
  399.9 3.1 copy-start.13
  404.9 3.2 slice-start
  405.0 3.2 slice-start.1
  421.0 137.1 %reduce-scatter.19.cloned.1.call-start = ((), (), s32[]{:S(2)}) async-start(), calls=%async_computation.15 | async-start | bytes 884736
  424.6 5.2 copy-start.49
  424.6 5.3 copy-start.48
  424.6 116.5 %copy-start.30 = (f32[1024]{0:T(1024)S(1)}, f32[1024]{0:T(1024)}, u32[]{:S(2)}) copy-start(f32[1024]{0:T(1024)} %copy-done.29) | copy-start | bytes 12292
  424.6 116.5 %copy-start.36 = (f32[768]{0:T(1024)S(1)}, f32[768]{0:T(1024)}, u32[]{:S(2)}) copy-start(f32[768]{0:T(1024)} %copy-done.35) | copy-start | bytes 9220
  424.6 116.5 %copy-start.38 = (f32[1024]{0:T(1024)S(1)}, f32[1024]{0:T(1024)}, u32[]{:S(2)}) copy-start(f32[1024]{0:T(1024)} %copy-done.37) | copy-start | bytes 12292
  424.6 143.5 %reduce-scatter.15.cloned.1.call-start = ((), (), s32[]{:S(2)}) async-start(), calls=%async_computation.13 | async-start | bytes 2654208 | tf_op jit(solution)/shard_map/reduce_scatter | solution.py:223
  429.8 116.0 %copy-start.55 = (f32[768]{0:T(1024)S(1)}, f32[768]{0:T(1024)}, u32[]{:S(2)}) copy-start(f32[768]{0:T(1024)} %copy-done.54) | copy-start | bytes 9220
  429.8 195.3 %reduce-scatter.21.cloned.1.call-start = ((), (), s32[]{:S(2)}) async-start(), calls=%async_computation.16 | async-start | bytes 442368
  545.7 5.0 copy-start.53
  545.7 149.2 %reduce-scatter.13.cloned.1.call-start = ((), (), s32[]{:S(2)}) async-start(), calls=%async_computation.12 | async-start | bytes 2211840 | tf_op jit(solution)/shard_map/reduce_scatter | solution.py:221
  550.7 184.0 %reduce-scatter.11.cloned.1.call-start = ((), (), s32[]{:S(2)}) async-start(), calls=%async_computation.11 | async-start | bytes 3932160 | tf_op jit(solution)/shard_map/reduce_scatter | solution.py:214
  558.1 1.9 copy-start.40
  563.7 4.4 copy-start.16
  563.8 62.1 %copy-start.50 = (f32[4,96]{1,0:T(4,128)S(1)}, f32[4,96]{1,0:T(4,128)}, u32[]{:S(2)}) copy-start(f32[4,96]{1,0:T(4,128)} %param.27) | copy-start | bytes 4612
  563.8 62.1 %copy-start.56 = (f32[4,96]{1,0:T(4,128)S(1)}, f32[4,96]{1,0:T(4,128)}, u32[]{:S(2)}) copy-start(f32[4,96]{1,0:T(4,128)} %param.32) | copy-start | bytes 4612
  563.9 62.1 %copy-start.57 = (f32[4,96]{1,0:T(4,128)S(1)}, f32[4,96]{1,0:T(4,128)}, u32[]{:S(2)}) copy-start(f32[4,96]{1,0:T(4,128)} %param.37) | copy-start | bytes 4612
  565.8 129.1 %copy-start.20 = (f32[96,576]{1,0:T(8,128)S(1)}, f32[96,576]{1,0:T(8,128)}, u32[]{:S(2)}) copy-start(f32[96,576]{1,0:T(8,128)} %param.23) | copy-start | bytes 663556
  565.8 129.1 %copy-start.23 = (f32[96,576]{1,0:T(8,128)S(1)}, f32[96,576]{1,0:T(8,128)}, u32[]{:S(2)}) copy-start(f32[96,576]{1,0:T(8,128)} %param.28) | copy-start | bytes 663556
  565.9 129.1 %copy-start.24 = (f32[96,576]{1,0:T(8,128)S(1)}, f32[96,576]{1,0:T(8,128)}, u32[]{:S(2)}) copy-start(f32[96,576]{1,0:T(8,128)} %param.33) | copy-start | bytes 663556
  (18 other events, 20.6 us)
Sparse Core Ops, SparseCore 0:
  10.4 22.3 all-gather.4
  123.3 65.9 all-reduce.4
  326.1 66.9 all-reduce.6
  421.1 119.9 all-reduce.8
Sparse Core Ops, SparseCore 1:
  126.5 38.9 all-gather.6
  203.7 69.1 reduce-scatter.16
  275.5 40.5 all-gather.8
  425.7 62.8 reduce-scatter.18
  492.4 68.4 reduce-scatter.14
  564.5 60.5 reduce-scatter.20
  628.9 66.0 reduce-scatter.12
  697.9 36.7 reduce-scatter.10
where the time goes:
time: 746 us; the launch traced here: 742 us
  waiting for transfers between devices  507 us (68%)
  blocking collectives  86.7 us (12%)
  matrix products  65.9 us (9%)
  other arithmetic  44.8 us (6%)
  local copies, waits for them, and re-layouts  20.3 us (3%)
  between operations  16.5 us (2%)
    psum x3, waiting for transfers between devices, row_sum(): return lax.psum(partial_value, 'mp')  235 us
    reduce_scatter x1, waiting for transfers between devices, local(): lax.psum_scatter(down_grad, 'dp', scatter_dimension=1, tiled=True)  69.2 us
    reduce_scatter x1, waiting for transfers between devices, local(): lax.psum_scatter(qkv_grad, 'dp', scatter_dimension=0, tiled=True)  68.3 us
    unnamed x14, waiting for transfers between devices  55.7 us
    all_gather x1, waiting for transfers between devices, local(): lax.all_gather(down_weight.astype(bf16), 'dp', axis=1, tiled=True)  40.8 us
    reduce_scatter x1, waiting for transfers between devices, local(): lax.psum_scatter(first_part, 'mp', scatter_dimension=1, tiled=True)  37.8 us
    all_gather x1, blocking collectives, local(): lax.all_gather(qkv_weight.astype(bf16), 'dp', axis=0, tiled=True)  33.3 us
    all_gather x1, blocking collectives, local(): lax.all_gather(proj_weight.astype(bf16), 'dp', axis=1, tiled=True)  31.1 us
  transfers between devices with their start and end apart: 12, of which 8 were waited for; matrix products, arithmetic and copies ran while one was open for 9% of the time, Pallas kernels for 0%

commit v1 on v0

v1 whole, which is shorter than its diff:
```python
import functools

import jax
import jax.numpy as jnp
import numpy as np
from jax import lax
from jax.experimental import pallas as pl
from jax.experimental.pallas import tpu as pltpu
from jax.sharding import PartitionSpec as P

H = 12
HD = 64
ADAM_STEP = 5
EPS = 1e-05
MASKED = -1e30
RB = 256
LANES = 128
RING = (0, 2, 4, 6, 7, 5, 3, 1)
OFFSETS = (0, -1, -2, -3, -4, 1, 2, 3)
GELU_A = 0.7978845608028654
GELU_B = 0.044715

bf16 = jnp.bfloat16
f32 = jnp.float32


def dot(a, b):
    return jnp.dot(a, b, preferred_element_type=f32)


def dot_nt(a, b):
    return lax.dot_general(a, b, (((1,), (1,)), ((), ())), preferred_element_type=f32)


def dot_tn(a, b):
    return lax.dot_general(a, b, (((0,), (0,)), ((), ())), preferred_element_type=f32)


def call(kernel, name, grid, scalars, ins, outs, flops, moved, scratch=(), exps=0, vmem=32):
    def spec(shape, given):
        if given is not None:
            return given
        return pl.BlockSpec(shape, lambda *_: (0,) * len(shape))

    return pl.pallas_call(
        kernel,
        grid_spec=pltpu.PrefetchScalarGridSpec(
            num_scalar_prefetch=len(scalars),
            grid=grid,
            in_specs=[spec(a.shape, s) for a, s in ins],
            out_specs=[spec(sh, s) for sh, _, s in outs],
            scratch_shapes=list(scratch),
        ),
        out_shape=[jax.ShapeDtypeStruct(sh, dt) for sh, dt, _ in outs],
        compiler_params=pltpu.CompilerParams(
            dimension_semantics=("arbitrary",) * len(grid), vmem_limit_bytes=vmem * 1024 * 1024
        ),
        cost_estimate=pl.CostEstimate(flops=flops, bytes_accessed=moved, transcendentals=exps),
        name=name,
    )(*scalars, *[a for a, _ in ins])


def assemble(info, pieces, target, lanes=None):
    rows = target.shape[0] // len(pieces)
    for k, piece in enumerate(pieces):
        at = pl.multiple_of(info[4 + k] * rows, rows)
        target[pl.ds(at, rows), :] = piece[...] if lanes is None else piece[:, lanes[0] : lanes[1]]


def norm_stats(values):
    center = values - jnp.mean(values, axis=-1, keepdims=True)
    scale = lax.rsqrt(jnp.mean(center * center, axis=-1, keepdims=True) + EPS)
    return center * scale, scale


def selection(sources, owner, heads, of_rows):
    width = heads * HD
    rows = lax.broadcasted_iota(jnp.int32, (width, width), 0)
    cols = lax.broadcasted_iota(jnp.int32, (width, width), 1)
    held, user = (cols, rows) if of_rows else (rows, cols)
    source = jnp.full((width, width), H, jnp.int32)
    for j in range(heads):
        source = jnp.where(user // HD == j, sources[j], source)
    hit = (owner * heads + held // HD == source) & (rows % HD == cols % HD)
    return jnp.where(hit, 1.0, 0.0).astype(bf16)


def qkv_kernel(n, heads, info, src, x_ref, f0, f1, f2, f3, *refs):
    pieces, (a1_ref, m_ref, v_ref, w_ref, norm_ref) = refs[:n], refs[n:]
    cols = m_ref.shape[1]

    @pl.when(pl.program_id(0) == 0)
    def _():
        assemble(info, pieces, w_ref)
        base = cols // LANES * LANES
        turned = w_ref[:, base : base + LANES].astype(f32).T
        norm_ref[...] = turned[cols - base : cols - base + 8]

    unit, _ = norm_stats(x_ref[...].astype(f32))
    a1 = (unit * norm_ref[0:1] + norm_ref[1:2]).astype(bf16)
    a1_ref[...] = a1
    mixed = dot(a1, w_ref[:, :cols]).astype(bf16)
    m_ref[...] = mixed
    mp = info[2]
    sources = [src[mp * heads + j] for j in range(heads)]
    chosen = jnp.zeros(v_ref.shape, f32)
    for r, first in enumerate((f0, f1, f2, f3)):
        chosen += dot(first[...], selection(sources, mp ^ r, heads, False))
    lane = lax.broadcasted_iota(jnp.int32, v_ref.shape, 1) // HD
    reuse = jnp.zeros(v_ref.shape, jnp.int32)
    for j in range(heads):
        reuse = jnp.where(lane == j, jnp.where(sources[j] < H, 1, 0), reuse)
    fresh = jnp.concatenate(
        [mixed[:, (3 * j + 2) * HD : (3 * j + 3) * HD].astype(f32) for j in range(heads)], 1
    )
    v_ref[...] = jnp.where(reuse == 1, chosen, fresh).astype(bf16)


def masked_tile():
    keys = lax.broadcasted_iota(jnp.int32, (RB, RB), 0)
    queries = lax.broadcasted_iota(jnp.int32, (RB, RB), 1)
    return keys <= queries


def attend_kernel(heads, base, m_ref, v_ref, c_ref, lse_ref):
    keep = masked_tile()
    blocks = c_ref.shape[0] // RB
    turned = [[None] * heads for _ in range(blocks)]
    lse_ref[...] = jnp.zeros(lse_ref.shape, f32)
    for h in range(heads):
        keys = m_ref[:, (3 * h + 1) * HD : (3 * h + 2) * HD]
        values_t = v_ref[:, h * HD : (h + 1) * HD].T
        for i in range(blocks):
            lo = base + i * RB
            hi = lo + RB
            query = m_ref[lo:hi, 3 * h * HD : (3 * h + 1) * HD] * bf16(HD**-0.5)
            diag = jnp.where(keep, dot_nt(keys[lo:hi], query), MASKED)
            peak = jnp.max(diag, 0, keepdims=True)
            if lo:
                left = dot_nt(keys[:lo], query)
                peak = jnp.maximum(peak, jnp.max(left, 0, keepdims=True))
            diag = jnp.exp(diag - peak)
            total = jnp.sum(diag, 0, keepdims=True)
            if lo:
                left = jnp.exp(left - peak)
                total += jnp.sum(left, 0, keepdims=True)
            inverse = 1.0 / total
            context = dot(values_t[:, lo:hi], (diag * inverse).astype(bf16))
            if lo:
                context += dot(values_t[:, :lo], (left * inverse).astype(bf16))
            turned[i][h] = context
            lse_ref[h : h + 1, i * RB : (i + 1) * RB] = peak + jnp.log(total)
    for i in range(blocks):
        c_ref[i * RB : (i + 1) * RB] = jnp.concatenate(turned[i], 0).T.astype(bf16)


def mlp_kernel(n, info, x_ref, e_ref, norm_ref, c0, c1, c2, c3, wpc_ref, *refs):
    fused, down = refs[:n], refs[n : 2 * n]
    (a2_ref, g_ref, du_ref, dsend, dkeep, ysend, ykeep, rkeep, nacc, wp_out) = refs[2 * n : 2 * n + 10]
    wf, wd, w2, w1, w3 = refs[2 * n + 10 :]
    w0 = wp_out
    step = pl.program_id(0)
    hid, cw = wf.shape[1], w0.shape[1]

    @pl.when(step == 0)
    def _():
        assemble(info, fused, wf, (0, hid))
        assemble(info, fused, w0, (hid, hid + cw))
        assemble(info, fused, w2, (hid + cw, hid + 2 * cw))
        rows = wf.shape[0] // n
        for k in range(n):
            at = pl.multiple_of(info[4 + k] * rows, rows)
            w1[pl.ds(at, rows), :] = wpc_ref[k * rows : (k + 1) * rows, :cw]
            w3[pl.ds(at, rows), :] = wpc_ref[k * rows : (k + 1) * rows, cw:]
        assemble(info, down, wd)
        nacc[...] = jnp.zeros(nacc.shape, f32)

    resid = x_ref[...].astype(f32) + (
        (dot_nt(c0[...], w0[...]) + dot_nt(c1[...], w1[...]))
        + (dot_nt(c2[...], w2[...]) + dot_nt(c3[...], w3[...]))
    )
    unit, _ = norm_stats(resid)
    a2 = (unit * norm_ref[2:3] + norm_ref[3:4]).astype(bf16)
    a2_ref[...] = a2
    u = dot(a2, wf[...])
    square = u * u
    t = jnp.tanh(GELU_A * u * (1.0 + GELU_B * square))
    g = (0.5 * u * (1.0 + t)).astype(bf16)
    slope = 0.5 * (1.0 + t) + 0.5 * u * (1.0 - t * t) * (GELU_A * (1.0 + 3.0 * GELU_B * square))
    g_ref[...] = g
    du = (dot(e_ref[...], wd[...]) * slope).astype(bf16)
    du_ref[...] = du
    grad = dot_nt(du, wf[...])
    out = dot_nt(g, wd[...])
    nacc[2:3] += jnp.sum(grad * unit, 0, keepdims=True)
    nacc[3:4] += jnp.sum(grad, 0, keepdims=True)

    @pl.when(step == 0)
    def _():
        dsend[...] = grad.astype(bf16)
        ysend[...] = out.astype(bf16)

    @pl.when(step == 1)
    def _():
        dkeep[...] = grad
        ykeep[...] = out
        rkeep[...] = resid


def mlp_grad_kernel(a2a, a2b, dua, dub, ea, eb, ga, gb, out):
    hid = dua.shape[1]
    out[:, :hid] = (dot_tn(a2a[...], dua[...]) + dot_tn(a2b[...], dub[...])).astype(bf16)
    out[:, hid:] = (dot_tn(ea[...], ga[...]) + dot_tn(eb[...], gb[...])).astype(bf16)


def norm_back(unit, scale, gain, grad):
    dy = grad * gain
    return scale * (
        dy - jnp.mean(dy, -1, keepdims=True) - unit * jnp.mean(dy * unit, -1, keepdims=True)
    )


def norm_two_kernel(info, r_ref, own, received, e_ref, norm_ref, dr_ref, ab_ref):
    unit, scale = norm_stats(r_ref[...])
    grad = own[...].astype(f32) + received[...].astype(f32)
    dr = e_ref[...].astype(f32) + norm_back(unit, scale, norm_ref[2:3], grad)
    dr_ref[...] = dr
    ab_ref[...] = dr.astype(bf16)


def attend_back_kernel(heads, base, last, info, src, m_ref, v_ref, own, part, wp, lse_ref, *refs):
    if last:
        dqa, dka, dva, ab_ref, dm_ref, dvr_ref = refs
    else:
        ab_ref, dq_ref, dk_ref, dv_ref = refs
    keep = masked_tile()
    core = info[0]
    rows = 2 * RB
    blocks = 2
    at = pl.multiple_of(core * RB, RB)
    ab_ref[pl.ds(at, RB), :] = own[...]
    at = pl.multiple_of((1 - core) * RB, RB)
    ab_ref[pl.ds(at, RB), :] = part[...]
    tiles = (base + rows) // RB
    dctx = [dot(ab_ref[i * RB : (i + 1) * RB], wp[...]).astype(bf16) for i in range(blocks)]
    dq_t = [[None] * heads for _ in range(blocks)]
    dks, dvs = [], []
    for h in range(heads):
        keys = m_ref[:, (3 * h + 1) * HD : (3 * h + 2) * HD]
        keys_t = keys.T
        values = v_ref[:, h * HD : (h + 1) * HD]
        dk = [None] * tiles
        dv = [None] * tiles
        for i in range(blocks):
            lo = base + i * RB
            count = lo // RB + 1
            query = m_ref[lo : lo + RB, 3 * h * HD : (3 * h + 1) * HD] * bf16(HD**-0.5)
            dc = dctx[i][:, h * HD : (h + 1) * HD]
            lse = lse_ref[h : h + 1, i * RB : (i + 1) * RB]
            probs, dprobs = [], []
            inner = jnp.zeros((1, RB), f32)
            for t in range(count):
                spot = slice(t * RB, (t + 1) * RB)
                score = dot_nt(keys[spot], query)
                prob = jnp.exp(score - lse)
                if t == count - 1:
                    prob = jnp.where(keep, prob, 0.0)
                dprob = dot_nt(values[spot], dc)
                inner += jnp.sum(prob * dprob, 0, keepdims=True)
                more = dot(prob.astype(bf16), dc)
                dv[t] = more if dv[t] is None else dv[t] + more
                probs.append(prob)
                dprobs.append(dprob)
            total = None
            for t in range(count):
                spot = slice(t * RB, (t + 1) * RB)
                ds = (probs[t] * (dprobs[t] - inner)).astype(bf16)
                more = dot(ds, query)
                dk[t] = more if dk[t] is None else dk[t] + more
                more = dot(keys_t[:, spot], ds)
                total = more if total is None else total + more
            dq_t[i][h] = total * HD**-0.5
        dks.append(dk)
        dvs.append(dv)
    dq = [jnp.concatenate(dq_t[i], 0).T for i in range(blocks)]
    if not last:
        for i in range(blocks):
            dq_ref[i * RB : (i + 1) * RB] = dq[i]
        for t in range(tiles):
            dk_ref[t * RB : (t + 1) * RB] = jnp.concatenate([dks[h][t] for h in range(heads)], 1)
            dv_ref[t * RB : (t + 1) * RB] = jnp.concatenate([dvs[h][t] for h in range(heads)], 1)
        return
    mp = info[2]
    fresh = [jnp.where(src[mp * heads + h] < H, 0.0, 1.0) for h in range(heads)]
    reuse = [jnp.where(src[mp * heads + h] < H, 1.0, 0.0) for h in range(heads)]
    for t in range(tiles):
        spot = slice(t * RB, (t + 1) * RB)
        first = t * RB < base
        parts, reused = [], []
        for h in range(heads):
            lane = slice(h * HD, (h + 1) * HD)
            dqh = dqa[spot, lane] if first else dq[t - base // RB][:, lane]
            dkh = dks[h][t] + dka[spot, lane] if first else dks[h][t]
            dvh = dvs[h][t] + dva[spot, lane] if first else dvs[h][t]
            parts += [dqh, dkh, dvh * fresh[h]]
            reused.append(dvh * reuse[h])
        pad = dm_ref.shape[1] - 3 * HD * heads
        parts.append(jnp.zeros((RB, pad), f32))
        dm_ref[spot, :] = jnp.concatenate(parts, 1).astype(bf16)
        dvr_ref[spot, :] = jnp.concatenate(reused, 1).astype(bf16)


def input_kernel(info, dm_ref, w_ref, x_ref, na, nb, send, keep, norm_out):
    step = pl.program_id(0)

    @pl.when(step == 0)
    def _():
        norm_out[...] = na[...] + nb[...]

    grad = dot_nt(dm_ref[...], w_ref[...])
    unit, _ = norm_stats(x_ref[...].astype(f32))
    norm_out[0:1] += jnp.sum(grad * unit, 0, keepdims=True)
    norm_out[1:2] += jnp.sum(grad, 0, keepdims=True)

    @pl.when(step < 2)
    def _():
        send[...] = grad.astype(bf16)

    @pl.when(step >= 2)
    def _():
        keep[...] = grad


def qkv_grad_kernel(cols, a1_ref, dm_ref, aba, abb, ca, cb, norm_ref, out):
    width = dm_ref.shape[1]
    base = cols // LANES * LANES
    grad = dot_tn(a1_ref[...], dm_ref[...])
    rows = norm_ref.shape[1]
    turned = jnp.concatenate(
        [jnp.zeros((cols - base, rows), f32), norm_ref[...], jnp.zeros((LANES - 8 - cols + base, rows), f32)], 0
    ).T
    out[:, :base] = grad[:, :base].astype(bf16)
    out[:, base:width] = (grad[:, base:] + turned).astype(bf16)
    out[:, width:] = (dot_tn(aba[...], ca[...]) + dot_tn(abb[...], cb[...])).astype(bf16)


def norm_one_kernel(info, x_ref, own, received, dra, drb, norm_ref, out):
    unit, scale = norm_stats(x_ref[...].astype(f32))
    grad = own[...] + received[...].astype(f32)
    dr = jnp.where(info[1] == 0, dra[...], drb[...])
    out[...] = dr + norm_back(unit, scale, norm_ref[0:1], grad)


def first_kernel(heads, info, src, d0, d1, d2, d3, out):
    mp = info[2]
    total = jnp.zeros(out.shape, f32)
    for r, ref in enumerate((d0, d1, d2, d3)):
        sources = [src[(mp ^ r) * heads + j] for j in range(heads)]
        total += dot(ref[...], selection(sources, mp, heads, True))
    out[...] = total


def swap_core(value):
    return lax.ppermute(value, "mp", [(i, i ^ 1) for i in range(4)])


def swap_x(value):
    return lax.ppermute(value, "mp", [(i, i ^ 2) for i in range(4)])


def gather_four(value):
    across = swap_x(value)
    return [value, swap_core(value), across, swap_core(across)]


FORWARD = [(RING[i], RING[(i + 1) % 8]) for i in range(8)]
BACKWARD = [(b, a) for a, b in FORWARD]


def gather_ring(piece):
    if lax.axis_size("dp") != len(RING):
        return [lax.all_gather(piece, "dp", axis=0, tiled=True)]
    ahead, behind = [], []
    a = b = piece
    for k in range(4):
        a = lax.ppermute(a, "dp", FORWARD)
        ahead.append(a)
        if k < 3:
            b = lax.ppermute(b, "dp", BACKWARD)
            behind.append(b)
    return [piece] + ahead + behind


def scatter_ring(full, info):
    n = lax.axis_size("dp")
    if n != len(RING):
        return lax.psum_scatter(full.astype(f32), "dp", scatter_dimension=0, tiled=True)
    rows = full.shape[0] // n

    def part(offset):
        at = info[4 + OFFSETS.index(offset)] * rows
        return lax.dynamic_slice_in_dim(full, at, rows, 0)

    a, b = part(-4), part(-3)
    for k in (3, 2, 1, 0):
        a = lax.ppermute(a, "dp", FORWARD)
        if k:
            a = (a.astype(f32) + part(k).astype(f32)).astype(bf16)
            b = lax.ppermute(b, "dp", BACKWARD)
            if k > 1:
                b = (b.astype(f32) + part(1 - k).astype(f32)).astype(bf16)
    return a.astype(f32) + b.astype(f32) + part(0).astype(f32)


def after(value, *others):
    return lax.optimization_barrier((value,) + others)[0]


def adamw(master, moment, second, grad, rate, weighted):
    moment_new = 0.9 * moment + 0.1 * grad
    second_new = 0.999 * second + 0.001 * grad * grad
    mean_hat = moment_new / (1.0 - 0.9**ADAM_STEP)
    var_hat = second_new / (1.0 - 0.999**ADAM_STEP)
    master_new = master - rate * (mean_hat / (jnp.sqrt(var_hat) + 1e-08) + weighted * master)
    return (master_new, moment_new, second_new)


def device_table(n):
    table = np.zeros((n * 4, 16), np.int32)
    for dp in range(n):
        for mp in range(4):
            table[dp * 4 + mp, :3] = (mp % 2, mp // 2, mp)
            if n == len(RING):
                at = RING.index(dp)
                for k, offset in enumerate(OFFSETS):
                    table[dp * 4 + mp, 4 + k] = RING[(at + offset) % n]
    return table


def local(
    tokens_in,
    first_values,
    skip_source,
    grad_out,
    qkv_weight,
    proj_weight,
    fc_weight,
    down_weight,
    norm_params,
    qkv_moment,
    proj_moment,
    fc_moment,
    down_moment,
    norm_moment,
    qkv_second,
    proj_second,
    fc_second,
    down_second,
    norm_second,
):
    n = lax.axis_size("dp")
    pieces = n if n == len(RING) else 1
    count, width = tokens_in.shape
    cols = qkv_weight.shape[1]
    heads = cols // (3 * HD)
    cw = heads * HD
    hid = fc_weight.shape[1]
    wide = -(-(cols + 4) // LANES) * LANES
    half = count // 2
    me = lax.axis_index("dp") * 4 + lax.axis_index("mp")
    info = lax.dynamic_slice_in_dim(jnp.asarray(device_table(n)), me, 1, 0)[0]
    src = skip_source

    shard = qkv_weight.shape[0]
    ring_one = jnp.concatenate(
        [
            qkv_weight.astype(bf16),
            norm_params.T.astype(bf16),
            jnp.zeros((shard, wide - cols - 4), bf16),
        ],
        1,
    )
    one = gather_ring(ring_one)
    firsts = gather_four(first_values)
    proj_t = proj_weight.T.astype(bf16)
    proj_pair = jnp.concatenate([proj_t, swap_x(proj_t)], 1)
    ring_two = jnp.concatenate([fc_weight.astype(bf16), proj_pair], 1)
    ring_two = after(ring_two, one[-1])
    two = gather_ring(ring_two)
    ring_three = after(down_weight.T.astype(bf16), two[len(two) // 8])
    three = gather_ring(ring_three)
    proj_other = swap_core(jnp.concatenate([p[:, hid:] for p in two], 0))

    row = lambda w: pl.BlockSpec((RB, w), lambda i, *_: (i, 0))
    a1, mixed, values, qkv_full, norms = call(
        functools.partial(qkv_kernel, pieces, heads),
        "qkv",
        (count // RB,),
        (info, src),
        [(tokens_in, row(width))] + [(f, row(cw)) for f in firsts] + [(p, None) for p in one],
        [
            ((count, width), bf16, row(width)),
            ((count, cols), bf16, row(cols)),
            ((count, cw), bf16, row(cw)),
            ((width, wide), bf16, None),
            ((8, width), f32, None),
        ],
        flops=2 * count * width * cols,
        moved=2 * count * (2 * width + 2 * cols),
    )

    def attend(part):
        keys = (part + 1) * half
        top = lambda w: pl.BlockSpec((keys, w), lambda i: (0, 0))
        return call(
            functools.partial(attend_kernel, heads, part * half),
            f"attend{part}",
            (1,),
            (),
            [(mixed, top(cols)), (values, top(cw))],
            [((half, cw), bf16, None), ((8, half), f32, None)],
            flops=4 * half * keys * 256 * heads,
            moved=2 * keys * (cols + cw),
            exps=half * keys * heads,
        )

    context, lse = zip(*[attend(part) for part in range(2)])
    contexts = [gather_four(c) for c in context]

    def mlp(part):
        block = lambda w: pl.BlockSpec((RB, w), lambda i, s: ((1 - s[0]) ^ i, 0))
        whole = lambda w: pl.BlockSpec((RB, w), lambda i, s: (2 * part + ((1 - s[0]) ^ i), 0))
        weights = lambda w: pltpu.VMEM((width, w), bf16)
        return call(
            functools.partial(mlp_kernel, pieces),
            f"mlp{part}",
            (2,),
            (info,),
            [(tokens_in, whole(width)), (grad_out, whole(width)), (norms, None)]
            + [(c, block(cw)) for c in contexts[part]]
            + [(proj_other, None)]
            + [(p, None) for p in two]
            + [(p, None) for p in three],
            [
                ((half, width), bf16, block(width)),
                ((half, hid), bf16, block(hid)),
                ((half, hid), bf16, block(hid)),
                ((RB, width), bf16, None),
                ((RB, width), f32, None),
                ((RB, width), bf16, None),
                ((RB, width), f32, None),
                ((RB, width), f32, None),
                ((8, width), f32, None),
                ((width, cw), bf16, None),
            ],
            flops=2 * half * width * (width + 4 * hid),
            moved=2 * half * width * 8 + 2 * width * 3 * hid,
            exps=half * hid,
            scratch=[weights(hid), weights(hid), weights(cw), weights(cw), weights(cw)],
            vmem=40,
        )

    a2, act, dpre, dsend, dkeep, ysend, ykeep, rkeep, nacc, wp_own = zip(
        *[mlp(part) for part in range(2)]
    )

    grads_r, grads_b = [], []
    for part in range(2):
        mine = (dkeep[part] + swap_core(dsend[part]).astype(f32)).astype(bf16)
        other = swap_x(mine)
        dr, ab = call(
            norm_two_kernel,
            f"norm_two{part}",
            (1,),
            (info,),
            [
                (rkeep[part], None),
                (mine, None),
                (other, None),
                (grad_out, pl.BlockSpec((RB, width), lambda i, s, part=part: (2 * part + s[0], 0))),
                (norms, None),
            ],
            [((RB, width), f32, None), ((RB, width), bf16, None)],
            flops=0,
            moved=RB * width * 16,
        )
        grads_r.append(dr)
        grads_b.append((ab, swap_core(ab)))

    turn = lambda: pl.BlockSpec((half, RB), lambda j: (0, j))
    down_half = lambda part: pl.BlockSpec((half, RB), lambda j: (part, j))
    (mlp_grad,) = call(
        mlp_grad_kernel,
        "mlp_grad",
        (width // RB,),
        (),
        [(a2[0], turn()), (a2[1], turn()), (dpre[0], None), (dpre[1], None)]
        + [(grad_out, down_half(0)), (grad_out, down_half(1)), (act[0], None), (act[1], None)],
        [((width, 2 * hid), bf16, pl.BlockSpec((RB, 2 * hid), lambda j: (j, 0)))],
        flops=4 * count * width * hid,
        moved=2 * (4 * count * width + 2 * width * hid),
    )
    mlp_shard = scatter_ring(mlp_grad, info)

    low = lax.axis_index("mp") < 2

    def to_rows(keep, received):
        sums = [k + r.astype(f32) for k, r in zip(keep, received)]
        mine = jnp.where(low, sums[0], sums[1])
        sent = jnp.where(low, sums[1], sums[0]).astype(bf16)
        return mine, swap_x(sent)

    mine, received = to_rows(ykeep, [swap_core(y) for y in ysend])
    block_out = (jnp.where(low, rkeep[0], rkeep[1]) + mine + received.astype(f32)).astype(bf16)

    def attend_back(part, before):
        keys = (part + 1) * half
        top = lambda w: pl.BlockSpec((keys, w), lambda i, *_: (0, 0))
        outs = [((half, width), bf16, None)]
        if part:
            outs += [((count, wide), bf16, None), ((count, cw), bf16, None)]
        else:
            outs += [((half, cw), f32, None)] * 3
        return call(
            functools.partial(attend_back_kernel, heads, part * half, bool(part)),
            f"attend_back{part}",
            (1,),
            (info, src),
            [(mixed, top(cols)), (values, top(cw)), (grads_b[part][0], None), (grads_b[part][1], None)]
            + [(wp_own[0], None), (lse[part], None)]
            + [(v, None) for v in before],
            outs,
            flops=10 * half * keys * 256 * heads,
            moved=2 * keys * (cols + cw) * 3,
            exps=half * keys * heads,
        )

    ab_one, dq, dk, dv = attend_back(0, [])
    ab_two, dmixed, dreused = attend_back(1, [dq, dk, dv])

    order = lambda i, s: 2 * (i % 2) + ((1 - s[0]) ^ (i // 2))
    spread = lambda w: pl.BlockSpec((RB, w), lambda i, s: (order(i, s), 0))
    isend, ikeep, norm_grad = call(
        input_kernel,
        "input",
        (4,),
        (info,),
        [(dmixed, spread(wide)), (qkv_full, None), (tokens_in, spread(width)), (nacc[0], None), (nacc[1], None)],
        [
            ((half, width), bf16, pl.BlockSpec((RB, width), lambda i, s: (jnp.minimum(i, 1), 0))),
            ((half, width), f32, pl.BlockSpec((RB, width), lambda i, s: (jnp.maximum(i - 2, 0), 0))),
            ((8, width), f32, None),
        ],
        flops=2 * count * width * wide,
        moved=2 * count * (wide + 3 * width),
    )
    (qkv_grad,) = call(
        functools.partial(qkv_grad_kernel, cols),
        "qkv_grad",
        (width // RB,),
        (),
        [
            (a1, pl.BlockSpec((count, RB), lambda j: (0, j))),
            (dmixed, None),
            (ab_one, turn()),
            (ab_two, turn()),
            (context[0], None),
            (context[1], None),
            (norm_grad, pl.BlockSpec((8, RB), lambda j: (0, j))),
        ],
        [((width, wide + cw), bf16, pl.BlockSpec((RB, wide + cw), lambda j: (j, 0)))],
        flops=2 * count * width * (wide + cw),
        moved=2 * count * (2 * width + wide + cw),
    )
    qkv_shard = scatter_ring(qkv_grad, info)
    theirs = swap_core(isend)
    mine, received = to_rows((ikeep[:RB], ikeep[RB:]), (theirs[:RB], theirs[RB:]))
    (input_grad,) = call(
        norm_one_kernel,
        "norm_one",
        (1,),
        (info,),
        [
            (tokens_in, pl.BlockSpec((RB, width), lambda i, s: (s[2], 0))),
            (mine, None),
            (received, None),
            (grads_r[0], None),
            (grads_r[1], None),
            (norms, None),
        ],
        [((RB, width), f32, None)],
        flops=0,
        moved=RB * width * 20,
    )
    (first_grad,) = call(
        functools.partial(first_kernel, heads),
        "first",
        (count // RB,),
        (info, src),
        [(d, row(cw)) for d in gather_four(dreused)],
        [((count, cw), f32, row(cw))],
        flops=8 * count * cw * cw,
        moved=count * cw * 12,
    )

    norm_part = qkv_shard[:, cols : cols + 4].T
    norm_part = norm_part + swap_core(norm_part)
    norm_part = norm_part + swap_x(norm_part)

    fc_new = adamw(fc_weight, fc_moment, fc_second, mlp_shard[:, :hid], 0.04, 0.1)
    down_new = adamw(down_weight, down_moment, down_second, mlp_shard[:, hid:].T, 0.03, 0.1)
    qkv_new = adamw(qkv_weight, qkv_moment, qkv_second, qkv_shard[:, :cols], 0.06, 0.1)
    proj_new = adamw(proj_weight, proj_moment, proj_second, qkv_shard[:, wide:].T, 0.15, 0.1)
    norm_new = adamw(norm_params, norm_moment, norm_second, norm_part, 0.3, 0.0)
    return (block_out, input_grad, first_grad) + qkv_new + proj_new + fc_new + down_new + norm_new


def solution(mesh):
    both = P("dp", "mp")
    turned = P("mp", "dp")
    rows = P("dp", None)
    every = P(None, "dp")
    state = (both, turned, both, turned, every)
    return jax.shard_map(
        local,
        mesh=mesh,
        in_specs=(rows, both, P(), rows) + state * 3,
        out_specs=(P(("dp", "mp"), None), P(("dp", "mp"), None), both)
        + (both,) * 3
        + (turned,) * 3
        + (both,) * 3
        + (turned,) * 3
        + (every,) * 3,
        check_vma=False,
    )
```

time: 746 us -> 249 us (0.33)
  waiting for transfers between devices: 507 us -> 37.8 us
  blocking collectives: 86.7 us -> 0 us
  matrix products: 65.9 us -> 0 us
  Pallas kernels: 0 us -> 59.6 us
  starting transfers between devices: 0.9 us -> 54.4 us
  local copies, waits for them, and re-layouts: 20.3 us -> 59.8 us
  other arithmetic: 44.8 us -> 28.9 us
  between operations: 16.5 us -> 6.62 us
    psum x3 -> x0, waiting for transfers between devices: 235 us -> none  [row_sum(): return lax.psum(partial_value, 'mp')]
    reduce_scatter x4 -> x0, waiting for transfers between devices: 175 us -> none  [the longest x1 69.2 us: local(): lax.psum_scatter(down_grad, 'dp', scatter_dimension=1, tiled=True)]
    all_gather x3 -> x0, blocking collectives: 86.7 us -> none  [the longest x1 33.3 us: local(): lax.all_gather(qkv_weight.astype(bf16), 'dp', axis=0, tiled=True)]
    dot_general x25 -> x0, matrix products: 62.4 us -> none  [the longest x1 6.24 us: local(): jnp.dot(hidden, down_full, preferred_element_type=f32)]
    pallas_call x0 -> x14, Pallas kernels: none -> 59.6 us  [call(): pl.pallas_call(kernel, grid_spec=pltpu.PrefetchScalarGridSpec(num_scalar_...]
    unnamed x14 -> x0, waiting for transfers between devices: 55.7 us -> none
    ppermute x0 -> x62, starting transfers between devices: none -> 54.4 us  [the longest x12 18 us: gather_ring(): a = lax.ppermute(a, 'dp', FORWARD)]
    all_gather x3 -> x0, waiting for transfers between devices: 40.8 us -> none  [the longest x1 40.8 us: local(): lax.all_gather(down_weight.astype(bf16), 'dp', axis=1, tiled=True)]
  transfers between devices with their start and end apart: 12 -> 62, of which waited for: 8 -> 18; matrix products, arithmetic and copies ran while one was open for 9% -> 23% of each run, Pallas kernels for 0% -> 18%
where the time goes in v1:
time: 249 us; the launch traced here: 247 us
  local copies, waits for them, and re-layouts  59.8 us (24%)
  Pallas kernels  59.6 us (24%)
  starting transfers between devices  54.4 us (22%)
  waiting for transfers between devices  37.8 us (15%)
  other arithmetic  28.9 us (12%)
  between operations  6.62 us (3%)
    pallas_call x14, Pallas kernels, call(): pl.pallas_call(kernel, grid_spec=pltpu.PrefetchScalarGridSpec(num_scalar_...  59.6 us
    unnamed x211, local copies, waits for them, and re-layouts  50.9 us
    ppermute x12, starting transfers between devices, gather_ring(): a = lax.ppermute(a, 'dp', FORWARD)  18 us
    ppermute x12, waiting for transfers between devices, gather_ring(): a = lax.ppermute(a, 'dp', FORWARD)  15.1 us
    ppermute x8, starting transfers between devices, scatter_ring(): a = lax.ppermute(a, 'dp', FORWARD)  11.1 us
    ppermute x10, starting transfers between devices, swap_x(): return lax.ppermute(value, 'mp', [(i, i ^ 2) for i in range(4)])  9.25 us
    ppermute x10, waiting for transfers between devices, swap_x(): return lax.ppermute(value, 'mp', [(i, i ^ 2) for i in range(4)])  8.24 us
    ppermute x9, starting transfers between devices, gather_ring(): b = lax.ppermute(b, 'dp', BACKWARD)  8.12 us
  transfers between devices with their start and end apart: 62, of which 18 were waited for; matrix products, arithmetic and copies ran while one was open for 23% of the time, Pallas kernels for 18%

profile of v1, /device:TPU:0, one launch (start us, length us, event | category | flops | bytes accessed | tf_op | source)
XLA Modules:
  0.0 247.1 jit_solution(11931024674830935228)
XLA Ops:
  2.6 3.1 %collective-permute-start.3 = (bf16[96,640]{1,0:T(8,128)(2,1)S(1)}, bf16[96,640]{1,0:T(8,128)(2,1)S(1)}, u32[]{:S(2)}, u32[]{:S(2)}) collective-permute-start(bf16[96,640]{1,0:T(8,128)(2,1)S(1)} %maximum_maximum_fusion.refs_0_), channel_id=1, source_target_pairs={{0,8},{8,16},{16,24},{24,28},{28,20},{20,12},{12,4},{4,0},{1,9},{9... | collective-permute-start | bytes 368648 | tf_op jit(solution)/shard_map/ppermute | solution.py:386
  7.0 2.0 collective-permute-start.1
  9.0 1.6 copy.68
  10.6 1.6 collective-permute-start.4
  12.6 1.5 convert_bitcast_fusion.1
  14.4 1.7 collective-permute-done.4.refs_2_
  16.1 1.6 collective-permute-start.5
  18.1 1.6 convert_bitcast_fusion.refs_8_
  19.8 1.6 convert_element_type.171
  23.7 1.9 collective-permute-start.14
  25.8 1.8 collective-permute-start.6
  28.3 3.8 %collective-permute-done.14.refs_1_ = bf16[96,1152]{1,0:T(8,128)(2,1)S(1)} collective-permute-done((bf16[96,1152]{1,0:T(8,128)(2,1)S(1)}, bf16[96,1152]{1,0:T(8,128)(2,1)S(1)}, u32[]{:S(2)}, u32[]{:S(2)}) %collective-permute-start.14) | collective-permute-done | bytes 221216 | tf_op jit(solution)/shard_map/ppermute | solution.py:386
  32.1 1.8 collective-permute-start.15
  34.8 3.6 %collective-permute-done.15.refs_2_ = bf16[96,1152]{1,0:T(8,128)(2,1)S(1)} collective-permute-done((bf16[96,1152]{1,0:T(8,128)(2,1)S(1)}, bf16[96,1152]{1,0:T(8,128)(2,1)S(1)}, u32[]{:S(2)}, u32[]{:S(2)}) %collective-permute-start.15) | collective-permute-done | bytes 221216 | tf_op jit(solution)/shard_map/ppermute | solution.py:386
  38.3 1.6 collective-permute-start.16
  40.6 4.1 %collective-permute-done.16.refs_3_ = bf16[96,1152]{1,0:T(8,128)(2,1)S(1)} collective-permute-done((bf16[96,1152]{1,0:T(8,128)(2,1)S(1)}, bf16[96,1152]{1,0:T(8,128)(2,1)S(1)}, u32[]{:S(2)}, u32[]{:S(2)}) %collective-permute-start.16) | collective-permute-done | bytes 221216 | tf_op jit(solution)/shard_map/ppermute | solution.py:386
  44.8 1.8 collective-permute-start.17
  47.3 1.6 collective-permute-start.22
  48.8 1.9 collective-permute-done.17.refs_4_
  50.7 1.8 collective-permute-start.20
  55.1 1.5 collective-permute-done.20.refs_7_
  58.7 1.8 collective-permute-start.26
  62.6 5.3 %qkv.1 = (bf16[1024,768]{1,0:T(8,128)(2,1)S(1)}, bf16[1024,576]{1,0:T(8,128)(2,1)S(1)}, bf16[1024,192]{1,0:T(8,128)(2,1)S(1)}, bf16[768,640]{1,0:T(8,128)(2,1)S(1)}, f32[8,768]{1,0:T(8,128)S(1)}) custom-call(s32[16]{0:T(128)S(1)} %get-tuple-element.175.info, s32[12]{0:T(128)S(1)} %copy-done.56, bf16[1024,768]{1,0:T(8,128)(2,1)S(1)} %copy-done.1, ...), custom_call_target="tpu_custom_call" | custom-call | flops 905969664 | bytes 5505024 | tf_op jit(solution)/shard_map/qkv/pallas_call | solution.py:45
  69.1 1.8 attend0.1
  71.0 1.8 collective-permute-start.11
  72.8 1.5 collective-permute-start.27
  74.9 4.6 %attend1.1 = (bf16[512,192]{1,0:T(8,128)(2,1)}, f32[8,512]{1,0:T(8,128)S(1)}) custom-call(bf16[1024,576]{1,0:T(8,128)(2,1)S(1)} %get-tuple-element.63.m_ref, bf16[1024,192]{1,0:T(8,128)(2,1)S(1)} %get-tuple-element.64.v_ref), custom_call_target="tpu_custom_call" | custom-call | flops 1610612736 | bytes 1572864 | tf_op jit(solution)/shard_map/attend1/pallas_call | solution.py:45
  81.2 1.8 collective-permute-start.28
  85.0 3.8 %collective-permute-done.30.c2 = bf16[512,192]{1,0:T(8,128)(2,1)} collective-permute-done((bf16[512,192]{1,0:T(8,128)(2,1)}, bf16[512,192]{1,0:T(8,128)(2,1)}, u32[]{:S(2)}, u32[]{:S(2)}) %collective-permute-start.30) | collective-permute-done | bytes 196640 | tf_op jit(solution)/shard_map/ppermute | solution.py:368
  101.5 8.8 %mlp0.1 = (bf16[512,768]{1,0:T(8,128)(2,1)S(1)}, bf16[512,768]{1,0:T(8,128)(2,1)S(1)}, bf16[512,768]{1,0:T(8,128)(2,1)S(1)}, bf16[256,768]{1,0:T(8,128)(2,1)S(1)...) custom-call(s32[16]{0:T(128)S(1)} %get-tuple-element.175.info, ...), custom_call_target="tpu_custom_call" | custom-call | flops 3019898880 | bytes 9830400 | tf_op jit(solution)/shard_map/mlp0/pallas_call | solution.py:45
  114.4 8.8 %mlp1.1 = (bf16[512,768]{1,0:T(8,128)(2,1)S(1)}, bf16[512,768]{1,0:T(8,128)(2,1)S(1)}, bf16[512,768]{1,0:T(8,128)(2,1)S(1)}, bf16[256,768]{1,0:T(8,128)(2,1)S(1)...) custom-call(s32[16]{0:T(128)S(1)} %get-tuple-element.175.info, ...), custom_call_target="tpu_custom_call" | custom-call | flops 3019898880 | bytes 9830400 | tf_op jit(solution)/shard_map/mlp1/pallas_call | solution.py:45
  123.3 3.3 %mlp_grad.1 = bf16[768,1536]{1,0:T(8,128)(2,1)S(1)} custom-call(bf16[512,768]{1,0:T(8,128)(2,1)S(1)} %get-tuple-element.100.a2a, bf16[512,768]{1,0:T(8,128)(2,1)S(1)} %get-tuple-element.101.a2b, bf16[512,768]{1,0:T(8,128)(2,1)S(1)} %get-tuple-element.102.dua, bf16[512,768]{1,0:T(8,128)(2,1)S(1)} %get-tuple-element.103.dub, bf16[1024,768]{1,0:T(8,128)(2,1)S(1)} %copy-done, ...), custom_call_target="tpu_custom_call" | custom-call | flops 2415919104 | bytes 8650752 | tf_op jit(solution)/shard_map/mlp_grad/pallas_call | solution.py:45
  129.0 1.6 collective-permute-start.53
  138.2 1.5 collective-permute-start.57
  141.7 1.9 add_convert_fusion.1.own
  144.3 2.5 collective-permute-done.57
  147.3 1.9 collective-permute-done.54
  149.2 2.0 add_convert_fusion.6
  151.2 1.6 collective-permute-start.55
  153.2 1.6 copy.69
  154.8 1.6 copy.70
  158.6 1.8 select_convert_fusion.1
  161.0 2.2 norm_two1.1
  164.4 2.1 norm_two0.1
  166.8 1.8 add_convert_fusion.5
  170.8 3.7 %attend_back0.1 = (bf16[512,768]{1,0:T(8,128)(2,1)S(1)}, f32[512,192]{1,0:T(8,128)S(1)}, f32[512,192]{1,0:T(8,128)S(1)}, f32[512,192]{1,0:T(8,128)S(1)}) custom-call(s32[16]{0:T(128)S(1)} %get-tuple-element.175.info, s32[12]{0:T(128)S(1)} %copy-done.56, bf16[1024,576]{1,0:T(8,128)(2,1)S(1)} %copy-done.58, bf16[1024,192]{1,0:T(8,128)(2,1)S(1)} %copy-done.60, ...), custom_call_target="tpu_custom_call" | custom-call | flops 2013265920 | bytes 2359296 | tf_op jit(solution)/shard_map/attend_back0/pallas_call | solution.py:45
  174.6 6.1 %attend_back1.1 = (bf16[512,768]{1,0:T(8,128)(2,1)S(1)}, bf16[1024,640]{1,0:T(8,128)(2,1)S(1)}, bf16[1024,192]{1,0:T(8,128)(2,1)S(1)}) custom-call(s32[16]{0:T(128)S(1)} %get-tuple-element.175.info, s32[12]{0:T(128)S(1)} %copy-done.56, bf16[1024,576]{1,0:T(8,128)(2,1)S(1)} %copy-done.58, bf16[1024,192]{1,0:T(8,128)(2,1)S(1)} %copy-done.60, ...), custom_call_target="tpu_custom_call" | custom-call | flops 4026531840 | bytes 4718592 | tf_op jit(solution)/shard_map/attend_back1/pallas_call | solution.py:45
  180.7 3.0 %input.1 = (bf16[512,768]{1,0:T(8,128)(2,1)S(1)}, f32[512,768]{1,0:T(8,128)S(1)}, f32[8,768]{1,0:T(8,128)S(1)}) custom-call(s32[16]{0:T(128)S(1)} %get-tuple-element.175.info, bf16[1024,640]{1,0:T(8,128)(2,1)S(1)} %get-tuple-element.87.dm_ref, bf16[768,640]{1,0:T(8,128)(2,1)S(1)} %copy-done.15, bf16[1024,768]{1,0:T(8,128)(2,1)S(1)} %copy-done.1, ...), custom_call_target="tpu_custom_call" | custom-call | flops 1006632960 | bytes 6029312 | tf_op jit(solution)/shard_map/input/pallas_call | solution.py:45
  184.9 3.5 %qkv_grad.1 = bf16[768,832]{1,0:T(8,128)(2,1)S(1)} custom-call(bf16[1024,768]{1,0:T(8,128)(2,1)S(1)} %copy-done.12, bf16[1024,640]{1,0:T(8,128)(2,1)S(1)} %get-tuple-element.87.dm_ref, bf16[512,768]{1,0:T(8,128)(2,1)S(1)} %get-tuple-element.97.aba, bf16[512,768]{1,0:T(8,128)(2,1)S(1)} %get-tuple-element.98.abb, bf16[512,192]{1,0:T(8,128)(2,1)S(1)} %copy-done.29, ...), custom_call_target="tpu_custom_call" | custom-call | flops 1308622848 | bytes 4849664 | tf_op jit(solution)/shard_map/qkv_grad/pallas_call | solution.py:45
  188.4 1.6 collective-permute-start.46
  190.1 2.1 add_convert_fusion.2
  192.7 1.9 collective-permute-done.46
  194.6 1.6 collective-permute-start.47
  198.0 2.1 collective-permute-done.47
  200.2 1.6 collective-permute-start.48
  205.7 1.9 collective-permute-done.51
  208.5 1.6 collective-permute-start.49
  211.7 2.9 %collective-permute-done.44.d2 = bf16[1024,192]{1,0:T(8,128)(2,1)S(1)} collective-permute-done((bf16[1024,192]{1,0:T(8,128)(2,1)S(1)}, bf16[1024,192]{1,0:T(8,128)(2,1)S(1)}, u32[]{:S(2)}, u32[]{:S(2)}) %collective-permute-start.44) | collective-permute-done | bytes 393248 | tf_op jit(solution)/shard_map/ppermute | solution.py:368
  217.7 1.6 copy.80
  219.3 1.6 copy.81
  220.9 1.6 copy.82
  224.7 2.5 %select_convert_fusion = (bf16[256,768]{1,0:T(8,128)(2,1)}, f32[256,768]{1,0:T(8,128)S(1)}) fusion(f32[512,768]{1,0:T(8,128)} %copy-done.13, pred[]{:T(512)S(6)} %lt.38, bf16[512,768]{1,0:T(8,128)(2,1)} %collective-permute-done.41), kind=kLoop, calls=%fused_computation | loop fusion | flops 1376256 | bytes 3538945 | tf_op jit(solution)/shard_map/convert_element_type | solution.py:610
  237.2 3.5 %first.1 = f32[1024,192]{1,0:T(8,128)S(1)} custom-call(s32[16]{0:T(128)S(1)} %get-tuple-element.175.info, s32[12]{0:T(128)S(1)} %copy-done.56, bf16[1024,192]{1,0:T(8,128)(2,1)S(1)} %copy-done.24, bf16[1024,192]{1,0:T(8,128)(2,1)} %collective-permute-done.43.d1, bf16[1024,192]{1,0:T(8,128)(2,1)S(1)} %copy-done.26, bf16[1024,192]{1,0:T(8,128)(2,1)} %collective-permute-done.45.d3), custom_call_target="tpu_custom_call" | custom-call | flops 301989888 | bytes 2359296 | tf_op jit(solution)/shard_map/first/pallas_call | solution.py:45
  244.1 3.0 %norm_one.1 = f32[256,768]{1,0:T(8,128)} custom-call(s32[16]{0:T(128)S(1)} %get-tuple-element.175.info, bf16[1024,768]{1,0:T(8,128)(2,1)S(1)} %copy-done.1, f32[256,768]{1,0:T(8,128)S(1)} %get-tuple-element.165.own, bf16[256,768]{1,0:T(8,128)(2,1)} %collective-permute-done.42.received, f32[256,768]{1,0:T(8,128)S(1)} %copy-done.22, ...), custom_call_target="tpu_custom_call" | custom-call | bytes 3932160 | tf_op jit(solution)/shard_map/norm_one/pallas_call | solution.py:45
  (329 shorter events, 81.9 us)
Async XLA Ops:
  2.6 8.0 %collective-permute-start.3 = (bf16[96,640]{1,0:T(8,128)(2,1)S(1)}, bf16[96,640]{1,0:T(8,128)(2,1)S(1)}, u32[]{:S(2)}, u32[]{:S(2)}) collective-permute-start(bf16[96,640]{1,0:T(8,128)(2,1)S(1)} %maximum_maximum_fusion.refs_0_), channel_id=1, source_target_pairs={{0,8},{8,16},{16,24},{24,28},{28,20},{20,12},{12,4},{4,0},{1,9},{9... | collective-permute-start | bytes 368648 | tf_op jit(solution)/shard_map/ppermute | solution.py:386
  5.7 6.5 %collective-permute-start.7 = (bf16[96,640]{1,0:T(8,128)(2,1)S(1)}, bf16[96,640]{1,0:T(8,128)(2,1)S(1)}, u32[]{:S(2)}, u32[]{:S(2)}) collective-permute-start(bf16[96,640]{1,0:T(8,128)(2,1)S(1)} %maximum_maximum_fusion.refs_0_), channel_id=1, source_target_pairs={{8,0},{16,8},{24,16},{28,24},{20,28},{12,20},{4,12},{0,4},{9,1},{1... | collective-permute-start | bytes 368648 | tf_op jit(solution)/shard_map/ppermute | solution.py:389
  6.9 53.9 %copy-start.1 = (bf16[1024,768]{1,0:T(8,128)(2,1)S(1)}, bf16[1024,768]{1,0:T(8,128)(2,1)}, u32[]{:S(2)}) copy-start(bf16[1024,768]{1,0:T(8,128)(2,1)} %x_ref.9) | copy-start | bytes 4718596
  6.9 53.9 %copy-start.56 = (s32[12]{0:T(128)S(1)}, s32[12]{0:T(128)}, u32[]{:S(2)}) copy-start(s32[12]{0:T(128)} %src.7) | copy-start | bytes 148
  6.9 51.8 %collective-permute-start = (bf16[1024,192]{1,0:T(8,128)(2,1)S(1)}, bf16[1024,192]{1,0:T(8,128)(2,1)S(1)}, u32[]{:S(2)}, u32[]{:S(2)}) collective-permute-start(bf16[1024,192]{1,0:T(8,128)(2,1)S(1)} %copy.67.f0), channel_id=1, source_target_pairs={{0,1},{1,0},{2,3},{3,2},{4,5},{5,4},{6,7},{7,6},{8,9},{9,8},{10,11... | collective-permute-start | bytes 1179656 | tf_op jit(solution)/shard_map/ppermute | solution.py:364
  7.0 21.3 %collective-permute-start.1 = (bf16[1024,192]{1,0:T(8,128)(2,1)S(1)}, bf16[1024,192]{1,0:T(8,128)(2,1)S(1)}, u32[]{:S(2)}, u32[]{:S(2)}) collective-permute-start(bf16[1024,192]{1,0:T(8,128)(2,1)S(1)} %copy.67.f0), channel_id=1, source_target_pairs={{0,2},{1,3},{2,0},{3,1},{4,6},{5,7},{6,4},{7,5},{8,10},{9,11},{10,... | collective-permute-start | bytes 1179656 | tf_op jit(solution)/shard_map/ppermute | solution.py:368
  10.6 5.5 %collective-permute-start.4 = (bf16[96,640]{1,0:T(8,128)(2,1)S(1)}, bf16[96,640]{1,0:T(8,128)(2,1)}, u32[]{:S(2)}, u32[]{:S(2)}) collective-permute-start(bf16[96,640]{1,0:T(8,128)(2,1)S(1)} %collective-permute-done.3.refs_1_), channel_id=1, source_target_pairs={{0,8},{8,16},{16,24},{24,28},{28,20},{20,12},{12,4},{4,0},{1,9},{9... | collective-permute-start | bytes 368648 | tf_op jit(solution)/shard_map/ppermute | solution.py:386
  12.2 5.5 %collective-permute-start.8 = (bf16[96,640]{1,0:T(8,128)(2,1)S(1)}, bf16[96,640]{1,0:T(8,128)(2,1)}, u32[]{:S(2)}, u32[]{:S(2)}) collective-permute-start(bf16[96,640]{1,0:T(8,128)(2,1)S(1)} %collective-permute-done.7.refs_5_), channel_id=1, source_target_pairs={{8,0},{16,8},{24,16},{28,24},{20,28},{12,20},{4,12},{0,4},{9,1},{1... | collective-permute-start | bytes 368648 | tf_op jit(solution)/shard_map/ppermute | solution.py:389
  14.2 8.5 %collective-permute-start.13 = (bf16[96,192]{1,0:T(8,128)(2,1)}, bf16[96,192]{1,0:T(8,128)(2,1)}, u32[]{:S(2)}, u32[]{:S(2)}) collective-permute-start(bf16[96,192]{1,0:T(8,128)(2,1)} %convert_bitcast_fusion.1), channel_id=1, source_target_pairs={{0,2},{1,3},{2,0},{3,1},{4,6},{5,7},{6,4},{7,5},{8,10},{9,11},{10,... | collective-permute-start | bytes 110600 | tf_op jit(solution)/shard_map/ppermute | solution.py:368
  16.1 9.7 %collective-permute-start.5 = (bf16[96,640]{1,0:T(8,128)(2,1)}, bf16[96,640]{1,0:T(8,128)(2,1)}, u32[]{:S(2)}, u32[]{:S(2)}) collective-permute-start(bf16[96,640]{1,0:T(8,128)(2,1)} %collective-permute-done.4.refs_2_), channel_id=1, source_target_pairs={{0,8},{8,16},{16,24},{24,28},{28,20},{20,12},{12,4},{4,0},{1,9},{9... | collective-permute-start | bytes 368648 | tf_op jit(solution)/shard_map/ppermute | solution.py:386
  17.7 6.0 %collective-permute-start.9 = (bf16[96,640]{1,0:T(8,128)(2,1)}, bf16[96,640]{1,0:T(8,128)(2,1)}, u32[]{:S(2)}, u32[]{:S(2)}) collective-permute-start(bf16[96,640]{1,0:T(8,128)(2,1)} %collective-permute-done.8.refs_6_), channel_id=1, source_target_pairs={{8,0},{16,8},{24,16},{28,24},{20,28},{12,20},{4,12},{0,4},{9,1},{1... | collective-permute-start | bytes 368648 | tf_op jit(solution)/shard_map/ppermute | solution.py:389
  23.7 8.4 %collective-permute-start.14 = (bf16[96,1152]{1,0:T(8,128)(2,1)S(1)}, bf16[96,1152]{1,0:T(8,128)(2,1)S(1)}, u32[]{:S(2)}, u32[]{:S(2)}) collective-permute-start(bf16[96,1152]{1,0:T(8,128)(2,1)S(1)} %concatenate.10.refs_0_), channel_id=1, source_target_pairs={{0,8},{8,16},{16,24},{24,28},{28,20},{20,12},{12,4},{4,0},{1,9},{9... | collective-permute-start | bytes 663560 | tf_op jit(solution)/shard_map/ppermute | solution.py:386
  25.6 8.3 %collective-permute-start.18 = (bf16[96,1152]{1,0:T(8,128)(2,1)S(1)}, bf16[96,1152]{1,0:T(8,128)(2,1)S(1)}, u32[]{:S(2)}, u32[]{:S(2)}) collective-permute-start(bf16[96,1152]{1,0:T(8,128)(2,1)S(1)} %concatenate.10.refs_0_), channel_id=1, source_target_pairs={{8,0},{16,8},{24,16},{28,24},{20,28},{12,20},{4,12},{0,4},{9,1},{1... | collective-permute-start | bytes 663560 | tf_op jit(solution)/shard_map/ppermute | solution.py:389
  25.8 34.9 %collective-permute-start.6 = (bf16[96,640]{1,0:T(8,128)(2,1)}, bf16[96,640]{1,0:T(8,128)(2,1)S(1)}, u32[]{:S(2)}, u32[]{:S(2)}) collective-permute-start(bf16[96,640]{1,0:T(8,128)(2,1)} %collective-permute-done.5.refs_3_), channel_id=1, source_target_pairs={{0,8},{8,16},{16,24},{24,28},{28,20},{20,12},{12,4},{4,0},{1,9},{9... | collective-permute-start | bytes 368648 | tf_op jit(solution)/shard_map/ppermute | solution.py:386
  28.3 32.4 %collective-permute-start.2 = (bf16[1024,192]{1,0:T(8,128)(2,1)S(1)}, bf16[1024,192]{1,0:T(8,128)(2,1)S(1)}, u32[]{:S(2)}, u32[]{:S(2)}) collective-permute-start(bf16[1024,192]{1,0:T(8,128)(2,1)S(1)} %collective-permute-done.1.f2), channel_id=1, source_target_pairs={{0,1},{1,0},{2,3},{3,2},{4,5},{5,4},{6,7},{7,6},{8,9},{9,8},{10,11... | collective-permute-start | bytes 1179656 | tf_op jit(solution)/shard_map/ppermute | solution.py:364
  32.1 6.3 %collective-permute-start.15 = (bf16[96,1152]{1,0:T(8,128)(2,1)S(1)}, bf16[96,1152]{1,0:T(8,128)(2,1)S(1)}, u32[]{:S(2)}, u32[]{:S(2)}) collective-permute-start(bf16[96,1152]{1,0:T(8,128)(2,1)S(1)} %collective-permute-done.14.refs_1_), channel_id=1, source_target_pairs={{0,8},{8,16},{16,24},{24,28},{28,20},{20,12},{12,4},{4,0},{1,9},{9... | collective-permute-start | bytes 663560 | tf_op jit(solution)/shard_map/ppermute | solution.py:386
  33.9 13.3 %collective-permute-start.19 = (bf16[96,1152]{1,0:T(8,128)(2,1)S(1)}, bf16[96,1152]{1,0:T(8,128)(2,1)S(1)}, u32[]{:S(2)}, u32[]{:S(2)}) collective-permute-start(bf16[96,1152]{1,0:T(8,128)(2,1)S(1)} %collective-permute-done.18.refs_5_), channel_id=1, source_target_pairs={{8,0},{16,8},{24,16},{28,24},{20,28},{12,20},{4,12},{0,4},{9,1},{1... | collective-permute-start | bytes 663560 | tf_op jit(solution)/shard_map/ppermute | solution.py:389
  38.3 6.4 %collective-permute-start.16 = (bf16[96,1152]{1,0:T(8,128)(2,1)S(1)}, bf16[96,1152]{1,0:T(8,128)(2,1)S(1)}, u32[]{:S(2)}, u32[]{:S(2)}) collective-permute-start(bf16[96,1152]{1,0:T(8,128)(2,1)S(1)} %collective-permute-done.15.refs_2_), channel_id=1, source_target_pairs={{0,8},{8,16},{16,24},{24,28},{28,20},{20,12},{12,4},{4,0},{1,9},{9... | collective-permute-start | bytes 663560 | tf_op jit(solution)/shard_map/ppermute | solution.py:386
  44.8 5.9 %collective-permute-start.17 = (bf16[96,1152]{1,0:T(8,128)(2,1)S(1)}, bf16[96,1152]{1,0:T(8,128)(2,1)S(1)}, u32[]{:S(2)}, u32[]{:S(2)}) collective-permute-start(bf16[96,1152]{1,0:T(8,128)(2,1)S(1)} %collective-permute-done.16.refs_3_), channel_id=1, source_target_pairs={{0,8},{8,16},{16,24},{24,28},{28,20},{20,12},{12,4},{4,0},{1,9},{9... | collective-permute-start | bytes 663560 | tf_op jit(solution)/shard_map/ppermute | solution.py:386
  47.3 13.2 %collective-permute-start.22 = (bf16[96,768]{1,0:T(8,128)(2,1)}, bf16[96,768]{1,0:T(8,128)(2,1)S(1)}, u32[]{:S(2)}, u32[]{:S(2)}) collective-permute-start(bf16[96,768]{1,0:T(8,128)(2,1)} %convert_bitcast_fusion.refs_8_), channel_id=1, source_target_pairs={{0,8},{8,16},{16,24},{24,28},{28,20},{20,12},{12,4},{4,0},{1,9},{9... | collective-permute-start | bytes 442376 | tf_op jit(solution)/shard_map/ppermute | solution.py:386
  50.7 5.9 %collective-permute-start.20 = (bf16[96,1152]{1,0:T(8,128)(2,1)S(1)}, bf16[96,1152]{1,0:T(8,128)(2,1)S(1)}, u32[]{:S(2)}, u32[]{:S(2)}) collective-permute-start(bf16[96,1152]{1,0:T(8,128)(2,1)S(1)} %collective-permute-done.19.refs_6_), channel_id=1, source_target_pairs={{8,0},{16,8},{24,16},{28,24},{20,28},{12,20},{4,12},{0,4},{9,1},{1... | collective-permute-start | bytes 663560 | tf_op jit(solution)/shard_map/ppermute | solution.py:389
  58.0 31.4 %collective-permute-start.21 = (bf16[768,384]{1,0:T(8,128)(2,1)}, bf16[768,384]{1,0:T(8,128)(2,1)}, u32[]{:S(2)}, u32[]{:S(2)}) collective-permute-start(bf16[768,384]{1,0:T(8,128)(2,1)} %slice_dynamic-update-slice_fusion), channel_id=1, source_target_pairs={{0,1},{1,0},{2,3},{3,2},{4,5},{5,4},{6,7},{7,6},{8,9},{9,8},{10,11... | collective-permute-start | bytes 1769480 | tf_op jit(solution)/shard_map/ppermute | solution.py:364
  58.7 14.1 %collective-permute-start.26 = (bf16[96,768]{1,0:T(8,128)(2,1)}, bf16[96,768]{1,0:T(8,128)(2,1)S(1)}, u32[]{:S(2)}, u32[]{:S(2)}) collective-permute-start(bf16[96,768]{1,0:T(8,128)(2,1)} %convert_bitcast_fusion.refs_8_), channel_id=1, source_target_pairs={{8,0},{16,8},{24,16},{28,24},{20,28},{12,20},{4,12},{0,4},{9,1},{1... | collective-permute-start | bytes 442376 | tf_op jit(solution)/shard_map/ppermute | solution.py:389
  60.5 13.9 %collective-permute-start.23 = (bf16[96,768]{1,0:T(8,128)(2,1)S(1)}, bf16[96,768]{1,0:T(8,128)(2,1)S(1)}, u32[]{:S(2)}, u32[]{:S(2)}) collective-permute-start(bf16[96,768]{1,0:T(8,128)(2,1)S(1)} %collective-permute-done.22.refs_9_), channel_id=1, source_target_pairs={{0,8},{8,16},{16,24},{24,28},{28,20},{20,12},{12,4},{4,0},{1,9},{9... | collective-permute-start | bytes 442376 | tf_op jit(solution)/shard_map/ppermute | solution.py:386
  71.0 9.4 %collective-permute-start.11 = (bf16[512,192]{1,0:T(8,128)(2,1)S(1)}, bf16[512,192]{1,0:T(8,128)(2,1)}, u32[]{:S(2)}, u32[]{:S(2)}) collective-permute-start(bf16[512,192]{1,0:T(8,128)(2,1)S(1)} %get-tuple-element.65.c0.ca), channel_id=1, source_target_pairs={{0,2},{1,3},{2,0},{3,1},{4,6},{5,7},{6,4},{7,5},{8,10},{9,11},{10,... | collective-permute-start | bytes 589832 | tf_op jit(solution)/shard_map/ppermute | solution.py:368
  72.8 7.3 %collective-permute-start.27 = (bf16[96,768]{1,0:T(8,128)(2,1)S(1)}, bf16[96,768]{1,0:T(8,128)(2,1)}, u32[]{:S(2)}, u32[]{:S(2)}) collective-permute-start(bf16[96,768]{1,0:T(8,128)(2,1)S(1)} %collective-permute-done.26.refs_13_), channel_id=1, source_target_pairs={{8,0},{16,8},{24,16},{28,24},{20,28},{12,20},{4,12},{0,4},{9,1},{1... | collective-permute-start | bytes 442376 | tf_op jit(solution)/shard_map/ppermute | solution.py:389
  74.3 6.1 %collective-permute-start.10 = (bf16[512,192]{1,0:T(8,128)(2,1)S(1)}, bf16[512,192]{1,0:T(8,128)(2,1)S(1)}, u32[]{:S(2)}, u32[]{:S(2)}) collective-permute-start(bf16[512,192]{1,0:T(8,128)(2,1)S(1)} %get-tuple-element.65.c0.ca), channel_id=1, source_target_pairs={{0,1},{1,0},{2,3},{3,2},{4,5},{5,4},{6,7},{7,6},{8,9},{9,8},{10,11... | collective-permute-start | bytes 589832 | tf_op jit(solution)/shard_map/ppermute | solution.py:364
  74.3 8.6 %collective-permute-start.24 = (bf16[96,768]{1,0:T(8,128)(2,1)S(1)}, bf16[96,768]{1,0:T(8,128)(2,1)}, u32[]{:S(2)}, u32[]{:S(2)}) collective-permute-start(bf16[96,768]{1,0:T(8,128)(2,1)S(1)} %collective-permute-done.23.refs_10_), channel_id=1, source_target_pairs={{0,8},{8,16},{16,24},{24,28},{28,20},{20,12},{12,4},{4,0},{1,9},{9... | collective-permute-start | bytes 442376 | tf_op jit(solution)/shard_map/ppermute | solution.py:386
  80.1 8.7 %collective-permute-start.30 = (bf16[512,192]{1,0:T(8,128)(2,1)}, bf16[512,192]{1,0:T(8,128)(2,1)}, u32[]{:S(2)}, u32[]{:S(2)}) collective-permute-start(bf16[512,192]{1,0:T(8,128)(2,1)} %get-tuple-element.69.c0.cb), channel_id=1, source_target_pairs={{0,2},{1,3},{2,0},{3,1},{4,6},{5,7},{6,4},{7,5},{8,10},{9,11},{10,... | collective-permute-start | bytes 589832 | tf_op jit(solution)/shard_map/ppermute | solution.py:368
  80.4 8.9 %collective-permute-start.12 = (bf16[512,192]{1,0:T(8,128)(2,1)}, bf16[512,192]{1,0:T(8,128)(2,1)}, u32[]{:S(2)}, u32[]{:S(2)}) collective-permute-start(bf16[512,192]{1,0:T(8,128)(2,1)} %collective-permute-done.11.c2), channel_id=1, source_target_pairs={{0,1},{1,0},{2,3},{3,2},{4,5},{5,4},{6,7},{7,6},{8,9},{9,8},{10,11... | collective-permute-start | bytes 589832 | tf_op jit(solution)/shard_map/ppermute | solution.py:364
  81.2 7.7 %collective-permute-start.28 = (bf16[96,768]{1,0:T(8,128)(2,1)}, bf16[96,768]{1,0:T(8,128)(2,1)}, u32[]{:S(2)}, u32[]{:S(2)}) collective-permute-start(bf16[96,768]{1,0:T(8,128)(2,1)} %collective-permute-done.27.refs_14_), channel_id=1, source_target_pairs={{8,0},{16,8},{24,16},{28,24},{20,28},{12,20},{4,12},{0,4},{9,1},{1... | collective-permute-start | bytes 442376 | tf_op jit(solution)/shard_map/ppermute | solution.py:389
  82.9 6.4 %collective-permute-start.25 = (bf16[96,768]{1,0:T(8,128)(2,1)}, bf16[96,768]{1,0:T(8,128)(2,1)}, u32[]{:S(2)}, u32[]{:S(2)}) collective-permute-start(bf16[96,768]{1,0:T(8,128)(2,1)} %collective-permute-done.24.refs_11_), channel_id=1, source_target_pairs={{0,8},{8,16},{16,24},{24,28},{28,20},{20,12},{12,4},{4,0},{1,9},{9... | collective-permute-start | bytes 442376 | tf_op jit(solution)/shard_map/ppermute | solution.py:386
  88.8 25.6 %collective-permute-start.29 = (bf16[512,192]{1,0:T(8,128)(2,1)}, bf16[512,192]{1,0:T(8,128)(2,1)S(1)}, u32[]{:S(2)}, u32[]{:S(2)}) collective-permute-start(bf16[512,192]{1,0:T(8,128)(2,1)} %get-tuple-element.69.c0.cb), channel_id=1, source_target_pairs={{0,1},{1,0},{2,3},{3,2},{4,5},{5,4},{6,7},{7,6},{8,9},{9,8},{10,11... | collective-permute-start | bytes 589832 | tf_op jit(solution)/shard_map/ppermute | solution.py:364
  88.8 25.6 %collective-permute-start.31 = (bf16[512,192]{1,0:T(8,128)(2,1)}, bf16[512,192]{1,0:T(8,128)(2,1)S(1)}, u32[]{:S(2)}, u32[]{:S(2)}) collective-permute-start(bf16[512,192]{1,0:T(8,128)(2,1)} %collective-permute-done.30.c2), channel_id=1, source_target_pairs={{0,1},{1,0},{2,3},{3,2},{4,5},{5,4},{6,7},{7,6},{8,9},{9,8},{10,11... | collective-permute-start | bytes 589832 | tf_op jit(solution)/shard_map/ppermute | solution.py:364
  129.0 9.2 %collective-permute-start.53 = (bf16[96,1536]{1,0:T(8,128)(2,1)}, bf16[96,1536]{1,0:T(8,128)(2,1)}, u32[]{:S(2)}, u32[]{:S(2)}) collective-permute-start(bf16[96,1536]{1,0:T(8,128)(2,1)} %get-tuple-element.162), channel_id=1, source_target_pairs={{0,8},{8,16},{16,24},{24,28},{28,20},{20,12},{12,4},{4,0},{1,9},{9... | collective-permute-start | bytes 884744 | tf_op jit(solution)/shard_map/ppermute | solution.py:406
  136.5 16.2 %collective-permute-start.32 = (bf16[256,768]{1,0:T(8,128)(2,1)}, bf16[256,768]{1,0:T(8,128)(2,1)}, u32[]{:S(2)}, u32[]{:S(2)}) collective-permute-start(bf16[256,768]{1,0:T(8,128)(2,1)} %get-tuple-element.72), channel_id=1, source_target_pairs={{0,1},{1,0},{2,3},{3,2},{4,5},{5,4},{6,7},{7,6},{8,9},{9,8},{10,11... | collective-permute-start | bytes 1179656 | tf_op jit(solution)/shard_map/ppermute | solution.py:364
  136.5 22.1 %collective-permute-start.33 = (bf16[256,768]{1,0:T(8,128)(2,1)}, bf16[256,768]{1,0:T(8,128)(2,1)}, u32[]{:S(2)}, u32[]{:S(2)}) collective-permute-start(bf16[256,768]{1,0:T(8,128)(2,1)} %copy-done.61), channel_id=1, source_target_pairs={{0,1},{1,0},{2,3},{3,2},{4,5},{5,4},{6,7},{7,6},{8,9},{9,8},{10,11... | collective-permute-start | bytes 1179656 | tf_op jit(solution)/shard_map/ppermute | solution.py:364
  137.0 3.9 %collective-permute-start.35 = (bf16[256,768]{1,0:T(8,128)(2,1)}, bf16[256,768]{1,0:T(8,128)(2,1)S(1)}, u32[]{:S(2)}, u32[]{:S(2)}) collective-permute-start(bf16[256,768]{1,0:T(8,128)(2,1)} %copy-done.64), channel_id=1, source_target_pairs={{0,1},{1,0},{2,3},{3,2},{4,5},{5,4},{6,7},{7,6},{8,9},{9,8},{10,11... | collective-permute-start | bytes 1179656 | tf_op jit(solution)/shard_map/ppermute | solution.py:364
  137.0 6.6 %collective-permute-start.38 = (bf16[256,768]{1,0:T(8,128)(2,1)S(1)}, bf16[256,768]{1,0:T(8,128)(2,1)S(1)}, u32[]{:S(2)}, u32[]{:S(2)}) collective-permute-start(bf16[256,768]{1,0:T(8,128)(2,1)S(1)} %copy-done.63), channel_id=1, source_target_pairs={{0,1},{1,0},{2,3},{3,2},{4,5},{5,4},{6,7},{7,6},{8,9},{9,8},{10,11... | collective-permute-start | bytes 1179656 | tf_op jit(solution)/shard_map/ppermute | solution.py:364
  138.2 8.5 %collective-permute-start.57 = (bf16[96,1536]{1,0:T(8,128)(2,1)}, bf16[96,1536]{1,0:T(8,128)(2,1)S(1)}, u32[]{:S(2)}, u32[]{:S(2)}) collective-permute-start(bf16[96,1536]{1,0:T(8,128)(2,1)} %get-tuple-element.163), channel_id=1, source_target_pairs={{8,0},{16,8},{24,16},{28,24},{20,28},{12,20},{4,12},{0,4},{9,1},{1... | collective-permute-start | bytes 884744 | tf_op jit(solution)/shard_map/ppermute | solution.py:409
  140.9 8.3 %collective-permute-start.54 = (bf16[96,1536]{1,0:T(8,128)(2,1)S(1)}, bf16[96,1536]{1,0:T(8,128)(2,1)S(1)}, u32[]{:S(2)}, u32[]{:S(2)}) collective-permute-start(bf16[96,1536]{1,0:T(8,128)(2,1)S(1)} %add_convert_fusion.7), channel_id=1, source_target_pairs={{0,8},{8,16},{16,24},{24,28},{28,20},{20,12},{12,4},{4,0},{1,9},{9... | collective-permute-start | bytes 884744 | tf_op jit(solution)/shard_map/ppermute | solution.py:406
  143.7 17.4 %collective-permute-start.36 = (bf16[256,768]{1,0:T(8,128)(2,1)}, bf16[256,768]{1,0:T(8,128)(2,1)}, u32[]{:S(2)}, u32[]{:S(2)}) collective-permute-start(bf16[256,768]{1,0:T(8,128)(2,1)} %add_convert_fusion.1.own), channel_id=1, source_target_pairs={{0,2},{1,3},{2,0},{3,1},{4,6},{5,7},{6,4},{7,5},{8,10},{9,11},{10,... | collective-permute-start | bytes 1179656 | tf_op jit(solution)/shard_map/ppermute | solution.py:368
  146.7 17.7 %collective-permute-start.39 = (bf16[256,768]{1,0:T(8,128)(2,1)S(1)}, bf16[256,768]{1,0:T(8,128)(2,1)}, u32[]{:S(2)}, u32[]{:S(2)}) collective-permute-start(bf16[256,768]{1,0:T(8,128)(2,1)S(1)} %add_convert_fusion.own), channel_id=1, source_target_pairs={{0,2},{1,3},{2,0},{3,1},{4,6},{5,7},{6,4},{7,5},{8,10},{9,11},{10,... | collective-permute-start | bytes 1179656 | tf_op jit(solution)/shard_map/ppermute | solution.py:368
  151.2 15.6 %collective-permute-start.55 = (bf16[96,1536]{1,0:T(8,128)(2,1)}, bf16[96,1536]{1,0:T(8,128)(2,1)}, u32[]{:S(2)}, u32[]{:S(2)}) collective-permute-start(bf16[96,1536]{1,0:T(8,128)(2,1)} %get-tuple-element.160), channel_id=1, source_target_pairs={{0,8},{8,16},{16,24},{24,28},{28,20},{20,12},{12,4},{4,0},{1,9},{9... | collective-permute-start | bytes 884744 | tf_op jit(solution)/shard_map/ppermute | solution.py:406
  152.8 14.1 %collective-permute-start.58 = (bf16[96,1536]{1,0:T(8,128)(2,1)}, bf16[96,1536]{1,0:T(8,128)(2,1)}, u32[]{:S(2)}, u32[]{:S(2)}) collective-permute-start(bf16[96,1536]{1,0:T(8,128)(2,1)} %get-tuple-element.161), channel_id=1, source_target_pairs={{8,0},{16,8},{24,16},{28,24},{20,28},{12,20},{4,12},{0,4},{9,1},{1... | collective-permute-start | bytes 884744 | tf_op jit(solution)/shard_map/ppermute | solution.py:409
  160.4 29.7 %collective-permute-start.34 = (bf16[256,768]{1,0:T(8,128)(2,1)S(1)}, bf16[256,768]{1,0:T(8,128)(2,1)S(1)}, u32[]{:S(2)}, u32[]{:S(2)}) collective-permute-start(bf16[256,768]{1,0:T(8,128)(2,1)S(1)} %select_convert_fusion.1), channel_id=1, source_target_pairs={{0,2},{1,3},{2,0},{3,1},{4,6},{5,7},{6,4},{7,5},{8,10},{9,11},{10,... | collective-permute-start | bytes 1179656 | tf_op jit(solution)/shard_map/ppermute | solution.py:368
  164.1 10.4 %collective-permute-start.37 = (bf16[256,768]{1,0:T(8,128)(2,1)S(1)}, bf16[256,768]{1,0:T(8,128)(2,1)S(1)}, u32[]{:S(2)}, u32[]{:S(2)}) collective-permute-start(bf16[256,768]{1,0:T(8,128)(2,1)S(1)} %get-tuple-element.77.own), channel_id=1, source_target_pairs={{0,1},{1,0},{2,3},{3,2},{4,5},{5,4},{6,7},{7,6},{8,9},{9,8},{10,11... | collective-permute-start | bytes 1179656 | tf_op jit(solution)/shard_map/ppermute | solution.py:364
  166.5 4.2 %collective-permute-start.40 = (bf16[256,768]{1,0:T(8,128)(2,1)S(1)}, bf16[256,768]{1,0:T(8,128)(2,1)S(1)}, u32[]{:S(2)}, u32[]{:S(2)}) collective-permute-start(bf16[256,768]{1,0:T(8,128)(2,1)S(1)} %get-tuple-element.82.own), channel_id=1, source_target_pairs={{0,1},{1,0},{2,3},{3,2},{4,5},{5,4},{6,7},{7,6},{8,9},{9,8},{10,11... | collective-permute-start | bytes 1179656 | tf_op jit(solution)/shard_map/ppermute | solution.py:364
  168.7 27.5 %collective-permute-start.59 = (bf16[96,1536]{1,0:T(8,128)(2,1)S(1)}, bf16[96,1536]{1,0:T(8,128)(2,1)S(1)}, u32[]{:S(2)}, u32[]{:S(2)}) collective-permute-start(bf16[96,1536]{1,0:T(8,128)(2,1)S(1)} %get-tuple-element.159), channel_id=1, source_target_pairs={{8,0},{16,8},{24,16},{28,24},{20,28},{12,20},{4,12},{0,4},{9,1},{1... | collective-permute-start | bytes 884744 | tf_op jit(solution)/shard_map/ppermute | solution.py:409
  169.9 26.3 %collective-permute-start.56 = (bf16[96,1536]{1,0:T(8,128)(2,1)S(1)}, bf16[96,1536]{1,0:T(8,128)(2,1)S(1)}, u32[]{:S(2)}, u32[]{:S(2)}) collective-permute-start(bf16[96,1536]{1,0:T(8,128)(2,1)S(1)} %get-tuple-element.158), channel_id=1, source_target_pairs={{0,8},{8,16},{16,24},{24,28},{28,20},{20,12},{12,4},{4,0},{1,9},{9... | collective-permute-start | bytes 884744 | tf_op jit(solution)/shard_map/ppermute | solution.py:406
  188.4 6.1 %collective-permute-start.46 = (bf16[96,832]{1,0:T(8,128)(2,1)S(1)}, bf16[96,832]{1,0:T(8,128)(2,1)S(1)}, u32[]{:S(2)}, u32[]{:S(2)}) collective-permute-start(bf16[96,832]{1,0:T(8,128)(2,1)S(1)} %get-tuple-element.170), channel_id=1, source_target_pairs={{0,8},{8,16},{16,24},{24,28},{28,20},{20,12},{12,4},{4,0},{1,9},{9... | collective-permute-start | bytes 479240 | tf_op jit(solution)/shard_map/ppermute | solution.py:406
  192.2 5.7 %collective-permute-start.50 = (bf16[96,832]{1,0:T(8,128)(2,1)S(1)}, bf16[96,832]{1,0:T(8,128)(2,1)S(1)}, u32[]{:S(2)}, u32[]{:S(2)}) collective-permute-start(bf16[96,832]{1,0:T(8,128)(2,1)S(1)} %get-tuple-element.171), channel_id=1, source_target_pairs={{8,0},{16,8},{24,16},{28,24},{20,28},{12,20},{4,12},{0,4},{9,1},{1... | collective-permute-start | bytes 479240 | tf_op jit(solution)/shard_map/ppermute | solution.py:409
  194.6 5.5 %collective-permute-start.47 = (bf16[96,832]{1,0:T(8,128)(2,1)S(1)}, bf16[96,832]{1,0:T(8,128)(2,1)S(1)}, u32[]{:S(2)}, u32[]{:S(2)}) collective-permute-start(bf16[96,832]{1,0:T(8,128)(2,1)S(1)} %add_convert_fusion.12), channel_id=1, source_target_pairs={{0,8},{8,16},{16,24},{24,28},{28,20},{20,12},{12,4},{4,0},{1,9},{9... | collective-permute-start | bytes 479240 | tf_op jit(solution)/shard_map/ppermute | solution.py:406
  200.2 5.5 %collective-permute-start.48 = (bf16[96,832]{1,0:T(8,128)(2,1)S(1)}, bf16[96,832]{1,0:T(8,128)(2,1)S(1)}, u32[]{:S(2)}, u32[]{:S(2)}) collective-permute-start(bf16[96,832]{1,0:T(8,128)(2,1)S(1)} %get-tuple-element.168), channel_id=1, source_target_pairs={{0,8},{8,16},{16,24},{24,28},{28,20},{20,12},{12,4},{4,0},{1,9},{9... | collective-permute-start | bytes 479240 | tf_op jit(solution)/shard_map/ppermute | solution.py:406
  201.8 5.8 %collective-permute-start.51 = (bf16[96,832]{1,0:T(8,128)(2,1)S(1)}, bf16[96,832]{1,0:T(8,128)(2,1)S(1)}, u32[]{:S(2)}, u32[]{:S(2)}) collective-permute-start(bf16[96,832]{1,0:T(8,128)(2,1)S(1)} %get-tuple-element.169), channel_id=1, source_target_pairs={{8,0},{16,8},{24,16},{28,24},{20,28},{12,20},{4,12},{0,4},{9,1},{1... | collective-permute-start | bytes 479240 | tf_op jit(solution)/shard_map/ppermute | solution.py:409
  203.4 11.3 %collective-permute-start.44 = (bf16[1024,192]{1,0:T(8,128)(2,1)S(1)}, bf16[1024,192]{1,0:T(8,128)(2,1)S(1)}, u32[]{:S(2)}, u32[]{:S(2)}) collective-permute-start(bf16[1024,192]{1,0:T(8,128)(2,1)S(1)} %get-tuple-element.95.d0), channel_id=1, source_target_pairs={{0,2},{1,3},{2,0},{3,1},{4,6},{5,7},{6,4},{7,5},{8,10},{9,11},{10,... | collective-permute-start | bytes 1179656 | tf_op jit(solution)/shard_map/ppermute | solution.py:368
  207.7 6.9 %collective-permute-start.52 = (bf16[96,832]{1,0:T(8,128)(2,1)S(1)}, bf16[96,832]{1,0:T(8,128)(2,1)S(1)}, u32[]{:S(2)}, u32[]{:S(2)}) collective-permute-start(bf16[96,832]{1,0:T(8,128)(2,1)S(1)} %get-tuple-element.167), channel_id=1, source_target_pairs={{8,0},{16,8},{24,16},{28,24},{20,28},{12,20},{4,12},{0,4},{9,1},{1... | collective-permute-start | bytes 479240 | tf_op jit(solution)/shard_map/ppermute | solution.py:409
  208.5 6.1 %collective-permute-start.49 = (bf16[96,832]{1,0:T(8,128)(2,1)S(1)}, bf16[96,832]{1,0:T(8,128)(2,1)S(1)}, u32[]{:S(2)}, u32[]{:S(2)}) collective-permute-start(bf16[96,832]{1,0:T(8,128)(2,1)S(1)} %get-tuple-element.166), channel_id=1, source_target_pairs={{0,8},{8,16},{16,24},{24,28},{28,20},{20,12},{12,4},{4,0},{1,9},{9... | collective-permute-start | bytes 479240 | tf_op jit(solution)/shard_map/ppermute | solution.py:406
  211.1 23.9 %collective-permute-start.43 = (bf16[1024,192]{1,0:T(8,128)(2,1)S(1)}, bf16[1024,192]{1,0:T(8,128)(2,1)}, u32[]{:S(2)}, u32[]{:S(2)}) collective-permute-start(bf16[1024,192]{1,0:T(8,128)(2,1)S(1)} %get-tuple-element.95.d0), channel_id=1, source_target_pairs={{0,1},{1,0},{2,3},{3,2},{4,5},{5,4},{6,7},{7,6},{8,9},{9,8},{10,11... | collective-permute-start | bytes 1179656 | tf_op jit(solution)/shard_map/ppermute | solution.py:364
  211.2 13.5 %collective-permute-start.41 = (bf16[512,768]{1,0:T(8,128)(2,1)S(1)}, bf16[512,768]{1,0:T(8,128)(2,1)}, u32[]{:S(2)}, u32[]{:S(2)}) collective-permute-start(bf16[512,768]{1,0:T(8,128)(2,1)S(1)} %get-tuple-element.92), channel_id=1, source_target_pairs={{0,1},{1,0},{2,3},{3,2},{4,5},{5,4},{6,7},{7,6},{8,9},{9,8},{10,11... | collective-permute-start | bytes 2359304 | tf_op jit(solution)/shard_map/ppermute | solution.py:364
  214.6 20.4 %collective-permute-start.45 = (bf16[1024,192]{1,0:T(8,128)(2,1)S(1)}, bf16[1024,192]{1,0:T(8,128)(2,1)}, u32[]{:S(2)}, u32[]{:S(2)}) collective-permute-start(bf16[1024,192]{1,0:T(8,128)(2,1)S(1)} %collective-permute-done.44.d2), channel_id=1, source_target_pairs={{0,1},{1,0},{2,3},{3,2},{4,5},{5,4},{6,7},{7,6},{8,9},{9,8},{10,11... | collective-permute-start | bytes 1179656 | tf_op jit(solution)/shard_map/ppermute | solution.py:364
  215.5 7.1 %collective-permute-start.60 = (f32[4,96]{0,1:T(8,128)}, f32[4,96]{0,1:T(8,128)}, u32[]{:S(2)}, u32[]{:S(2)}) collective-permute-start(f32[4,96]{0,1:T(8,128)} %slice_bitcast_fusion.2), channel_id=1, source_target_pairs={{0,1},{1,0},{2,3},{3,2},{4,5},{5,4},{6,7},{7,6},{8,9},{9,8},{10,11... | collective-permute-start | bytes 4616 | tf_op jit(solution)/shard_map/ppermute | solution.py:364
  223.5 4.6 %collective-permute-start.61 = (f32[4,96]{0,1:T(8,128)S(1)}, f32[4,96]{0,1:T(8,128)S(1)}, u32[]{:S(2)}, u32[]{:S(2)}) collective-permute-start(f32[4,96]{0,1:T(8,128)S(1)} %fusion.7), channel_id=1, source_target_pairs={{0,2},{1,3},{2,0},{3,1},{4,6},{5,7},{6,4},{7,5},{8,10},{9,11},{10,... | collective-permute-start | bytes 4616 | tf_op jit(solution)/shard_map/ppermute | solution.py:368
  227.2 14.6 %collective-permute-start.42 = (bf16[256,768]{1,0:T(8,128)(2,1)}, bf16[256,768]{1,0:T(8,128)(2,1)}, u32[]{:S(2)}, u32[]{:S(2)}) collective-permute-start(bf16[256,768]{1,0:T(8,128)(2,1)} %get-tuple-element.164), channel_id=1, source_target_pairs={{0,2},{1,3},{2,0},{3,1},{4,6},{5,7},{6,4},{7,5},{8,10},{9,11},{10,... | collective-permute-start | bytes 1179656 | tf_op jit(solution)/shard_map/ppermute | solution.py:368
  (94 other events, 605.8 us)

commit v2 on v1

v2 whole, which is shorter than its diff:
```python
import functools

import jax
import jax.numpy as jnp
import numpy as np
from jax import lax
from jax.experimental import pallas as pl
from jax.experimental.pallas import tpu as pltpu
from jax.sharding import PartitionSpec as P

H = 12
HD = 64
ADAM_STEP = 5
EPS = 1e-05
MASKED = -1e30
RB = 256
LANES = 128
RING = (0, 2, 4, 6, 7, 5, 3, 1)
OFFSETS = (0, -1, -2, -3, -4, 1, 2, 3)
GELU_A = 0.7978845608028654
GELU_B = 0.044715
RATES = {"qkv": 0.06, "proj": 0.15, "fc": 0.04, "down": 0.03, "norm": 0.3}

bf16 = jnp.bfloat16
f32 = jnp.float32


def dot(a, b):
    return jnp.dot(a, b, preferred_element_type=f32)


def dot_nt(a, b):
    return lax.dot_general(a, b, (((1,), (1,)), ((), ())), preferred_element_type=f32)


def dot_tn(a, b):
    return lax.dot_general(a, b, (((0,), (0,)), ((), ())), preferred_element_type=f32)


class Place:
    def __init__(self):
        self.mp, self.dp = lax.axis_index("mp"), lax.axis_index("dp")

    def __getitem__(self, k):
        if k < 4:
            return (self.mp % 2, self.mp // 2, self.mp, self.dp)[k]
        if lax.axis_size("dp") != len(RING):
            return 0
        z, y = self.dp // 2, self.dp % 2
        at = (jnp.where(y == 0, z, 7 - z) + OFFSETS[k - 4] + 8) % 8
        return jnp.where(at < 4, 2 * at, 2 * (7 - at) + 1)


HERE = object()


def call(kernel, name, scalars, ins, outs, scratch=(), vmem=16, far=False):
    if HERE in scalars:
        inner = kernel
        kernel = lambda *refs: inner(Place(), *refs)
        scalars = scalars[1:]
    smem = pl.BlockSpec(memory_space=pltpu.SMEM)
    full = pl.BlockSpec(memory_space=pltpu.VMEM)
    given = pl.BlockSpec(memory_space=pltpu.HBM) if far else full
    return pl.pallas_call(
        kernel,
        in_specs=[smem] * len(scalars) + [given] * len(ins),
        out_specs=[full] * len(outs),
        out_shape=[jax.ShapeDtypeStruct(sh, dt) for sh, dt in outs],
        scratch_shapes=list(scratch),
        compiler_params=pltpu.CompilerParams(vmem_limit_bytes=vmem * 1024 * 1024),
        cost_estimate=pl.CostEstimate(flops=1, bytes_accessed=1, transcendentals=0),
        name=name,
    )(*scalars, *ins)


def block(index, size=RB):
    return pl.ds(pl.multiple_of(index * size, size), size)


def fetch(pairs, sems):
    copies = [pltpu.make_async_copy(src, dst, sems.at[k]) for k, (src, dst) in enumerate(pairs)]
    for copy in copies:
        copy.start()
    for copy in copies:
        copy.wait()


def prep_one_kernel(q_ref, n_ref, out, q, norms, turn, sems):
    rows, cols = q.shape
    turn[...] = jnp.zeros(turn.shape, f32)
    fetch([(q_ref, q), (n_ref, norms)], sems)
    turn[: norms.shape[0], :rows] = norms[...]
    out[:, :cols] = q[...].astype(bf16)
    out[:, cols:] = turn[...].T[:rows, : out.shape[1] - cols].astype(bf16)


def prep_two_kernel(p_ref, f_ref, d_ref, proj, fc, down, p, f, d, turn, sems):
    rows = proj.shape[0]
    turn[...] = jnp.zeros(turn.shape, f32)
    fetch([(p_ref, p), (f_ref, f), (d_ref, d)], sems)
    turn[:, :rows] = p[...]
    proj[...] = turn[...].T[:rows].astype(bf16)
    fc[...] = f[...].astype(bf16)
    down[...] = d[...].astype(bf16)


def join_kernel(f_ref, own, across, out):
    hid, cw = f_ref.shape[1], own.shape[1]
    out[:, :hid] = f_ref[...]
    out[:, hid:] = jnp.concatenate([own[...], across[...]], 1)


def norm_stats(values):
    center = values - jnp.mean(values, axis=-1, keepdims=True)
    scale = lax.rsqrt(jnp.mean(center * center, axis=-1, keepdims=True) + EPS)
    return center * scale, scale


def unit_kernel(x_ref, unit_ref):
    for i in range(x_ref.shape[0] // RB):
        at = slice(i * RB, (i + 1) * RB)
        unit_ref[at] = norm_stats(x_ref[at].astype(f32))[0]


def loop(count, body):
    lax.fori_loop(0, count, lambda i, carry: (body(i), carry)[1], 0)


def qkv_kernel(n, heads, info, unit_ref, *refs):
    pieces, (a1_ref, m_ref, v_ref, w_ref, norm_ref) = refs[:n], refs[n:]
    cols = m_ref.shape[1]
    base = cols // LANES * LANES
    rows = w_ref.shape[0] // n
    for k, piece in enumerate(pieces):
        w_ref[block(info[4 + k], rows), :] = piece[...]
    turned = w_ref[:, base : base + LANES].astype(f32).T
    norm_ref[...] = turned[cols - base : cols - base + 8]

    def step(i):
        at = block(i)
        a1 = (unit_ref[at, :] * norm_ref[0:1] + norm_ref[1:2]).astype(bf16)
        a1_ref[at, :] = a1
        mixed = dot(a1, w_ref[:, :cols])
        m_ref[at, :] = mixed.astype(bf16)
        for h in range(heads):
            fresh = mixed[:, (3 * h + 2) * HD : (3 * h + 3) * HD]
            v_ref[h * HD : (h + 1) * HD, at] = fresh.T.astype(bf16)

    loop(m_ref.shape[0] // RB, step)


def values_kernel(heads, info, src, fresh, f0, f1, f2, f3, v_ref):
    mp = info[2]
    for h in range(heads):
        source = src[mp * heads + h]
        held = source // heads
        mine = slice(h * HD, (h + 1) * HD)

        @pl.when(source >= H)
        def _():
            v_ref[mine, :] = fresh[mine, :]

        for r, first in enumerate((f0, f1, f2, f3)):

            @pl.when((source < H) & (held == mp ^ r))
            def _():
                v_ref[mine, :] = first[block(source - held * heads, HD), :]


def masked_tile():
    keys = lax.broadcasted_iota(jnp.int32, (RB, RB), 0)
    queries = lax.broadcasted_iota(jnp.int32, (RB, RB), 1)
    return keys <= queries


def attend_kernel(heads, base, m_ref, v_ref, c_ref, lse_ref):
    keep = masked_tile()
    blocks = c_ref.shape[0] // RB
    turned = [[None] * heads for _ in range(blocks)]
    lse_ref[...] = jnp.zeros(lse_ref.shape, f32)
    for h in range(heads):
        top = base + blocks * RB
        keys = m_ref[:top, (3 * h + 1) * HD : (3 * h + 2) * HD]
        values_t = v_ref[h * HD : (h + 1) * HD, :top]
        for i in range(blocks):
            lo = base + i * RB
            hi = lo + RB
            query = m_ref[lo:hi, 3 * h * HD : (3 * h + 1) * HD] * bf16(HD**-0.5)
            diag = jnp.where(keep, dot_nt(keys[lo:hi], query), MASKED)
            peak = jnp.max(diag, 0, keepdims=True)
            if lo:
                left = dot_nt(keys[:lo], query)
                peak = jnp.maximum(peak, jnp.max(left, 0, keepdims=True))
            diag = jnp.exp(diag - peak)
            total = jnp.sum(diag, 0, keepdims=True)
            if lo:
                left = jnp.exp(left - peak)
                total += jnp.sum(left, 0, keepdims=True)
            inverse = 1.0 / total
            context = dot(values_t[:, lo:hi], (diag * inverse).astype(bf16))
            if lo:
                context += dot(values_t[:, :lo], (left * inverse).astype(bf16))
            turned[i][h] = context
            lse_ref[h : h + 1, i * RB : (i + 1) * RB] = peak + jnp.log(total)
    for i in range(blocks):
        c_ref[i * RB : (i + 1) * RB] = jnp.concatenate(turned[i], 0).T.astype(bf16)


def assemble_two_kernel(n, info, *refs):
    pieces, (wf, own, across, turn) = refs[:n], refs[n:]
    width, hid = wf.shape
    cw = own.shape[0]
    rows = width // n
    for k, piece in enumerate(pieces):
        at = block(info[4 + k], rows)
        wf[at, :] = piece[:, :hid]
        turn[at, :] = piece[:, hid:]
    pair = turn[...].T
    own[...] = pair[:cw]
    across[...] = pair[cw:]


def assemble_three_kernel(n, info, *refs):
    pieces, (wd,) = refs[:n], refs[n:]
    rows = wd.shape[0] // n
    for k, piece in enumerate(pieces):
        wd[block(info[4 + k], rows), :] = piece[...]


def mlp_kernel(part, x_ref, norm_ref, c0, c1, c2, c3, w0, w1, w2, w3, wf, r_ref, unit_ref, a2_ref, g_ref, slope_ref):
    def step(i):
        at = block(i)
        resid = x_ref[block(2 * part + i), :].astype(f32) + (
            (dot(c0[at, :], w0[...]) + dot(c1[at, :], w1[...]))
            + (dot(c2[at, :], w2[...]) + dot(c3[at, :], w3[...]))
        )
        r_ref[at, :] = resid
        unit, _ = norm_stats(resid)
        unit_ref[at, :] = unit
        a2 = (unit * norm_ref[2:3] + norm_ref[3:4]).astype(bf16)
        a2_ref[at, :] = a2
        u = dot(a2, wf[...])
        square = u * u
        t = jnp.tanh(GELU_A * u * (1.0 + GELU_B * square))
        g_ref[at, :] = (0.5 * u * (1.0 + t)).astype(bf16)
        slope_ref[at, :] = 0.5 * (1.0 + t) + 0.5 * u * (1.0 - t * t) * (
            GELU_A * (1.0 + 3.0 * GELU_B * square)
        )

    loop(2, step)


def mlp_back_kernel(part, info, e_ref, unit_ref, slope_ref, wf, wd, du_ref, top, bottom, keep, nacc):
    core = info[0]
    nacc[...] = jnp.zeros(nacc.shape, f32)

    def step(i):
        spot = jnp.where(i == 1, core, 1 - core)
        at = block(spot)
        du = (dot(e_ref[block(2 * part + spot), :], wd[...]) * slope_ref[at, :]).astype(bf16)
        du_ref[at, :] = du
        grad = dot_nt(du, wf[...])
        nacc[2:3] += jnp.sum(grad * unit_ref[at, :], 0, keepdims=True)
        nacc[3:4] += jnp.sum(grad, 0, keepdims=True)
        keep[...] = grad

        @pl.when(i == 0)
        def _():
            top[...] = grad[: RB // 2].astype(bf16)
            bottom[...] = grad[RB // 2 :].astype(bf16)

    loop(2, step)


def mlp_out_kernel(info, g_ref, wd, ysend, ykeep):
    ykeep[...] = dot_nt(g_ref[block(info[0]), :], wd[...])
    ysend[...] = dot_nt(g_ref[block(1 - info[0]), :], wd[...]).astype(bf16)


def add_kernel(keep, top, bottom, out):
    out[: RB // 2] = (keep[: RB // 2] + top[...].astype(f32)).astype(bf16)
    out[RB // 2 :] = (keep[RB // 2 :] + bottom[...].astype(f32)).astype(bf16)


def starts(info, full, fw, bw):
    rows = fw.shape[0]
    fw[...] = full[block(info[4 + OFFSETS.index(-4)], rows), :].astype(bf16)
    bw[...] = full[block(info[4 + OFFSETS.index(-3)], rows), :].astype(bf16)


def mlp_grad_kernel(info, a2a, a2b, dua, dub, e_ref, ga, gb, out, fw, bw):
    hid = dua.shape[1]
    half = dua.shape[0]

    def step(j):
        at = block(j)
        out[at, :hid] = (dot_tn(a2a[:, at], dua[...]) + dot_tn(a2b[:, at], dub[...])).astype(out.dtype)
        out[at, hid:] = (dot_tn(e_ref[:half, at], ga[...]) + dot_tn(e_ref[half:, at], gb[...])).astype(out.dtype)

    loop(out.shape[0] // RB, step)
    starts(info, out, fw, bw)


def hop_kernel(ahead, behind, info, full, a, b, a_out, b_out):
    rows = a.shape[0]
    for offset, value, out in ((ahead, a, a_out), (behind, b, b_out)):
        term = full[block(info[4 + OFFSETS.index(offset)], rows), :]
        out[...] = (value[...].astype(f32) + term.astype(f32)).astype(bf16)


def hop_last_kernel(info, full, a, a_out):
    term = full[block(info[4 + OFFSETS.index(1)], a.shape[0]), :]
    a_out[...] = (a[...].astype(f32) + term.astype(f32)).astype(bf16)


def norm_back(unit, scale, gain, grad):
    dy = grad * gain
    return scale * (
        dy - jnp.mean(dy, -1, keepdims=True) - unit * jnp.mean(dy * unit, -1, keepdims=True)
    )


def norm_two_kernel(part, info, r_ref, own, received, e_ref, norm_ref, dr_ref, top, bottom):
    unit, scale = norm_stats(r_ref[block(info[0]), :])
    grad = own[...].astype(f32) + received[...].astype(f32)
    e = e_ref[block(2 * part + info[0]), :].astype(f32)
    dr = e + norm_back(unit, scale, norm_ref[2:3], grad)
    dr_ref[...] = dr
    top[...] = dr[: RB // 2].astype(bf16)
    bottom[...] = dr[RB // 2 :].astype(bf16)


def attend_back_kernel(heads, base, last, info, src, m_ref, v_ref, o0, o1, p0, p1, wp, lse_ref, *refs):
    if last:
        dqa, dka, dva, ab_ref, dm_ref, dvr_ref = refs
    else:
        ab_ref, dq_ref, dk_ref, dv_ref = refs
    keep = masked_tile()
    core = info[0]
    rows = 2 * RB
    blocks = 2
    for k, (own, partner) in enumerate(((o0, p0), (o1, p1))):
        ab_ref[block(2 * core + k, RB // 2), :] = own[...]
        ab_ref[block(2 * (1 - core) + k, RB // 2), :] = partner[...]
    top = base + rows
    tiles = top // RB
    dctx = [dot_nt(ab_ref[i * RB : (i + 1) * RB], wp[...]).astype(bf16) for i in range(blocks)]
    dq_t = [[None] * heads for _ in range(blocks)]
    dks, dvs = [], []
    for h in range(heads):
        keys = m_ref[:top, (3 * h + 1) * HD : (3 * h + 2) * HD]
        keys_t = keys.T
        values = v_ref[h * HD : (h + 1) * HD, :top].T
        dk = [None] * tiles
        dv = [None] * tiles
        for i in range(blocks):
            lo = base + i * RB
            count = lo // RB + 1
            query = m_ref[lo : lo + RB, 3 * h * HD : (3 * h + 1) * HD] * bf16(HD**-0.5)
            dc = dctx[i][:, h * HD : (h + 1) * HD]
            lse = lse_ref[h : h + 1, i * RB : (i + 1) * RB]
            probs, dprobs = [], []
            inner = jnp.zeros((1, RB), f32)
            for t in range(count):
                spot = slice(t * RB, (t + 1) * RB)
                score = dot_nt(keys[spot], query)
                prob = jnp.exp(score - lse)
                if t == count - 1:
                    prob = jnp.where(keep, prob, 0.0)
                dprob = dot_nt(values[spot], dc)
                inner += jnp.sum(prob * dprob, 0, keepdims=True)
                more = dot(prob.astype(bf16), dc)
                dv[t] = more if dv[t] is None else dv[t] + more
                probs.append(prob)
                dprobs.append(dprob)
            total = None
            for t in range(count):
                spot = slice(t * RB, (t + 1) * RB)
                ds = (probs[t] * (dprobs[t] - inner)).astype(bf16)
                more = dot(ds, query)
                dk[t] = more if dk[t] is None else dk[t] + more
                more = dot(keys_t[:, spot], ds)
                total = more if total is None else total + more
            dq_t[i][h] = total * HD**-0.5
        dks.append(dk)
        dvs.append(dv)
    dq = [jnp.concatenate(dq_t[i], 0).T for i in range(blocks)]
    if not last:
        for i in range(blocks):
            dq_ref[i * RB : (i + 1) * RB] = dq[i]
        for t in range(tiles):
            dk_ref[t * RB : (t + 1) * RB] = jnp.concatenate([dks[h][t] for h in range(heads)], 1)
            dv_ref[t * RB : (t + 1) * RB] = jnp.concatenate([dvs[h][t] for h in range(heads)], 1)
        return
    mp = info[2]
    fresh = [jnp.where(src[mp * heads + h] < H, 0.0, 1.0) for h in range(heads)]
    for t in range(tiles):
        spot = slice(t * RB, (t + 1) * RB)
        first = t * RB < base
        parts = []
        for h in range(heads):
            lane = slice(h * HD, (h + 1) * HD)
            dqh = dqa[spot, lane] if first else dq[t - base // RB][:, lane]
            dkh = dks[h][t] + dka[spot, lane] if first else dks[h][t]
            dvh = dvs[h][t] + dva[spot, lane] if first else dvs[h][t]
            parts += [dqh, dkh, dvh * fresh[h]]
            dvr_ref[h * HD : (h + 1) * HD, spot] = dvh.T.astype(bf16)
        dm_ref[spot, :] = jnp.concatenate(parts, 1).astype(bf16)


def input_kernel(info, dm_ref, w_ref, unit_ref, na, nb, send, keep):
    core = info[0]
    cols = dm_ref.shape[1]
    sums = na[...] + nb[...]
    keep[2 * RB :] = jnp.concatenate([sums, jnp.zeros(sums.shape, f32)], 0)

    def step(i):
        half = i % 2
        spot = jnp.where(i < 2, 1 - core, core)
        at = block(2 * half + spot)
        grad = dot_nt(dm_ref[at, :], w_ref[:, :cols])
        keep[2 * RB : 2 * RB + 1] += jnp.sum(grad * unit_ref[at, :], 0, keepdims=True)
        keep[2 * RB + 1 : 2 * RB + 2] += jnp.sum(grad, 0, keepdims=True)
        keep[block(half), :] = grad

        @pl.when(i < 2)
        def _():
            send[block(half), :] = grad.astype(bf16)

    loop(4, step)
    send[2 * RB :] = keep[2 * RB :].astype(bf16)


def to_rows_kernel(info, keep, received, mine, sent):
    own = info[1]
    for out, half in ((mine, own), (sent, 1 - own)):
        at = block(half)
        out[:RB] = (keep[at, :] + received[at, :].astype(f32)).astype(out.dtype)
        if out.shape[0] > RB:
            out[RB:] = (keep[2 * RB :] + received[2 * RB :].astype(f32)).astype(out.dtype)


def output_rows_kernel(info, ka, kb, ra, rb, mine, sent):
    low = info[1] == 0
    first = ka[...] + ra[...].astype(f32)
    second = kb[...] + rb[...].astype(f32)
    mine[...] = jnp.where(low, first, second)
    sent[...] = jnp.where(low, second, first).astype(bf16)


def output_kernel(info, ra, rb, mine, received, out):
    at = block(info[0])
    resid = jnp.where(info[1] == 0, ra[at, :], rb[at, :])
    out[...] = (resid + mine[...] + received[...].astype(f32)).astype(bf16)


def qkv_grad_kernel(info, a1_ref, dm_ref, aba, abb, ca, cb, out, fw, bw):
    def step(j):
        at = block(j)
        grad = dot_tn(a1_ref[:, at], dm_ref[...])
        proj = dot_tn(aba[:, at], ca[...]) + dot_tn(abb[:, at], cb[...])
        out[at, :] = jnp.concatenate([grad, proj], 1).astype(out.dtype)

    loop(out.shape[0] // RB, step)
    starts(info, out, fw, bw)


def norm_one_kernel(info, x_ref, own, received, dra, drb, norm_ref, out, sums):
    unit, scale = norm_stats(x_ref[block(info[2]), :].astype(f32))
    grad = own[:RB] + received[:RB].astype(f32)
    dr = jnp.where(info[1] == 0, dra[...], drb[...])
    out[...] = dr + norm_back(unit, scale, norm_ref[0:1], grad)
    total = own[RB:] + received[RB:].astype(f32)
    sums[...] = total[:8]


def first_kernel(heads, info, src, d0, d1, d2, d3, out):
    mp = info[2]
    out[...] = jnp.zeros(out.shape, f32)
    for g in range(heads):
        user = jnp.int32(H)
        for h in range(H):
            user = jnp.where(src[h] == mp * heads + g, h, user)
        held = user // heads
        for r, ref in enumerate((d0, d1, d2, d3)):

            @pl.when((user < H) & (held == mp ^ r))
            def _():
                out[g * HD : (g + 1) * HD, :] = ref[block(user - held * heads, HD), :].astype(f32)


def adamw(master, moment, second, grad, rate, weighted):
    moment_new = 0.9 * moment + 0.1 * grad
    second_new = 0.999 * second + 0.001 * grad * grad
    mean_hat = moment_new / (1.0 - 0.9**ADAM_STEP)
    var_hat = second_new / (1.0 - 0.999**ADAM_STEP)
    master_new = master - rate * (mean_hat / (jnp.sqrt(var_hat) + 1e-08) + weighted * master)
    return (master_new, moment_new, second_new)


def adam_kernel(names, turned, info, full, a, b, *refs):
    ins, outs = refs[:6], refs[6:12]
    rows = a.shape[0]
    grad = a[...].astype(f32) + b[...].astype(f32)
    grad += full[block(info[4], rows), :].astype(f32)
    cols = ins[0].shape[1]
    second = grad[:, cols:]
    if turned:
        second = jnp.concatenate([second, jnp.zeros((LANES - rows, second.shape[1]), f32)], 0).T[:, :rows]
    for k, (name, part) in enumerate(zip(names, (grad[:, :cols], second))):
        new = adamw(*[r[...] for r in ins[3 * k : 3 * k + 3]], part, RATES[name], 0.1)
        for ref, value in zip(outs[3 * k : 3 * k + 3], new):
            ref[...] = value


def norm_adam_kernel(info, sums, received, w, m, s, w_out, m_out, s_out):
    total = sums[...] + received[...]
    cols = w.shape[1]
    shift = total.shape[1] - info[3] * cols
    grad = pltpu.roll(total, shift, 1)[:4, :cols]
    new = adamw(w[...], m[...], s[...], grad, RATES["norm"], 0.0)
    for ref, value in zip((w_out, m_out, s_out), new):
        ref[...] = value


def sum_kernel(a, b, out):
    out[...] = a[...] + b[...]


def swap_core(value):
    return lax.ppermute(value, "mp", [(i, i ^ 1) for i in range(4)])


def swap_x(value):
    return lax.ppermute(value, "mp", [(i, i ^ 2) for i in range(4)])


FORWARD = [(RING[i], RING[(i + 1) % 8]) for i in range(8)]
BACKWARD = [(b, a) for a, b in FORWARD]


def ahead(value):
    return lax.ppermute(value, "dp", FORWARD)


def behind(value):
    return lax.ppermute(value, "dp", BACKWARD)


def after(value, *others):
    return lax.optimization_barrier((value,) + others)[0]


class Gather:
    def __init__(self, piece):
        self.ring = lax.axis_size("dp") == len(RING)
        self.start = self.a = self.b = piece
        self.ahead, self.behind = [], []

    def step(self, *gates):
        if not self.ring:
            return
        self.a, self.b = lax.optimization_barrier((self.a, self.b) + gates)[:2]
        self.a = ahead(self.a)
        self.ahead.append(self.a)
        if len(self.behind) < 3:
            self.b = behind(self.b)
            self.behind.append(self.b)

    def pieces(self):
        if not self.ring:
            return [lax.all_gather(self.start, "dp", axis=0, tiled=True)]
        return [self.start] + self.ahead + self.behind


class Scatter:
    def __init__(self, name, info, full, fw, bw):
        self.ring = lax.axis_size("dp") == len(RING)
        self.name, self.info, self.full, self.a, self.b = name, info, full, fw, bw
        self.steps = 0

    def step(self, *gates):
        if not self.ring:
            return
        self.a = after(self.a, *gates)
        k = 4 - self.steps
        shape = (self.a.shape, bf16)
        if k in (3, 2):
            kernel = functools.partial(hop_kernel, k, 1 - k)
            self.a, self.b = call(kernel, f"{self.name}_hop{k}", (self.info,), [self.full, self.a, self.b], [shape] * 2)
        if k == 1:
            (self.a,) = call(hop_last_kernel, f"{self.name}_hop1", (self.info,), [self.full, self.a], [shape])
        self.last = self.a
        self.a = ahead(self.a)
        if k > 1:
            self.b = behind(self.b)
        self.steps += 1

    def ends(self):
        return (self.a, self.b) if self.ring else None


def update(name, info, full, ends, firsts, seconds, turned):
    first, second = name
    outs = [(w.shape, f32) for w in firsts + seconds]
    if ends is not None:
        new = call(
            functools.partial(adam_kernel, name, turned),
            f"adam_{first}",
            (info,),
            [full, *ends, *firsts, *seconds],
            outs,
        )
        return tuple(new[:3]), tuple(new[3:])
    grad = lax.psum_scatter(full.astype(f32), "dp", scatter_dimension=0, tiled=True)
    cols = firsts[0].shape[1]
    other = grad[:, cols:]
    return (
        adamw(*firsts, grad[:, :cols], RATES[first], 0.1),
        adamw(*seconds, other.T if turned else other, RATES[second], 0.1),
    )


def local(
    tokens_in,
    first_values,
    skip_source,
    grad_out,
    qkv_weight,
    proj_weight,
    fc_weight,
    down_weight,
    norm_params,
    qkv_moment,
    proj_moment,
    fc_moment,
    down_moment,
    norm_moment,
    qkv_second,
    proj_second,
    fc_second,
    down_second,
    norm_second,
):
    n = lax.axis_size("dp")
    ring = n == len(RING)
    pieces = n if ring else 1
    count, width = tokens_in.shape
    cols = qkv_weight.shape[1]
    heads = cols // (3 * HD)
    cw = heads * HD
    hid = fc_weight.shape[1]
    wide = -(-(cols + 4) // LANES) * LANES
    half = count // 2
    shard = qkv_weight.shape[0]
    info = HERE
    src = skip_source

    if ring:
        (ring_one,) = call(
            prep_one_kernel,
            "prep_one",
            (),
            [qkv_weight, norm_params],
            [((shard, wide), bf16)],
            scratch=[
                pltpu.VMEM((shard, cols), f32),
                pltpu.VMEM(norm_params.shape, f32),
                pltpu.VMEM((LANES, LANES), f32),
                pltpu.SemaphoreType.DMA((2,)),
            ],
            far=True,
        )
        proj_t, fc_low, down_t = call(
            prep_two_kernel,
            "prep_two",
            (),
            [after(proj_weight, ring_one), fc_weight, down_weight.T],
            [((shard, cw), bf16), ((shard, hid), bf16), ((shard, hid), bf16)],
            scratch=[
                pltpu.VMEM((cw, shard), f32),
                pltpu.VMEM((shard, hid), f32),
                pltpu.VMEM((shard, hid), f32),
                pltpu.VMEM((cw, LANES), f32),
                pltpu.SemaphoreType.DMA((3,)),
            ],
            far=True,
        )
    else:
        blank = jnp.zeros((shard, wide - cols - 4), bf16)
        ring_one = jnp.concatenate([qkv_weight.astype(bf16), norm_params.T.astype(bf16), blank], 1)
        proj_t, fc_low, down_t = proj_weight.T.astype(bf16), fc_weight.astype(bf16), down_weight.T.astype(bf16)
    fence = lambda *values: lax.optimization_barrier(values)
    fence = lambda *values: lax.optimization_barrier(values)
    one = Gather(ring_one)
    one.step()
    one.a, one.b, proj_t, tokens = fence(one.a, one.b, proj_t, tokens_in)
    one.step()
    proj_x = swap_x(proj_t)
    (unit_one,) = call(unit_kernel, "unit", (), [tokens], [((count, width), f32)])
    one.a, one.b, proj_x, unit_one = fence(one.a, one.b, proj_x, unit_one)
    one.step()
    if ring:
        (ring_two,) = call(
            join_kernel, "join", (), [fc_low, proj_t, proj_x], [((shard, hid + 2 * cw), bf16)]
        )
    else:
        ring_two = jnp.concatenate([fc_low, proj_t, proj_x], 1)
    two, three = Gather(ring_two), Gather(down_t)
    two.step()
    first_t = first_values.T
    first_x, first_c = swap_x(first_t), swap_core(first_t)
    one.a, one.b = fence(one.a, one.b)
    one.step()
    one.a, two.a, two.b, unit_one, first_x, three.a = fence(one.a, two.a, two.b, unit_one, first_x, three.a)
    if ring:
        one.ahead[-1] = one.a
    first_xc = swap_core(first_x)
    two.step()
    three.step()

    a1, mixed, fresh, qkv_full, norms = call(
        functools.partial(qkv_kernel, pieces, heads),
        "qkv",
        (info,),
        [unit_one, *one.pieces()],
        [
            ((count, width), bf16),
            ((count, cols), bf16),
            ((cw, count), bf16),
            ((width, wide), bf16),
            ((8, width), f32),
        ],
    )
    (values,) = call(
        functools.partial(values_kernel, heads),
        "values",
        (info, src),
        [fresh, first_t, first_c, first_x, first_xc],
        [((cw, count), bf16)],
    )

    def attend(part, mixed):
        return call(
            functools.partial(attend_kernel, heads, part * half),
            f"attend{part}",
            (),
            [mixed, values],
            [((half, cw), bf16), ((8, half), f32)],
        )

    ctx_a, lse_a = attend(0, mixed)
    xa, ca = swap_x(ctx_a), swap_core(ctx_a)
    ctx_b, lse_b = attend(1, after(mixed, ctx_a))
    xb, cb = swap_x(ctx_b), swap_core(ctx_b)
    xca, xcb = swap_core(xa), swap_core(xb)
    two.step()
    three.step()
    two.step()
    three.step()
    start, xca, xcb, two_last, three.a, three.b = fence(two.start, xca, xcb, two.a, three.a, three.b)
    three.step()
    context, lse = (ctx_a, ctx_b), (lse_a, lse_b)
    wf, own_w, across_w = call(
        functools.partial(assemble_two_kernel, pieces),
        "assemble_two",
        (info,),
        [start, *two.pieces()[1:]] if ring else two.pieces(),
        [((width, hid), bf16), ((cw, width), bf16), ((cw, width), bf16)],
        scratch=[pltpu.VMEM((width, 2 * cw), bf16)],
    )
    pair = own_w, swap_core(own_w), across_w, swap_core(across_w)

    def mlp(part, norms, contexts):
        return call(
            functools.partial(mlp_kernel, part),
            f"mlp{part}",
            (),
            [tokens, norms, *contexts, *pair, wf],
            [
                ((half, width), f32),
                ((half, width), f32),
                ((half, width), bf16),
                ((half, hid), bf16),
                ((half, hid), f32),
            ],
        )

    def mlp_back(part, grad):
        return call(
            functools.partial(mlp_back_kernel, part),
            f"mlp_back{part}",
            (info,),
            [grad, unit_two[part], slope[part], wf, wd],
            [((half, hid), bf16)] + [((RB // 2, width), bf16)] * 2 + [((RB, width), f32), ((8, width), f32)],
        )

    def mlp_out(part, gate):
        return call(
            mlp_out_kernel,
            f"mlp_out{part}",
            (info,),
            [after(act[part], gate), wd],
            [((RB, width), bf16), ((RB, width), f32)],
        )

    def add(part, keep, *received):
        return call(add_kernel, f"add{part}", (), [keep, *received], [((RB, width), bf16)])[0]

    forward_a = mlp(0, norms, (ctx_a, ca, xa, xca))
    forward_b = mlp(1, after(norms, forward_a[0]), (ctx_b, cb, xb, xcb))
    resid, unit_two, a2, act, slope = zip(forward_a, forward_b)
    start, last = fence(three.start, act[1])
    (wd,) = call(
        functools.partial(assemble_three_kernel, pieces),
        "assemble_three",
        (info,),
        [start, *three.pieces()[1:]] if ring else three.pieces(),
        [((width, hid), bf16)],
    )
    dpre_a, top_a, bottom_a, dkeep_a, nacc_a = mlp_back(0, after(grad_out, act[1]))
    received_a = swap_core(top_a), swap_core(bottom_a)
    dpre_b, top_b, bottom_b, dkeep_b, nacc_b = mlp_back(1, after(grad_out, dpre_a))
    mine_a = add(0, after(dkeep_a, dpre_b), *received_a)
    received_b = swap_core(top_b), swap_core(bottom_b)
    across_a = swap_x(mine_a)

    piece = lambda w: [((width // pieces if ring else 16, w), bf16)] * 2
    mlp_grad, mlp_fw, mlp_bw = call(
        mlp_grad_kernel,
        "mlp_grad",
        (info,),
        [after(a2[0], mine_a), a2[1], dpre_a, dpre_b, grad_out, act[0], act[1]],
        [((width, 2 * hid), bf16 if ring else f32)] + piece(2 * hid),
    )
    mlp_sum = Scatter("mlp", info, mlp_grad, mlp_fw, mlp_bw)
    mlp_sum.step()
    mine_b = add(1, after(dkeep_b, mlp_grad), *received_b)
    ysend_a, ykeep_a = mlp_out(0, mine_b)
    ysend_b, ykeep_b = mlp_out(1, ysend_a)
    yreceived_a, yreceived_b = swap_core(ysend_a), swap_core(ysend_b)
    across_a, mine_b, ykeep_b = fence(across_a, mine_b, ykeep_b)
    across_b = swap_x(mine_b)

    def norm_two(part, mine, across):
        return call(
            functools.partial(norm_two_kernel, part),
            f"norm_two{part}",
            (info,),
            [resid[part], mine, across, grad_out, norms],
            [((RB, width), f32)] + [((RB // 2, width), bf16)] * 2,
        )

    def attend_back(part, own, partner, before):
        outs = [((half, width), bf16)]
        if part:
            outs += [((count, cols), bf16), ((cw, count), bf16)]
        else:
            outs += [((half, cw), f32)] * 3
        return call(
            functools.partial(attend_back_kernel, heads, part * half, bool(part)),
            f"attend_back{part}",
            (info, src),
            [mixed, values, *own, *partner, own_w, lse[part], *before],
            outs,
            vmem=24,
        )

    dr_a, *ab_a = norm_two(0, after(mine_a, mine_b), across_a)

    rows_mine, rows_sent = call(
        output_rows_kernel,
        "output_rows",
        (info,),
        [after(ykeep_a, dr_a), ykeep_b, yreceived_a, yreceived_b],
        [((RB, width), f32), ((RB, width), bf16)],
    )
    partner = [swap_core(v) for v in ab_a]
    mlp_sum.a, mlp_sum.b, rows_sent, *partner = fence(mlp_sum.a, mlp_sum.b, rows_sent, *partner)
    ab_one, dq, dk, dv = attend_back(0, ab_a, partner, [])
    mlp_sum.step()
    dr_b, *ab_b = norm_two(1, after(mine_b, dq), across_b)
    rows_received = swap_x(after(rows_sent, dr_b))
    ab_two, dmixed, dreused = attend_back(1, ab_b, [swap_core(v) for v in ab_b], [dq, dk, dv])
    mlp_sum.a, mlp_sum.b, dmixed, rows_received = fence(mlp_sum.a, mlp_sum.b, dmixed, rows_received)
    mlp_sum.step()

    qkv_grad, qkv_fw, qkv_bw = call(
        qkv_grad_kernel,
        "qkv_grad",
        (info,),
        [a1, after(dmixed, mlp_sum.last) if ring else dmixed, ab_one, ab_two, context[0], context[1]],
        [((width, cols + cw), bf16 if ring else f32)] + piece(cols + cw),
    )
    qkv_sum = Scatter("qkv", info, qkv_grad, qkv_fw, qkv_bw)
    qkv_sum.step()
    isend, ikeep = call(
        input_kernel,
        "input",
        (info,),
        [after(dmixed, qkv_fw), qkv_full, unit_one, nacc_a, nacc_b],
        [((half + 16, width), bf16), ((half + 16, width), f32)],
    )
    mine, sent = call(
        to_rows_kernel,
        "to_rows",
        (info,),
        [ikeep, swap_core(isend)],
        [((RB + 16, width), f32), ((RB + 16, width), bf16)],
    )
    across = swap_x(sent)
    mlp_sum.a, mlp_sum.b, qkv_sum.a, qkv_sum.b = fence(mlp_sum.a, mlp_sum.b, qkv_sum.a, qkv_sum.b)
    qkv_sum.step()
    mlp_sum.step()
    qkv_sum.a, qkv_sum.b = fence(qkv_sum.a, qkv_sum.b)
    qkv_sum.step()
    dx, dc = swap_x(dreused), swap_core(dreused)
    qkv_sum.a, qkv_sum.b, across = fence(qkv_sum.a, qkv_sum.b, across)
    qkv_sum.step()
    input_grad, sums = call(
        norm_one_kernel,
        "norm_one",
        (info,),
        [tokens, mine, across, dr_a, dr_b, norms],
        [((RB, width), f32), ((8, width), f32)],
    )
    (block_out,) = call(
        output_kernel,
        "output",
        (info,),
        [resid[0], resid[1], after(rows_mine, input_grad), rows_received],
        [((RB, width), bf16)],
    )
    dxc = swap_core(dx)
    mlp_ends = mlp_sum.ends()
    if ring:
        hop = lambda value, bit: lax.ppermute(value, "dp", [(i, i ^ bit) for i in range(n)])
        for bit in (1, 2):
            (sums,) = call(sum_kernel, f"sum{bit}", (), [sums, hop(sums, bit)], [(sums.shape, f32)])
        received = hop(sums, 4)
    fc_new, down_new = update(
        ("fc", "down"),
        info,
        mlp_grad,
        mlp_ends,
        [fc_weight, fc_moment, fc_second],
        [down_weight.T, down_moment.T, down_second.T],
        False,
    )
    down_new = tuple(v.T for v in down_new)
    (first_grad,) = call(
        functools.partial(first_kernel, heads),
        "first",
        (info, src),
        [dreused, dc, dx, dxc],
        [((cw, count), f32)],
    )
    qkv_new, proj_new = update(
        ("qkv", "proj"),
        info,
        qkv_grad,
        qkv_sum.ends(),
        [after(qkv_weight, first_grad), qkv_moment, qkv_second],
        [proj_weight, proj_moment, proj_second],
        True,
    )
    if ring:
        norm_new = call(
            norm_adam_kernel,
            "adam_norm",
            (info,),
            [sums, received, norm_params, norm_moment, norm_second],
            [(norm_params.shape, f32)] * 3,
        )
    else:
        own = lax.psum_scatter(sums, "dp", scatter_dimension=1, tiled=True)[:4]
        norm_new = adamw(norm_params, norm_moment, norm_second, own, RATES["norm"], 0.0)
    return (block_out, input_grad, first_grad.T, *qkv_new, *proj_new, *fc_new, *down_new, *norm_new)


def solution(mesh):
    both = P("dp", "mp")
    turned = P("mp", "dp")
    rows = P("dp", None)
    every = P(None, "dp")
    state = (both, turned, both, turned, every)
    return jax.shard_map(
        local,
        mesh=mesh,
        in_specs=(rows, both, P(), rows) + state * 3,
        out_specs=(P(("dp", "mp"), None), P(("dp", "mp"), None), both)
        + (both,) * 3
        + (turned,) * 3
        + (both,) * 3
        + (turned,) * 3
        + (every,) * 3,
        check_vma=False,
    )
```

time: 249 us -> 174 us (0.70)
  local copies, waits for them, and re-layouts: 59.8 us -> 7.21 us
  other arithmetic: 28.9 us -> 0 us
  waiting for transfers between devices: 37.8 us -> 56.9 us
  Pallas kernels: 59.6 us -> 51.3 us
  between operations: 6.62 us -> 1.27 us
    unnamed x211 -> x50, local copies, waits for them, and re-layouts: 50.9 us -> 7.21 us
    convert_element_type x16 -> x0, other arithmetic: 20.1 us -> none  [the longest x6 5.19 us: scatter_ring(): a = (a.astype(f32) + part(k).astype(f32)).astype(bf16)]
    ppermute x35 -> x38, waiting for transfers between devices: 29.5 us -> 47.7 us  [the longest x20 26.4 us: ahead(): return lax.ppermute(value, 'dp', FORWARD)]
    pallas_call x14 -> x41, Pallas kernels: 59.6 us -> 51.3 us  [call(): pl.pallas_call(kernel, in_specs=[smem] * len(scalars) + [given] * len(ins...]
    sub x5 -> x0, other arithmetic: 4.61 us -> none  [adamw(): master - rate * (mean_hat / (jnp.sqrt(var_hat) + 1e-08) + weighted * master)]
    add x4 -> x0, other arithmetic: 2.73 us -> none  [the longest x2 1.12 us: scatter_ring(): return a.astype(f32) + b.astype(f32) + part(0).astype(f32)]
    ppermute x10 -> x9, starting transfers between devices: 9.25 us -> 11.9 us  [swap_x(): return lax.ppermute(value, 'mp', [(i, i ^ 2) for i in range(4)])]
    ppermute x35 -> x38, starting transfers between devices: 42.2 us -> 40.2 us  [the longest x20 29 us: ahead(): return lax.ppermute(value, 'dp', FORWARD)]
  transfers between devices with their start and end apart: 62 -> 68, of which waited for: 18 -> 25; matrix products, arithmetic and copies ran while one was open for 23% -> 0% of each run, Pallas kernels for 18% -> 24%
where the time goes in v2:
time: 174 us; the launch traced here: 173 us
  waiting for transfers between devices  56.9 us (33%)
  starting transfers between devices  56.7 us (33%)
  Pallas kernels  51.3 us (29%)
  local copies, waits for them, and re-layouts  7.21 us (4%)
    pallas_call x41, Pallas kernels, call(): pl.pallas_call(kernel, in_specs=[smem] * len(scalars) + [given] * len(ins...  51.3 us
    ppermute x20, starting transfers between devices, ahead(): return lax.ppermute(value, 'dp', FORWARD)  29 us
    ppermute x20, waiting for transfers between devices, ahead(): return lax.ppermute(value, 'dp', FORWARD)  26.4 us
    ppermute x15, waiting for transfers between devices, behind(): return lax.ppermute(value, 'dp', BACKWARD)  16.1 us
    ppermute x9, starting transfers between devices, swap_x(): return lax.ppermute(value, 'mp', [(i, i ^ 2) for i in range(4)])  11.9 us
    ppermute x15, starting transfers between devices, behind(): return lax.ppermute(value, 'dp', BACKWARD)  8.14 us
    ppermute x9, waiting for transfers between devices, swap_x(): return lax.ppermute(value, 'mp', [(i, i ^ 2) for i in range(4)])  8.02 us
    unnamed x50, local copies, waits for them, and re-layouts  7.21 us
  transfers between devices with their start and end apart: 68, of which 25 were waited for; matrix products, arithmetic and copies ran while one was open for 0% of the time, Pallas kernels for 24%

profile of v2, /device:TPU:0, one launch (start us, length us, event | category | flops | bytes accessed | tf_op | source)
XLA Modules:
  0.0 173.4 jit_solution(12640884876338735709)
XLA Ops:
  2.8 3.1 %collective-permute-start = (bf16[96,640]{1,0:T(8,128)(2,1)S(1)}, bf16[96,640]{1,0:T(8,128)(2,1)S(1)}, u32[]{:S(2)}, u32[]{:S(2)}) collective-permute-start(bf16[96,640]{1,0:T(8,128)(2,1)S(1)} %prep_one.1.refs_1_), channel_id=1, source_target_pairs={{0,8},{8,16},{16,24},{24,28},{28,20},{20,12},{12,4},{4,0},{1,9},{9... | collective-permute-start | bytes 368648 | tf_op jit(solution)/shard_map/ppermute | solution.py:544
  5.9 1.9 %collective-permute-start.10 = (bf16[192,1024]{1,0:T(8,128)(2,1)}, bf16[192,1024]{1,0:T(8,128)(2,1)S(1)}, u32[]{:S(2)}, u32[]{:S(2)}) collective-permute-start(bf16[192,1024]{1,0:T(8,128)(2,1)} %bitcast.10), channel_id=1, source_target_pairs={{0,2},{1,3},{2,0},{3,1},{4,6},{5,7},{6,4},{7,5},{8,10},{9,11},{10,... | collective-permute-start | bytes 1179656 | tf_op jit(solution)/shard_map/ppermute | solution.py:536
  8.8 1.0 copy-done.5
  11.1 1.6 collective-permute-start.2
  13.1 1.1 collective-permute-start.4
  14.3 1.4 copy-done.1
  16.6 1.1 collective-permute-done.4.across
  17.7 1.7 %collective-permute-start.5 = (bf16[96,640]{1,0:T(8,128)(2,1)S(1)}, bf16[96,640]{1,0:T(8,128)(2,1)S(1)}, u32[]{:S(2)}, u32[]{:S(2)}) collective-permute-start(bf16[96,640]{1,0:T(8,128)(2,1)S(1)} %collective-permute-done.2.refs_3_), channel_id=1, source_target_pairs={{0,8},{8,16},{16,24},{24,28},{28,20},{20,12},{12,4},{4,0},{1,9},{9... | collective-permute-start | bytes 368648 | tf_op jit(solution)/shard_map/ppermute | solution.py:544
  19.8 1.8 %collective-permute-start.8 = (bf16[96,1152]{1,0:T(8,128)(2,1)S(1)}, bf16[96,1152]{1,0:T(8,128)(2,1)S(1)}, u32[]{:S(2)}, u32[]{:S(2)}) collective-permute-start(bf16[96,1152]{1,0:T(8,128)(2,1)S(1)} %join.1.refs_0_), channel_id=1, source_target_pairs={{0,8},{8,16},{16,24},{24,28},{28,20},{20,12},{12,4},{4,0},{1,9},{9... | collective-permute-start | bytes 663560 | tf_op jit(solution)/shard_map/ppermute | solution.py:544
  21.9 2.0 %collective-permute-done.5.refs_4_ = bf16[96,640]{1,0:T(8,128)(2,1)S(1)} collective-permute-done((bf16[96,640]{1,0:T(8,128)(2,1)S(1)}, bf16[96,640]{1,0:T(8,128)(2,1)S(1)}, u32[]{:S(2)}, u32[]{:S(2)}) %collective-permute-start.5) | collective-permute-done | bytes 122912 | tf_op jit(solution)/shard_map/ppermute | solution.py:544
  23.9 1.5 collective-permute-done.6.refs_8_
  25.4 1.6 collective-permute-start.7
  27.9 2.4 %collective-permute-done.7.refs_5_ = bf16[96,640]{1,0:T(8,128)(2,1)S(1)} collective-permute-done((bf16[96,640]{1,0:T(8,128)(2,1)S(1)}, bf16[96,640]{1,0:T(8,128)(2,1)S(1)}, u32[]{:S(2)}, u32[]{:S(2)}) %collective-permute-start.7) | collective-permute-done | bytes 122912 | tf_op jit(solution)/shard_map/ppermute | solution.py:544
  30.3 1.6 collective-permute-start.18
  32.3 1.6 collective-permute-start.23
  33.9 4.6 %collective-permute-done.18.refs_2_ = bf16[96,1152]{1,0:T(8,128)(2,1)S(1)} collective-permute-done((bf16[96,1152]{1,0:T(8,128)(2,1)S(1)}, bf16[96,1152]{1,0:T(8,128)(2,1)S(1)}, u32[]{:S(2)}, u32[]{:S(2)}) %collective-permute-start.18) | collective-permute-done | bytes 221216 | tf_op jit(solution)/shard_map/ppermute | solution.py:544
  39.4 1.6 collective-permute-start.20
  41.9 2.4 %qkv.1 = (bf16[1024,768]{1,0:T(8,128)(2,1)S(1)}, bf16[1024,576]{1,0:T(8,128)(2,1)S(1)}, bf16[192,1024]{1,0:T(8,128)(2,1)S(1)}, bf16[768,640]{1,0:T(8,128)(2,1)S(1)}, f32[8,768]{1,0:T(8,128)S(1)}) custom-call(f32[1024,768]{1,0:T(8,128)S(1)} %unit.1.refs_0_.refs_2_, bf16[96,640]{1,0:T(8,128)(2,1)S(1)} %prep_one.1.refs_1_, ...), custom_call_target="tpu_custom_call" | custom-call | flops 1 | bytes 1 | tf_op jit(solution)/shard_map/qkv/pallas_call | solution.py:65
  45.1 1.8 %attend0.1 = (bf16[512,192]{1,0:T(8,128)(2,1)S(1)}, f32[8,512]{1,0:T(8,128)S(1)}) custom-call(bf16[1024,576]{1,0:T(8,128)(2,1)S(1)} %get-tuple-element.214.m_ref.refs_1_, bf16[192,1024]{1,0:T(8,128)(2,1)S(1)} %values.1.v_ref.refs_2_), custom_call_target="tpu_custom_call" | custom-call | flops 1 | bytes 1 | tf_op jit(solution)/shard_map/attend0/pallas_call | solution.py:65
  46.9 1.5 collective-permute-start.14
  48.4 3.9 %attend1.1 = (bf16[512,192]{1,0:T(8,128)(2,1)S(1)}, f32[8,512]{1,0:T(8,128)S(1)}) custom-call(bf16[1024,576]{1,0:T(8,128)(2,1)S(1)} %get-tuple-element.214.m_ref.refs_1_, bf16[192,1024]{1,0:T(8,128)(2,1)S(1)} %values.1.v_ref.refs_2_), custom_call_target="tpu_custom_call" | custom-call | flops 1 | bytes 1 | tf_op jit(solution)/shard_map/attend1/pallas_call | solution.py:65
  53.0 1.6 collective-permute-start.25
  55.0 1.6 collective-permute-start.22
  56.6 2.7 %collective-permute-done.16.c2 = bf16[512,192]{1,0:T(8,128)(2,1)S(1)} collective-permute-done((bf16[512,192]{1,0:T(8,128)(2,1)S(1)}, bf16[512,192]{1,0:T(8,128)(2,1)S(1)}, u32[]{:S(2)}, u32[]{:S(2)}) %collective-permute-start.16) | collective-permute-done | bytes 196640 | tf_op jit(solution)/shard_map/ppermute | solution.py:536
  59.7 1.6 collective-permute-start.27
  61.8 3.9 %collective-permute-done.27.refs_3_ = bf16[96,768]{1,0:T(8,128)(2,1)S(1)} collective-permute-done((bf16[96,768]{1,0:T(8,128)(2,1)S(1)}, bf16[96,768]{1,0:T(8,128)(2,1)S(1)}, u32[]{:S(2)}, u32[]{:S(2)}) %collective-permute-start.27) | collective-permute-done | bytes 147488 | tf_op jit(solution)/shard_map/ppermute | solution.py:544
  65.7 1.3 collective-permute-done.28.refs_7_
  68.5 1.6 collective-permute-start.32
  70.0 3.4 %mlp0.1 = (f32[512,768]{1,0:T(8,128)S(1)}, f32[512,768]{1,0:T(8,128)S(1)}, bf16[512,768]{1,0:T(8,128)(2,1)S(1)}, bf16[512,768]{1,0:T(8,128)(2,1)S(1)}, f32[512,768]{1,0:T(8,128)S(1)}) custom-call(bf16[1024,768]{1,0:T(8,128)(2,1)S(1)} %copy-done.2, f32[8,768]{1,0:T(8,128)S(1)} %get-tuple-element.236.norm_ref.refs_4_.refs_5_, ...), custom_call_target="tpu_custom_call" | custom-call | flops 1 | bytes 1 | tf_op jit(solution)/shard_map/mlp0/pallas_call | solution.py:65
  73.5 3.4 %mlp1.1 = (f32[512,768]{1,0:T(8,128)S(1)}, f32[512,768]{1,0:T(8,128)S(1)}, bf16[512,768]{1,0:T(8,128)(2,1)S(1)}, bf16[512,768]{1,0:T(8,128)(2,1)S(1)}, f32[512,768]{1,0:T(8,128)S(1)}) custom-call(bf16[1024,768]{1,0:T(8,128)(2,1)S(1)} %copy-done.2, f32[8,768]{1,0:T(8,128)S(1)} %get-tuple-element.236.norm_ref.refs_4_.refs_5_, ...), custom_call_target="tpu_custom_call" | custom-call | flops 1 | bytes 1 | tf_op jit(solution)/shard_map/mlp1/pallas_call | solution.py:65
  77.0 1.3 copy-done
  78.3 1.9 %mlp_back0.1 = (bf16[512,768]{1,0:T(8,128)(2,1)S(1)}, bf16[128,768]{1,0:T(8,128)(2,1)S(1)}, bf16[128,768]{1,0:T(8,128)(2,1)S(1)}, f32[256,768]{1,0:T(8,128)S(1)}, f32[8,768]{1,0:T(8,128)S(1)}) custom-call(bf16[1024,768]{1,0:T(8,128)(2,1)S(1)} %copy-done, f32[512,768]{1,0:T(8,128)S(1)} %get-tuple-element.242.refs_1_, ...), custom_call_target="tpu_custom_call" | custom-call | flops 1 | bytes 1 | tf_op jit(solution)/shard_map/mlp_back0/pallas_call | solution.py:65
  80.8 1.9 %mlp_back1.1 = (bf16[512,768]{1,0:T(8,128)(2,1)S(1)}, bf16[128,768]{1,0:T(8,128)(2,1)S(1)}, bf16[128,768]{1,0:T(8,128)(2,1)S(1)}, f32[256,768]{1,0:T(8,128)S(1)}, f32[8,768]{1,0:T(8,128)S(1)}) custom-call(bf16[1024,768]{1,0:T(8,128)(2,1)S(1)} %copy-done, f32[512,768]{1,0:T(8,128)S(1)} %get-tuple-element.248.refs_1_, ...), custom_call_target="tpu_custom_call" | custom-call | flops 1 | bytes 1 | tf_op jit(solution)/shard_map/mlp_back1/pallas_call | solution.py:65
  83.4 1.6 collective-permute-start.37
  84.9 3.1 %mlp_grad.1 = (bf16[768,1536]{1,0:T(8,128)(2,1)S(1)}, bf16[96,1536]{1,0:T(8,128)(2,1)S(1)}, bf16[96,1536]{1,0:T(8,128)(2,1)S(1)}) custom-call(bf16[512,768]{1,0:T(8,128)(2,1)S(1)} %get-tuple-element.257.refs_0_, bf16[512,768]{1,0:T(8,128)(2,1)S(1)} %get-tuple-element.258.refs_1_, bf16[512,768]{1,0:T(8,128)(2,1)S(1)} %get-tuple-element.246.refs_2_, ...), custom_call_target="tpu_custom_call" | custom-call | flops 1 | bytes 1 | tf_op jit(solution)/shard_map/mlp_grad/pallas_call | solution.py:65
  90.4 4.1 %collective-permute-done.37.refs_2_ = bf16[256,768]{1,0:T(8,128)(2,1)S(1)} collective-permute-done((bf16[256,768]{1,0:T(8,128)(2,1)S(1)}, bf16[256,768]{1,0:T(8,128)(2,1)S(1)}, u32[]{:S(2)}, u32[]{:S(2)}) %collective-permute-start.37) | collective-permute-done | bytes 393248 | tf_op jit(solution)/shard_map/ppermute | solution.py:536
  94.5 1.5 collective-permute-start.46
  96.0 1.5 collective-permute-start.40
  99.4 4.5 %collective-permute-done.40.refs_1_ = bf16[96,1536]{1,0:T(8,128)(2,1)S(1)} collective-permute-done((bf16[96,1536]{1,0:T(8,128)(2,1)S(1)}, bf16[96,1536]{1,0:T(8,128)(2,1)S(1)}, u32[]{:S(2)}, u32[]{:S(2)}) %collective-permute-start.40) | collective-permute-done | bytes 294944 | tf_op jit(solution)/shard_map/ppermute | solution.py:544
  103.9 1.2 collective-permute-done.41.refs_2_
  105.1 3.8 %attend_back0.1 = (bf16[512,768]{1,0:T(8,128)(2,1)S(1)}, f32[512,192]{1,0:T(8,128)S(1)}, f32[512,192]{1,0:T(8,128)S(1)}, f32[512,192]{1,0:T(8,128)S(1)}) custom-call(s32[12]{0:T(128)S(1)} %copy-done.20, bf16[1024,576]{1,0:T(8,128)(2,1)S(1)} %get-tuple-element.214.m_ref.refs_1_, bf16[192,1024]{1,0:T(8,128)(2,1)S(1)} %values.1.v_ref.refs_2_, ...), custom_call_target="tpu_custom_call" | custom-call | flops 1 | bytes 1 | tf_op jit(solution)/shard_map/attend_back0/pallas_call | solution.py:65
  110.3 1.5 collective-permute-start.44
  114.1 6.2 %attend_back1.1 = (bf16[512,768]{1,0:T(8,128)(2,1)S(1)}, bf16[1024,576]{1,0:T(8,128)(2,1)S(1)}, bf16[192,1024]{1,0:T(8,128)(2,1)S(1)}) custom-call(s32[12]{0:T(128)S(1)} %copy-done.20, bf16[1024,576]{1,0:T(8,128)(2,1)S(1)} %get-tuple-element.214.m_ref.refs_1_, bf16[192,1024]{1,0:T(8,128)(2,1)S(1)} %values.1.v_ref.refs_2_, ...), custom_call_target="tpu_custom_call" | custom-call | flops 1 | bytes 1 | tf_op jit(solution)/shard_map/attend_back1/pallas_call | solution.py:65
  120.5 2.5 %qkv_grad.1 = (bf16[768,768]{1,0:T(8,128)(2,1)S(1)}, bf16[96,768]{1,0:T(8,128)(2,1)S(1)}, bf16[96,768]{1,0:T(8,128)(2,1)S(1)}) custom-call(bf16[1024,768]{1,0:T(8,128)(2,1)S(1)} %get-tuple-element.300.refs_0_, bf16[1024,576]{1,0:T(8,128)(2,1)S(1)} %get-tuple-element.308.refs_1_.refs_0_, bf16[512,768]{1,0:T(8,128)(2,1)S(1)} %get-tuple-element.305.refs_2_, ...), custom_call_target="tpu_custom_call" | custom-call | flops 1 | bytes 1 | tf_op jit(solution)/shard_map/qkv_grad/pallas_call | solution.py:65
  123.0 2.2 %input.1 = (bf16[528,768]{1,0:T(8,128)(2,1)S(1)}, f32[528,768]{1,0:T(8,128)S(1)}) custom-call(bf16[1024,576]{1,0:T(8,128)(2,1)S(1)} %get-tuple-element.308.refs_1_.refs_0_, bf16[768,640]{1,0:T(8,128)(2,1)S(1)} %get-tuple-element.309.refs_1_, f32[1024,768]{1,0:T(8,128)S(1)} %unit.1.refs_0_.refs_2_, f32[8,768]{1,0:T(8,128)S(1)} %get-tuple-element.310.refs_3_, ...), custom_call_target="tpu_custom_call" | custom-call | flops 1 | bytes 1 | tf_op jit(solution)/shard_map/input/pallas_call | solution.py:65
  125.5 1.5 collective-permute-start.53
  127.6 1.5 collective-permute-start.51
  129.0 1.5 collective-permute-start.61
  130.5 1.7 collective-permute-done.53.refs_1_
  132.7 6.4 %collective-permute-done.54.refs_2_ = bf16[96,768]{1,0:T(8,128)(2,1)S(1)} collective-permute-done((bf16[96,768]{1,0:T(8,128)(2,1)S(1)}, bf16[96,768]{1,0:T(8,128)(2,1)S(1)}, u32[]{:S(2)}, u32[]{:S(2)}) %collective-permute-start.54) | collective-permute-done | bytes 147488 | tf_op jit(solution)/shard_map/ppermute | solution.py:548
  139.8 1.4 collective-permute-start.56
  141.4 1.5 collective-permute-start.59
  143.0 1.4 collective-permute-done.55.refs_1_
  146.7 5.0 %collective-permute-done.57.refs_1_ = bf16[96,768]{1,0:T(8,128)(2,1)S(1)} collective-permute-done((bf16[96,768]{1,0:T(8,128)(2,1)S(1)}, bf16[96,768]{1,0:T(8,128)(2,1)S(1)}, u32[]{:S(2)}, u32[]{:S(2)}) %collective-permute-start.57) | collective-permute-done | bytes 147488 | tf_op jit(solution)/shard_map/ppermute | solution.py:544
  151.7 1.3 collective-permute-start.58
  153.0 3.8 %collective-permute-done.58.refs_2_ = bf16[96,768]{1,0:T(8,128)(2,1)S(1)} collective-permute-done((bf16[96,768]{1,0:T(8,128)(2,1)S(1)}, bf16[96,768]{1,0:T(8,128)(2,1)S(1)}, u32[]{:S(2)}, u32[]{:S(2)}) %collective-permute-start.58) | collective-permute-done | bytes 147488 | tf_op jit(solution)/shard_map/ppermute | solution.py:548
  157.4 1.5 norm_one.1
  159.0 1.6 collective-permute-start.65
  160.6 2.3 %collective-permute-done.65.b = f32[8,768]{1,0:T(8,128)S(1)} collective-permute-done((f32[8,768]{1,0:T(8,128)S(1)}, f32[8,768]{1,0:T(8,128)S(1)}, u32[]{:S(2)}, u32[]{:S(2)}) %collective-permute-start.65) | collective-permute-done | bytes 24608 | tf_op jit(solution)/shard_map/ppermute | solution.py:938
  162.9 1.1 collective-permute-start.66
  164.0 2.7 %collective-permute-done.66.b = f32[8,768]{1,0:T(8,128)S(1)} collective-permute-done((f32[8,768]{1,0:T(8,128)S(1)}, f32[8,768]{1,0:T(8,128)S(1)}, u32[]{:S(2)}, u32[]{:S(2)}) %collective-permute-start.66) | collective-permute-done | bytes 24608 | tf_op jit(solution)/shard_map/ppermute | solution.py:938
  167.0 1.6 first.1
  168.7 1.6 adam_fc.1
  172.2 1.3 adam_qkv.1
  (163 shorter events, 30.3 us)
Async XLA Ops:
  2.8 8.3 %collective-permute-start = (bf16[96,640]{1,0:T(8,128)(2,1)S(1)}, bf16[96,640]{1,0:T(8,128)(2,1)S(1)}, u32[]{:S(2)}, u32[]{:S(2)}) collective-permute-start(bf16[96,640]{1,0:T(8,128)(2,1)S(1)} %prep_one.1.refs_1_), channel_id=1, source_target_pairs={{0,8},{8,16},{16,24},{24,28},{28,20},{20,12},{12,4},{4,0},{1,9},{9... | collective-permute-start | bytes 368648 | tf_op jit(solution)/shard_map/ppermute | solution.py:544
  5.9 5.2 %collective-permute-start.1 = (bf16[96,640]{1,0:T(8,128)(2,1)S(1)}, bf16[96,640]{1,0:T(8,128)(2,1)S(1)}, u32[]{:S(2)}, u32[]{:S(2)}) collective-permute-start(bf16[96,640]{1,0:T(8,128)(2,1)S(1)} %prep_one.1.refs_1_), channel_id=1, source_target_pairs={{8,0},{16,8},{24,16},{28,24},{20,28},{12,20},{4,12},{0,4},{9,1},{1... | collective-permute-start | bytes 368648 | tf_op jit(solution)/shard_map/ppermute | solution.py:548
  5.9 21.1 %collective-permute-start.10 = (bf16[192,1024]{1,0:T(8,128)(2,1)}, bf16[192,1024]{1,0:T(8,128)(2,1)S(1)}, u32[]{:S(2)}, u32[]{:S(2)}) collective-permute-start(bf16[192,1024]{1,0:T(8,128)(2,1)} %bitcast.10), channel_id=1, source_target_pairs={{0,2},{1,3},{2,0},{3,1},{4,6},{5,7},{6,4},{7,5},{8,10},{9,11},{10,... | collective-permute-start | bytes 1179656 | tf_op jit(solution)/shard_map/ppermute | solution.py:536
  11.1 6.7 %collective-permute-start.2 = (bf16[96,640]{1,0:T(8,128)(2,1)S(1)}, bf16[96,640]{1,0:T(8,128)(2,1)S(1)}, u32[]{:S(2)}, u32[]{:S(2)}) collective-permute-start(bf16[96,640]{1,0:T(8,128)(2,1)S(1)} %collective-permute-done.refs_2_), channel_id=1, source_target_pairs={{0,8},{8,16},{16,24},{24,28},{28,20},{20,12},{12,4},{4,0},{1,9},{9... | collective-permute-start | bytes 368648 | tf_op jit(solution)/shard_map/ppermute | solution.py:544
  12.7 5.0 %collective-permute-start.3 = (bf16[96,640]{1,0:T(8,128)(2,1)S(1)}, bf16[96,640]{1,0:T(8,128)(2,1)S(1)}, u32[]{:S(2)}, u32[]{:S(2)}) collective-permute-start(bf16[96,640]{1,0:T(8,128)(2,1)S(1)} %collective-permute-done.1.refs_6_), channel_id=1, source_target_pairs={{8,0},{16,8},{24,16},{28,24},{20,28},{12,20},{4,12},{0,4},{9,1},{1... | collective-permute-start | bytes 368648 | tf_op jit(solution)/shard_map/ppermute | solution.py:548
  13.1 4.6 %collective-permute-start.4 = (bf16[96,192]{1,0:T(8,128)(2,1)S(1)}, bf16[96,192]{1,0:T(8,128)(2,1)S(1)}, u32[]{:S(2)}, u32[]{:S(2)}) collective-permute-start(bf16[96,192]{1,0:T(8,128)(2,1)S(1)} %get-tuple-element.195.own), channel_id=1, source_target_pairs={{0,2},{1,3},{2,0},{3,1},{4,6},{5,7},{6,4},{7,5},{8,10},{9,11},{10,... | collective-permute-start | bytes 110600 | tf_op jit(solution)/shard_map/ppermute | solution.py:536
  17.7 6.2 %collective-permute-start.5 = (bf16[96,640]{1,0:T(8,128)(2,1)S(1)}, bf16[96,640]{1,0:T(8,128)(2,1)S(1)}, u32[]{:S(2)}, u32[]{:S(2)}) collective-permute-start(bf16[96,640]{1,0:T(8,128)(2,1)S(1)} %collective-permute-done.2.refs_3_), channel_id=1, source_target_pairs={{0,8},{8,16},{16,24},{24,28},{28,20},{20,12},{12,4},{4,0},{1,9},{9... | collective-permute-start | bytes 368648 | tf_op jit(solution)/shard_map/ppermute | solution.py:544
  19.5 6.0 %collective-permute-start.6 = (bf16[96,640]{1,0:T(8,128)(2,1)S(1)}, bf16[96,640]{1,0:T(8,128)(2,1)S(1)}, u32[]{:S(2)}, u32[]{:S(2)}) collective-permute-start(bf16[96,640]{1,0:T(8,128)(2,1)S(1)} %collective-permute-done.3.refs_7_), channel_id=1, source_target_pairs={{8,0},{16,8},{24,16},{28,24},{20,28},{12,20},{4,12},{0,4},{9,1},{1... | collective-permute-start | bytes 368648 | tf_op jit(solution)/shard_map/ppermute | solution.py:548
  19.8 8.1 %collective-permute-start.8 = (bf16[96,1152]{1,0:T(8,128)(2,1)S(1)}, bf16[96,1152]{1,0:T(8,128)(2,1)S(1)}, u32[]{:S(2)}, u32[]{:S(2)}) collective-permute-start(bf16[96,1152]{1,0:T(8,128)(2,1)S(1)} %join.1.refs_0_), channel_id=1, source_target_pairs={{0,8},{8,16},{16,24},{24,28},{28,20},{20,12},{12,4},{4,0},{1,9},{9... | collective-permute-start | bytes 663560 | tf_op jit(solution)/shard_map/ppermute | solution.py:544
  21.6 6.3 %collective-permute-start.9 = (bf16[96,1152]{1,0:T(8,128)(2,1)S(1)}, bf16[96,1152]{1,0:T(8,128)(2,1)S(1)}, u32[]{:S(2)}, u32[]{:S(2)}) collective-permute-start(bf16[96,1152]{1,0:T(8,128)(2,1)S(1)} %join.1.refs_0_), channel_id=1, source_target_pairs={{8,0},{16,8},{24,16},{28,24},{20,28},{12,20},{4,12},{0,4},{9,1},{1... | collective-permute-start | bytes 663560 | tf_op jit(solution)/shard_map/ppermute | solution.py:548
  25.4 4.9 %collective-permute-start.7 = (bf16[96,640]{1,0:T(8,128)(2,1)S(1)}, bf16[96,640]{1,0:T(8,128)(2,1)S(1)}, u32[]{:S(2)}, u32[]{:S(2)}) collective-permute-start(bf16[96,640]{1,0:T(8,128)(2,1)S(1)} %collective-permute-done.5.refs_4_), channel_id=1, source_target_pairs={{0,8},{8,16},{16,24},{24,28},{28,20},{20,12},{12,4},{4,0},{1,9},{9... | collective-permute-start | bytes 368648 | tf_op jit(solution)/shard_map/ppermute | solution.py:544
  27.0 14.5 %collective-permute-start.11 = (bf16[192,1024]{1,0:T(8,128)(2,1)S(1)}, bf16[192,1024]{1,0:T(8,128)(2,1)S(1)}, u32[]{:S(2)}, u32[]{:S(2)}) collective-permute-start(bf16[192,1024]{1,0:T(8,128)(2,1)S(1)} %bitcast.11), channel_id=1, source_target_pairs={{0,1},{1,0},{2,3},{3,2},{4,5},{5,4},{6,7},{7,6},{8,9},{9,8},{10,11... | collective-permute-start | bytes 1179656 | tf_op jit(solution)/shard_map/ppermute | solution.py:532
  30.3 14.0 %collective-permute-start.12 = (bf16[192,1024]{1,0:T(8,128)(2,1)S(1)}, bf16[192,1024]{1,0:T(8,128)(2,1)S(1)}, u32[]{:S(2)}, u32[]{:S(2)}) collective-permute-start(bf16[192,1024]{1,0:T(8,128)(2,1)S(1)} %collective-permute-done.10.refs_4_), channel_id=1, source_target_pairs={{0,1},{1,0},{2,3},{3,2},{4,5},{5,4},{6,7},{7,6},{8,9},{9,8},{10,11... | collective-permute-start | bytes 1179656 | tf_op jit(solution)/shard_map/ppermute | solution.py:532
  30.3 8.2 %collective-permute-start.18 = (bf16[96,1152]{1,0:T(8,128)(2,1)S(1)}, bf16[96,1152]{1,0:T(8,128)(2,1)S(1)}, u32[]{:S(2)}, u32[]{:S(2)}) collective-permute-start(bf16[96,1152]{1,0:T(8,128)(2,1)S(1)} %collective-permute-done.8.refs_1_), channel_id=1, source_target_pairs={{0,8},{8,16},{16,24},{24,28},{28,20},{20,12},{12,4},{4,0},{1,9},{9... | collective-permute-start | bytes 663560 | tf_op jit(solution)/shard_map/ppermute | solution.py:544
  31.9 7.6 %collective-permute-start.19 = (bf16[96,1152]{1,0:T(8,128)(2,1)S(1)}, bf16[96,1152]{1,0:T(8,128)(2,1)S(1)}, u32[]{:S(2)}, u32[]{:S(2)}) collective-permute-start(bf16[96,1152]{1,0:T(8,128)(2,1)S(1)} %collective-permute-done.9.refs_5_), channel_id=1, source_target_pairs={{8,0},{16,8},{24,16},{28,24},{20,28},{12,20},{4,12},{0,4},{9,1},{1... | collective-permute-start | bytes 663560 | tf_op jit(solution)/shard_map/ppermute | solution.py:548
  32.3 20.0 %collective-permute-start.23 = (bf16[96,768]{1,0:T(8,128)(2,1)S(1)}, bf16[96,768]{1,0:T(8,128)(2,1)S(1)}, u32[]{:S(2)}, u32[]{:S(2)}) collective-permute-start(bf16[96,768]{1,0:T(8,128)(2,1)S(1)} %get-tuple-element.244.refs_0_), channel_id=1, source_target_pairs={{0,8},{8,16},{16,24},{24,28},{28,20},{20,12},{12,4},{4,0},{1,9},{9... | collective-permute-start | bytes 442376 | tf_op jit(solution)/shard_map/ppermute | solution.py:544
  39.4 15.2 %collective-permute-start.20 = (bf16[96,1152]{1,0:T(8,128)(2,1)S(1)}, bf16[96,1152]{1,0:T(8,128)(2,1)S(1)}, u32[]{:S(2)}, u32[]{:S(2)}) collective-permute-start(bf16[96,1152]{1,0:T(8,128)(2,1)S(1)} %collective-permute-done.18.refs_2_), channel_id=1, source_target_pairs={{0,8},{8,16},{16,24},{24,28},{28,20},{20,12},{12,4},{4,0},{1,9},{9... | collective-permute-start | bytes 663560 | tf_op jit(solution)/shard_map/ppermute | solution.py:544
  41.0 12.0 %collective-permute-start.24 = (bf16[96,768]{1,0:T(8,128)(2,1)S(1)}, bf16[96,768]{1,0:T(8,128)(2,1)S(1)}, u32[]{:S(2)}, u32[]{:S(2)}) collective-permute-start(bf16[96,768]{1,0:T(8,128)(2,1)S(1)} %get-tuple-element.244.refs_0_), channel_id=1, source_target_pairs={{8,0},{16,8},{24,16},{28,24},{20,28},{12,20},{4,12},{0,4},{9,1},{1... | collective-permute-start | bytes 442376 | tf_op jit(solution)/shard_map/ppermute | solution.py:548
  41.5 13.6 %collective-permute-start.21 = (bf16[96,1152]{1,0:T(8,128)(2,1)S(1)}, bf16[96,1152]{1,0:T(8,128)(2,1)S(1)}, u32[]{:S(2)}, u32[]{:S(2)}) collective-permute-start(bf16[96,1152]{1,0:T(8,128)(2,1)S(1)} %collective-permute-done.19.refs_6_), channel_id=1, source_target_pairs={{8,0},{16,8},{24,16},{28,24},{20,28},{12,20},{4,12},{0,4},{9,1},{1... | collective-permute-start | bytes 663560 | tf_op jit(solution)/shard_map/ppermute | solution.py:548
  46.9 9.7 %collective-permute-start.14 = (bf16[512,192]{1,0:T(8,128)(2,1)S(1)}, bf16[512,192]{1,0:T(8,128)(2,1)S(1)}, u32[]{:S(2)}, u32[]{:S(2)}) collective-permute-start(bf16[512,192]{1,0:T(8,128)(2,1)S(1)} %get-tuple-element.213.c0.refs_4_), channel_id=1, source_target_pairs={{0,2},{1,3},{2,0},{3,1},{4,6},{5,7},{6,4},{7,5},{8,10},{9,11},{10,... | collective-permute-start | bytes 589832 | tf_op jit(solution)/shard_map/ppermute | solution.py:536
  52.4 7.0 %collective-permute-start.16 = (bf16[512,192]{1,0:T(8,128)(2,1)S(1)}, bf16[512,192]{1,0:T(8,128)(2,1)S(1)}, u32[]{:S(2)}, u32[]{:S(2)}) collective-permute-start(bf16[512,192]{1,0:T(8,128)(2,1)S(1)} %get-tuple-element.215.c0.refs_5_), channel_id=1, source_target_pairs={{0,2},{1,3},{2,0},{3,1},{4,6},{5,7},{6,4},{7,5},{8,10},{9,11},{10,... | collective-permute-start | bytes 589832 | tf_op jit(solution)/shard_map/ppermute | solution.py:536
  53.0 6.4 %collective-permute-start.25 = (bf16[96,768]{1,0:T(8,128)(2,1)S(1)}, bf16[96,768]{1,0:T(8,128)(2,1)S(1)}, u32[]{:S(2)}, u32[]{:S(2)}) collective-permute-start(bf16[96,768]{1,0:T(8,128)(2,1)S(1)} %collective-permute-done.23.refs_1_), channel_id=1, source_target_pairs={{0,8},{8,16},{16,24},{24,28},{28,20},{20,12},{12,4},{4,0},{1,9},{9... | collective-permute-start | bytes 442376 | tf_op jit(solution)/shard_map/ppermute | solution.py:544
  54.6 5.1 %collective-permute-start.26 = (bf16[96,768]{1,0:T(8,128)(2,1)S(1)}, bf16[96,768]{1,0:T(8,128)(2,1)S(1)}, u32[]{:S(2)}, u32[]{:S(2)}) collective-permute-start(bf16[96,768]{1,0:T(8,128)(2,1)S(1)} %collective-permute-done.24.refs_5_), channel_id=1, source_target_pairs={{8,0},{16,8},{24,16},{28,24},{20,28},{12,20},{4,12},{0,4},{9,1},{1... | collective-permute-start | bytes 442376 | tf_op jit(solution)/shard_map/ppermute | solution.py:548
  55.0 11.9 %collective-permute-start.22 = (bf16[96,1152]{1,0:T(8,128)(2,1)S(1)}, bf16[96,1152]{1,0:T(8,128)(2,1)S(1)}, u32[]{:S(2)}, u32[]{:S(2)}) collective-permute-start(bf16[96,1152]{1,0:T(8,128)(2,1)S(1)} %collective-permute-done.20.refs_3_), channel_id=1, source_target_pairs={{0,8},{8,16},{16,24},{24,28},{28,20},{20,12},{12,4},{4,0},{1,9},{9... | collective-permute-start | bytes 663560 | tf_op jit(solution)/shard_map/ppermute | solution.py:544
  56.6 10.3 %collective-permute-start.15 = (bf16[512,192]{1,0:T(8,128)(2,1)S(1)}, bf16[512,192]{1,0:T(8,128)(2,1)S(1)}, u32[]{:S(2)}, u32[]{:S(2)}) collective-permute-start(bf16[512,192]{1,0:T(8,128)(2,1)S(1)} %collective-permute-done.14.c2), channel_id=1, source_target_pairs={{0,1},{1,0},{2,3},{3,2},{4,5},{5,4},{6,7},{7,6},{8,9},{9,8},{10,11... | collective-permute-start | bytes 589832 | tf_op jit(solution)/shard_map/ppermute | solution.py:532
  59.4 7.6 %collective-permute-start.17 = (bf16[512,192]{1,0:T(8,128)(2,1)S(1)}, bf16[512,192]{1,0:T(8,128)(2,1)S(1)}, u32[]{:S(2)}, u32[]{:S(2)}) collective-permute-start(bf16[512,192]{1,0:T(8,128)(2,1)S(1)} %collective-permute-done.16.c2), channel_id=1, source_target_pairs={{0,1},{1,0},{2,3},{3,2},{4,5},{5,4},{6,7},{7,6},{8,9},{9,8},{10,11... | collective-permute-start | bytes 589832 | tf_op jit(solution)/shard_map/ppermute | solution.py:532
  59.7 5.9 %collective-permute-start.27 = (bf16[96,768]{1,0:T(8,128)(2,1)S(1)}, bf16[96,768]{1,0:T(8,128)(2,1)S(1)}, u32[]{:S(2)}, u32[]{:S(2)}) collective-permute-start(bf16[96,768]{1,0:T(8,128)(2,1)S(1)} %collective-permute-done.25.refs_2_), channel_id=1, source_target_pairs={{0,8},{8,16},{16,24},{24,28},{28,20},{20,12},{12,4},{4,0},{1,9},{9... | collective-permute-start | bytes 442376 | tf_op jit(solution)/shard_map/ppermute | solution.py:544
  61.3 5.6 %collective-permute-start.28 = (bf16[96,768]{1,0:T(8,128)(2,1)S(1)}, bf16[96,768]{1,0:T(8,128)(2,1)S(1)}, u32[]{:S(2)}, u32[]{:S(2)}) collective-permute-start(bf16[96,768]{1,0:T(8,128)(2,1)S(1)} %collective-permute-done.26.refs_6_), channel_id=1, source_target_pairs={{8,0},{16,8},{24,16},{28,24},{20,28},{12,20},{4,12},{0,4},{9,1},{1... | collective-permute-start | bytes 442376 | tf_op jit(solution)/shard_map/ppermute | solution.py:548
  67.4 2.7 %collective-permute-start.30 = (bf16[192,768]{1,0:T(8,128)(2,1)S(1)}, bf16[192,768]{1,0:T(8,128)(2,1)S(1)}, u32[]{:S(2)}, u32[]{:S(2)}) collective-permute-start(bf16[192,768]{1,0:T(8,128)(2,1)S(1)} %get-tuple-element.233.w2), channel_id=1, source_target_pairs={{0,1},{1,0},{2,3},{3,2},{4,5},{5,4},{6,7},{7,6},{8,9},{9,8},{10,11... | collective-permute-start | bytes 884744 | tf_op jit(solution)/shard_map/ppermute | solution.py:532
  68.0 5.4 %collective-permute-start.31 = (bf16[512,192]{1,0:T(8,128)(2,1)S(1)}, bf16[512,192]{1,0:T(8,128)(2,1)S(1)}, u32[]{:S(2)}, u32[]{:S(2)}) collective-permute-start(bf16[512,192]{1,0:T(8,128)(2,1)S(1)} %get-tuple-element.215.c0.refs_5_), channel_id=1, source_target_pairs={{0,1},{1,0},{2,3},{3,2},{4,5},{5,4},{6,7},{7,6},{8,9},{9,8},{10,11... | collective-permute-start | bytes 589832 | tf_op jit(solution)/shard_map/ppermute | solution.py:532
  68.5 8.4 %collective-permute-start.32 = (bf16[96,768]{1,0:T(8,128)(2,1)S(1)}, bf16[96,768]{1,0:T(8,128)(2,1)S(1)}, u32[]{:S(2)}, u32[]{:S(2)}) collective-permute-start(bf16[96,768]{1,0:T(8,128)(2,1)S(1)} %collective-permute-done.27.refs_3_), channel_id=1, source_target_pairs={{0,8},{8,16},{16,24},{24,28},{28,20},{20,12},{12,4},{4,0},{1,9},{9... | collective-permute-start | bytes 442376 | tf_op jit(solution)/shard_map/ppermute | solution.py:544
  80.2 3.1 %collective-permute-start.33 = (bf16[128,768]{1,0:T(8,128)(2,1)S(1)}, bf16[128,768]{1,0:T(8,128)(2,1)S(1)}, u32[]{:S(2)}, u32[]{:S(2)}) collective-permute-start(bf16[128,768]{1,0:T(8,128)(2,1)S(1)} %get-tuple-element.255), channel_id=1, source_target_pairs={{0,1},{1,0},{2,3},{3,2},{4,5},{5,4},{6,7},{7,6},{8,9},{9,8},{10,11... | collective-permute-start | bytes 589832 | tf_op jit(solution)/shard_map/ppermute | solution.py:532
  80.3 3.0 %collective-permute-start.34 = (bf16[128,768]{1,0:T(8,128)(2,1)S(1)}, bf16[128,768]{1,0:T(8,128)(2,1)S(1)}, u32[]{:S(2)}, u32[]{:S(2)}) collective-permute-start(bf16[128,768]{1,0:T(8,128)(2,1)S(1)} %get-tuple-element.256), channel_id=1, source_target_pairs={{0,1},{1,0},{2,3},{3,2},{4,5},{5,4},{6,7},{7,6},{8,9},{9,8},{10,11... | collective-permute-start | bytes 589832 | tf_op jit(solution)/shard_map/ppermute | solution.py:532
  82.7 5.4 %collective-permute-start.35 = (bf16[128,768]{1,0:T(8,128)(2,1)S(1)}, bf16[128,768]{1,0:T(8,128)(2,1)S(1)}, u32[]{:S(2)}, u32[]{:S(2)}) collective-permute-start(bf16[128,768]{1,0:T(8,128)(2,1)S(1)} %get-tuple-element.261), channel_id=1, source_target_pairs={{0,1},{1,0},{2,3},{3,2},{4,5},{5,4},{6,7},{7,6},{8,9},{9,8},{10,11... | collective-permute-start | bytes 589832 | tf_op jit(solution)/shard_map/ppermute | solution.py:532
  82.8 5.3 %collective-permute-start.36 = (bf16[128,768]{1,0:T(8,128)(2,1)S(1)}, bf16[128,768]{1,0:T(8,128)(2,1)S(1)}, u32[]{:S(2)}, u32[]{:S(2)}) collective-permute-start(bf16[128,768]{1,0:T(8,128)(2,1)S(1)} %get-tuple-element.262), channel_id=1, source_target_pairs={{0,1},{1,0},{2,3},{3,2},{4,5},{5,4},{6,7},{7,6},{8,9},{9,8},{10,11... | collective-permute-start | bytes 589832 | tf_op jit(solution)/shard_map/ppermute | solution.py:532
  83.4 11.2 %collective-permute-start.37 = (bf16[256,768]{1,0:T(8,128)(2,1)S(1)}, bf16[256,768]{1,0:T(8,128)(2,1)S(1)}, u32[]{:S(2)}, u32[]{:S(2)}) collective-permute-start(bf16[256,768]{1,0:T(8,128)(2,1)S(1)} %add0.1.refs_1_), channel_id=1, source_target_pairs={{0,2},{1,3},{2,0},{3,1},{4,6},{5,7},{6,4},{7,5},{8,10},{9,11},{10,... | collective-permute-start | bytes 1179656 | tf_op jit(solution)/shard_map/ppermute | solution.py:536
  89.8 8.8 %collective-permute-start.39 = (bf16[256,768]{1,0:T(8,128)(2,1)S(1)}, bf16[256,768]{1,0:T(8,128)(2,1)S(1)}, u32[]{:S(2)}, u32[]{:S(2)}) collective-permute-start(bf16[256,768]{1,0:T(8,128)(2,1)S(1)} %get-tuple-element.274), channel_id=1, source_target_pairs={{0,1},{1,0},{2,3},{3,2},{4,5},{5,4},{6,7},{7,6},{8,9},{9,8},{10,11... | collective-permute-start | bytes 1179656 | tf_op jit(solution)/shard_map/ppermute | solution.py:532
  89.9 8.8 %collective-permute-start.38 = (bf16[256,768]{1,0:T(8,128)(2,1)S(1)}, bf16[256,768]{1,0:T(8,128)(2,1)S(1)}, u32[]{:S(2)}, u32[]{:S(2)}) collective-permute-start(bf16[256,768]{1,0:T(8,128)(2,1)S(1)} %get-tuple-element.265), channel_id=1, source_target_pairs={{0,1},{1,0},{2,3},{3,2},{4,5},{5,4},{6,7},{7,6},{8,9},{9,8},{10,11... | collective-permute-start | bytes 1179656 | tf_op jit(solution)/shard_map/ppermute | solution.py:532
  94.5 14.4 %collective-permute-start.46 = (bf16[256,768]{1,0:T(8,128)(2,1)S(1)}, bf16[256,768]{1,0:T(8,128)(2,1)S(1)}, u32[]{:S(2)}, u32[]{:S(2)}) collective-permute-start(bf16[256,768]{1,0:T(8,128)(2,1)S(1)} %add1.1.refs_1_), channel_id=1, source_target_pairs={{0,2},{1,3},{2,0},{3,1},{4,6},{5,7},{6,4},{7,5},{8,10},{9,11},{10,... | collective-permute-start | bytes 1179656 | tf_op jit(solution)/shard_map/ppermute | solution.py:536
  96.0 7.9 %collective-permute-start.40 = (bf16[96,1536]{1,0:T(8,128)(2,1)S(1)}, bf16[96,1536]{1,0:T(8,128)(2,1)S(1)}, u32[]{:S(2)}, u32[]{:S(2)}) collective-permute-start(bf16[96,1536]{1,0:T(8,128)(2,1)S(1)} %get-tuple-element.276), channel_id=1, source_target_pairs={{0,8},{8,16},{16,24},{24,28},{28,20},{20,12},{12,4},{4,0},{1,9},{9... | collective-permute-start | bytes 884744 | tf_op jit(solution)/shard_map/ppermute | solution.py:544
  97.5 7.6 %collective-permute-start.41 = (bf16[96,1536]{1,0:T(8,128)(2,1)S(1)}, bf16[96,1536]{1,0:T(8,128)(2,1)S(1)}, u32[]{:S(2)}, u32[]{:S(2)}) collective-permute-start(bf16[96,1536]{1,0:T(8,128)(2,1)S(1)} %get-tuple-element.277), channel_id=1, source_target_pairs={{8,0},{16,8},{24,16},{28,24},{20,28},{12,20},{4,12},{0,4},{9,1},{1... | collective-permute-start | bytes 884744 | tf_op jit(solution)/shard_map/ppermute | solution.py:548
  98.6 6.5 %collective-permute-start.42 = (bf16[128,768]{1,0:T(8,128)(2,1)S(1)}, bf16[128,768]{1,0:T(8,128)(2,1)S(1)}, u32[]{:S(2)}, u32[]{:S(2)}) collective-permute-start(bf16[128,768]{1,0:T(8,128)(2,1)S(1)} %get-tuple-element.279.refs_3_), channel_id=1, source_target_pairs={{0,1},{1,0},{2,3},{3,2},{4,5},{5,4},{6,7},{7,6},{8,9},{9,8},{10,11... | collective-permute-start | bytes 589832 | tf_op jit(solution)/shard_map/ppermute | solution.py:532
  98.7 6.4 %collective-permute-start.43 = (bf16[128,768]{1,0:T(8,128)(2,1)S(1)}, bf16[128,768]{1,0:T(8,128)(2,1)S(1)}, u32[]{:S(2)}, u32[]{:S(2)}) collective-permute-start(bf16[128,768]{1,0:T(8,128)(2,1)S(1)} %get-tuple-element.280.refs_4_), channel_id=1, source_target_pairs={{0,1},{1,0},{2,3},{3,2},{4,5},{5,4},{6,7},{7,6},{8,9},{9,8},{10,11... | collective-permute-start | bytes 589832 | tf_op jit(solution)/shard_map/ppermute | solution.py:532
  109.5 10.9 %collective-permute-start.49 = (bf16[256,768]{1,0:T(8,128)(2,1)S(1)}, bf16[256,768]{1,0:T(8,128)(2,1)S(1)}, u32[]{:S(2)}, u32[]{:S(2)}) collective-permute-start(bf16[256,768]{1,0:T(8,128)(2,1)S(1)} %get-tuple-element.298), channel_id=1, source_target_pairs={{0,2},{1,3},{2,0},{3,1},{4,6},{5,7},{6,4},{7,5},{8,10},{9,11},{10,... | collective-permute-start | bytes 1179656 | tf_op jit(solution)/shard_map/ppermute | solution.py:536
  110.3 10.1 %collective-permute-start.44 = (bf16[96,1536]{1,0:T(8,128)(2,1)S(1)}, bf16[96,1536]{1,0:T(8,128)(2,1)S(1)}, u32[]{:S(2)}, u32[]{:S(2)}) collective-permute-start(bf16[96,1536]{1,0:T(8,128)(2,1)S(1)} %get-tuple-element.283), channel_id=1, source_target_pairs={{0,8},{8,16},{16,24},{24,28},{28,20},{20,12},{12,4},{4,0},{1,9},{9... | collective-permute-start | bytes 884744 | tf_op jit(solution)/shard_map/ppermute | solution.py:544
  111.8 8.5 %collective-permute-start.45 = (bf16[96,1536]{1,0:T(8,128)(2,1)S(1)}, bf16[96,1536]{1,0:T(8,128)(2,1)S(1)}, u32[]{:S(2)}, u32[]{:S(2)}) collective-permute-start(bf16[96,1536]{1,0:T(8,128)(2,1)S(1)} %get-tuple-element.284), channel_id=1, source_target_pairs={{8,0},{16,8},{24,16},{28,24},{20,28},{12,20},{4,12},{0,4},{9,1},{1... | collective-permute-start | bytes 884744 | tf_op jit(solution)/shard_map/ppermute | solution.py:548
  125.2 16.0 %collective-permute-start.50 = (bf16[528,768]{1,0:T(8,128)(2,1)S(1)}, bf16[528,768]{1,0:T(8,128)(2,1)S(1)}, u32[]{:S(2)}, u32[]{:S(2)}) collective-permute-start(bf16[528,768]{1,0:T(8,128)(2,1)S(1)} %get-tuple-element.313), channel_id=1, source_target_pairs={{0,1},{1,0},{2,3},{3,2},{4,5},{5,4},{6,7},{7,6},{8,9},{9,8},{10,11... | collective-permute-start | bytes 2433032 | tf_op jit(solution)/shard_map/ppermute | solution.py:532
  125.5 6.7 %collective-permute-start.53 = (bf16[96,768]{1,0:T(8,128)(2,1)S(1)}, bf16[96,768]{1,0:T(8,128)(2,1)S(1)}, u32[]{:S(2)}, u32[]{:S(2)}) collective-permute-start(bf16[96,768]{1,0:T(8,128)(2,1)S(1)} %get-tuple-element.307), channel_id=1, source_target_pairs={{0,8},{8,16},{16,24},{24,28},{28,20},{20,12},{12,4},{4,0},{1,9},{9... | collective-permute-start | bytes 442376 | tf_op jit(solution)/shard_map/ppermute | solution.py:544
  127.0 12.1 %collective-permute-start.52 = (bf16[96,1536]{1,0:T(8,128)(2,1)S(1)}, bf16[96,1536]{1,0:T(8,128)(2,1)S(1)}, u32[]{:S(2)}, u32[]{:S(2)}) collective-permute-start(bf16[96,1536]{1,0:T(8,128)(2,1)S(1)} %get-tuple-element.316), channel_id=1, source_target_pairs={{8,0},{16,8},{24,16},{28,24},{20,28},{12,20},{4,12},{0,4},{9,1},{1... | collective-permute-start | bytes 884744 | tf_op jit(solution)/shard_map/ppermute | solution.py:548
  127.6 11.5 %collective-permute-start.51 = (bf16[96,1536]{1,0:T(8,128)(2,1)S(1)}, bf16[96,1536]{1,0:T(8,128)(2,1)S(1)}, u32[]{:S(2)}, u32[]{:S(2)}) collective-permute-start(bf16[96,1536]{1,0:T(8,128)(2,1)S(1)} %get-tuple-element.303), channel_id=1, source_target_pairs={{0,8},{8,16},{16,24},{24,28},{28,20},{20,12},{12,4},{4,0},{1,9},{9... | collective-permute-start | bytes 884744 | tf_op jit(solution)/shard_map/ppermute | solution.py:544
  129.0 16.6 %collective-permute-start.61 = (bf16[192,1024]{1,0:T(8,128)(2,1)S(1)}, bf16[192,1024]{1,0:T(8,128)(2,1)S(1)}, u32[]{:S(2)}, u32[]{:S(2)}) collective-permute-start(bf16[192,1024]{1,0:T(8,128)(2,1)S(1)} %get-tuple-element.331.refs_1_), channel_id=1, source_target_pairs={{0,2},{1,3},{2,0},{3,1},{4,6},{5,7},{6,4},{7,5},{8,10},{9,11},{10,... | collective-permute-start | bytes 1179656 | tf_op jit(solution)/shard_map/ppermute | solution.py:536
  132.2 6.9 %collective-permute-start.54 = (bf16[96,768]{1,0:T(8,128)(2,1)S(1)}, bf16[96,768]{1,0:T(8,128)(2,1)S(1)}, u32[]{:S(2)}, u32[]{:S(2)}) collective-permute-start(bf16[96,768]{1,0:T(8,128)(2,1)S(1)} %get-tuple-element.317), channel_id=1, source_target_pairs={{8,0},{16,8},{24,16},{28,24},{20,28},{12,20},{4,12},{0,4},{9,1},{1... | collective-permute-start | bytes 442376 | tf_op jit(solution)/shard_map/ppermute | solution.py:548
  139.2 5.2 %collective-permute-start.55 = (bf16[96,768]{1,0:T(8,128)(2,1)S(1)}, bf16[96,768]{1,0:T(8,128)(2,1)S(1)}, u32[]{:S(2)}, u32[]{:S(2)}) collective-permute-start(bf16[96,768]{1,0:T(8,128)(2,1)S(1)} %get-tuple-element.320), channel_id=1, source_target_pairs={{0,8},{8,16},{16,24},{24,28},{28,20},{20,12},{12,4},{4,0},{1,9},{9... | collective-permute-start | bytes 442376 | tf_op jit(solution)/shard_map/ppermute | solution.py:544
  139.8 5.1 %collective-permute-start.56 = (bf16[96,768]{1,0:T(8,128)(2,1)S(1)}, bf16[96,768]{1,0:T(8,128)(2,1)S(1)}, u32[]{:S(2)}, u32[]{:S(2)}) collective-permute-start(bf16[96,768]{1,0:T(8,128)(2,1)S(1)} %get-tuple-element.321), channel_id=1, source_target_pairs={{8,0},{16,8},{24,16},{28,24},{20,28},{12,20},{4,12},{0,4},{9,1},{1... | collective-permute-start | bytes 442376 | tf_op jit(solution)/shard_map/ppermute | solution.py:548
  141.4 15.4 %collective-permute-start.59 = (bf16[272,768]{1,0:T(8,128)(2,1)S(1)}, bf16[272,768]{1,0:T(8,128)(2,1)S(1)}, u32[]{:S(2)}, u32[]{:S(2)}) collective-permute-start(bf16[272,768]{1,0:T(8,128)(2,1)S(1)} %get-tuple-element.326), channel_id=1, source_target_pairs={{0,2},{1,3},{2,0},{3,1},{4,6},{5,7},{6,4},{7,5},{8,10},{9,11},{10,... | collective-permute-start | bytes 1253384 | tf_op jit(solution)/shard_map/ppermute | solution.py:536
  145.1 6.6 %collective-permute-start.57 = (bf16[96,768]{1,0:T(8,128)(2,1)S(1)}, bf16[96,768]{1,0:T(8,128)(2,1)S(1)}, u32[]{:S(2)}, u32[]{:S(2)}) collective-permute-start(bf16[96,768]{1,0:T(8,128)(2,1)S(1)} %get-tuple-element.324), channel_id=1, source_target_pairs={{0,8},{8,16},{16,24},{24,28},{28,20},{20,12},{12,4},{4,0},{1,9},{9... | collective-permute-start | bytes 442376 | tf_op jit(solution)/shard_map/ppermute | solution.py:544
  145.6 21.4 %collective-permute-start.60 = (bf16[192,1024]{1,0:T(8,128)(2,1)S(1)}, bf16[192,1024]{1,0:T(8,128)(2,1)S(1)}, u32[]{:S(2)}, u32[]{:S(2)}) collective-permute-start(bf16[192,1024]{1,0:T(8,128)(2,1)S(1)} %get-tuple-element.331.refs_1_), channel_id=1, source_target_pairs={{0,1},{1,0},{2,3},{3,2},{4,5},{5,4},{6,7},{7,6},{8,9},{9,8},{10,11... | collective-permute-start | bytes 1179656 | tf_op jit(solution)/shard_map/ppermute | solution.py:532
  145.6 21.4 %collective-permute-start.62 = (bf16[192,1024]{1,0:T(8,128)(2,1)S(1)}, bf16[192,1024]{1,0:T(8,128)(2,1)S(1)}, u32[]{:S(2)}, u32[]{:S(2)}) collective-permute-start(bf16[192,1024]{1,0:T(8,128)(2,1)S(1)} %collective-permute-done.61.refs_3_), channel_id=1, source_target_pairs={{0,1},{1,0},{2,3},{3,2},{4,5},{5,4},{6,7},{7,6},{8,9},{9,8},{10,11... | collective-permute-start | bytes 1179656 | tf_op jit(solution)/shard_map/ppermute | solution.py:532
  146.2 22.4 %collective-permute-start.64 = (bf16[96,1536]{1,0:T(8,128)(2,1)S(1)}, bf16[96,1536]{1,0:T(8,128)(2,1)S(1)}, u32[]{:S(2)}, u32[]{:S(2)}) collective-permute-start(bf16[96,1536]{1,0:T(8,128)(2,1)S(1)} %mlp_hop1.1), channel_id=1, source_target_pairs={{0,8},{8,16},{16,24},{24,28},{28,20},{20,12},{12,4},{4,0},{1,9},{9... | collective-permute-start | bytes 884744 | tf_op jit(solution)/shard_map/ppermute | solution.py:544
  151.7 5.1 %collective-permute-start.58 = (bf16[96,768]{1,0:T(8,128)(2,1)S(1)}, bf16[96,768]{1,0:T(8,128)(2,1)S(1)}, u32[]{:S(2)}, u32[]{:S(2)}) collective-permute-start(bf16[96,768]{1,0:T(8,128)(2,1)S(1)} %get-tuple-element.325), channel_id=1, source_target_pairs={{8,0},{16,8},{24,16},{28,24},{20,28},{12,20},{4,12},{0,4},{9,1},{1... | collective-permute-start | bytes 442376 | tf_op jit(solution)/shard_map/ppermute | solution.py:548
  156.9 15.2 %collective-permute-start.63 = (bf16[96,768]{1,0:T(8,128)(2,1)S(1)}, bf16[96,768]{1,0:T(8,128)(2,1)S(1)}, u32[]{:S(2)}, u32[]{:S(2)}) collective-permute-start(bf16[96,768]{1,0:T(8,128)(2,1)S(1)} %qkv_hop1.1), channel_id=1, source_target_pairs={{0,8},{8,16},{16,24},{24,28},{28,20},{20,12},{12,4},{4,0},{1,9},{9... | collective-permute-start | bytes 442376 | tf_op jit(solution)/shard_map/ppermute | solution.py:544
  159.0 3.9 %collective-permute-start.65 = (f32[8,768]{1,0:T(8,128)S(1)}, f32[8,768]{1,0:T(8,128)S(1)}, u32[]{:S(2)}, u32[]{:S(2)}) collective-permute-start(f32[8,768]{1,0:T(8,128)S(1)} %get-tuple-element.349.a), channel_id=1, source_target_pairs={{0,4},{4,0},{8,12},{12,8},{16,20},{20,16},{24,28},{28,24},{1,5},{5... | collective-permute-start | bytes 73736 | tf_op jit(solution)/shard_map/ppermute | solution.py:938
  162.9 3.8 %collective-permute-start.66 = (f32[8,768]{1,0:T(8,128)S(1)}, f32[8,768]{1,0:T(8,128)S(1)}, u32[]{:S(2)}, u32[]{:S(2)}) collective-permute-start(f32[8,768]{1,0:T(8,128)S(1)} %sum1.1.a), channel_id=1, source_target_pairs={{0,8},{4,12},{8,0},{12,4},{16,24},{20,28},{24,16},{28,20},{1,9},{5... | collective-permute-start | bytes 73736 | tf_op jit(solution)/shard_map/ppermute | solution.py:938
  166.7 4.7 %collective-permute-start.67 = (f32[8,768]{1,0:T(8,128)S(1)}, f32[8,768]{1,0:T(8,128)S(1)}, u32[]{:S(2)}, u32[]{:S(2)}) collective-permute-start(f32[8,768]{1,0:T(8,128)S(1)} %sum2.1.refs_0_), channel_id=1, source_target_pairs={{0,16},{4,20},{8,24},{12,28},{16,0},{20,4},{24,8},{28,12},{1,17},{... | collective-permute-start | bytes 73736 | tf_op jit(solution)/shard_map/ppermute | solution.py:938
  (29 other events, 136.0 us)

commit v3 on v2

--- a/solution.py
+++ b/solution.py
@@ -121,6 +121,12 @@
     for i in range(x_ref.shape[0] // RB):
         at = slice(i * RB, (i + 1) * RB)
         unit_ref[at] = norm_stats(x_ref[at].astype(f32))[0]
+
+
+def fetch_kernel(src, out, sem):
+    copy = pltpu.make_async_copy(src, out, sem)
+    copy.start()
+    copy.wait()
 
 
 def loop(count, body):
@@ -331,35 +337,52 @@
     bottom[...] = dr[RB // 2 :].astype(bf16)
 
 
-def attend_back_kernel(heads, base, last, info, src, m_ref, v_ref, o0, o1, p0, p1, wp, lse_ref, *refs):
-    if last:
-        dqa, dka, dva, ab_ref, dm_ref, dvr_ref = refs
+def attend_back_kernel(heads, base, blocks, stage, info, src, m_ref, v_ref, *refs):
+    if stage < 2:
+        halves, refs = refs[:4], refs[4:]
     else:
+        ab_in, refs = refs[0], refs[1:]
+    wp, lse_ref, *refs = refs
+    if stage:
+        dk_in, dv_in, *refs = refs
+    if stage == 0:
         ab_ref, dq_ref, dk_ref, dv_ref = refs
+    elif stage == 1:
+        ab_ref, dq_ref, dk_ref, dv_ref = refs
+    else:
+        dq_first, dq_second, dm_ref, dvr_ref = refs
     keep = masked_tile()
     core = info[0]
-    rows = 2 * RB
-    blocks = 2
-    for k, (own, partner) in enumerate(((o0, p0), (o1, p1))):
-        ab_ref[block(2 * core + k, RB // 2), :] = own[...]
-        ab_ref[block(2 * (1 - core) + k, RB // 2), :] = partner[...]
-    top = base + rows
+    if stage < 2:
+        for k in range(2):
+            ab_ref[block(2 * core + k, RB // 2), :] = halves[k][...]
+            ab_ref[block(2 * (1 - core) + k, RB // 2), :] = halves[2 + k][...]
+        source, skip = ab_ref, 0
+    else:
+        source, skip = ab_in, ab_in.shape[0] - blocks * RB
+    top = base + blocks * RB
     tiles = top // RB
-    dctx = [dot_nt(ab_ref[i * RB : (i + 1) * RB], wp[...]).astype(bf16) for i in range(blocks)]
+    dctx = [dot_nt(source[skip + i * RB : skip + (i + 1) * RB], wp[...]).astype(bf16) for i in range(blocks)]
     dq_t = [[None] * heads for _ in range(blocks)]
     dks, dvs = [], []
     for h in range(heads):
+        lane = slice(h * HD, (h + 1) * HD)
         keys = m_ref[:top, (3 * h + 1) * HD : (3 * h + 2) * HD]
         keys_t = keys.T
         values = v_ref[h * HD : (h + 1) * HD, :top].T
         dk = [None] * tiles
         dv = [None] * tiles
+        if stage:
+            for t in range(base // RB):
+                dk[t] = dk_in[t * RB : (t + 1) * RB, lane]
+                dv[t] = dv_in[t * RB : (t + 1) * RB, lane]
         for i in range(blocks):
             lo = base + i * RB
             count = lo // RB + 1
             query = m_ref[lo : lo + RB, 3 * h * HD : (3 * h + 1) * HD] * bf16(HD**-0.5)
-            dc = dctx[i][:, h * HD : (h + 1) * HD]
-            lse = lse_ref[h : h + 1, i * RB : (i + 1) * RB]
+            dc = dctx[i][:, lane]
+            first = lse_ref.shape[1] - blocks * RB if stage == 2 else 0
+            lse = lse_ref[h : h + 1, first + i * RB : first + (i + 1) * RB]
             probs, dprobs = [], []
             inner = jnp.zeros((1, RB), f32)
             for t in range(count):
@@ -386,7 +409,7 @@
         dks.append(dk)
         dvs.append(dv)
     dq = [jnp.concatenate(dq_t[i], 0).T for i in range(blocks)]
-    if not last:
+    if stage < 2:
         for i in range(blocks):
             dq_ref[i * RB : (i + 1) * RB] = dq[i]
         for t in range(tiles):
@@ -395,50 +418,51 @@
         return
     mp = info[2]
     fresh = [jnp.where(src[mp * heads + h] < H, 0.0, 1.0) for h in range(heads)]
+    split = dq_first.shape[0]
     for t in range(tiles):
         spot = slice(t * RB, (t + 1) * RB)
-        first = t * RB < base
         parts = []
         for h in range(heads):
             lane = slice(h * HD, (h + 1) * HD)
-            dqh = dqa[spot, lane] if first else dq[t - base // RB][:, lane]
-            dkh = dks[h][t] + dka[spot, lane] if first else dks[h][t]
-            dvh = dvs[h][t] + dva[spot, lane] if first else dvs[h][t]
-            parts += [dqh, dkh, dvh * fresh[h]]
-            dvr_ref[h * HD : (h + 1) * HD, spot] = dvh.T.astype(bf16)
+            if t * RB < split:
+                dqh = dq_first[spot, lane]
+            elif t * RB < base:
+                dqh = dq_second[t * RB - split : (t + 1) * RB - split, lane]
+            else:
+                dqh = dq[t - base // RB][:, lane]
+            parts += [dqh, dks[h][t], dvs[h][t] * fresh[h]]
+            dvr_ref[h * HD : (h + 1) * HD, spot] = dvs[h][t].T.astype(bf16)
         dm_ref[spot, :] = jnp.concatenate(parts, 1).astype(bf16)
 
 
-def input_kernel(info, dm_ref, w_ref, unit_ref, na, nb, send, keep):
+def input_kernel(info, dm_ref, w_ref, unit_ref, na, nb, s0, s1, keep, sums):
     core = info[0]
     cols = dm_ref.shape[1]
-    sums = na[...] + nb[...]
-    keep[2 * RB :] = jnp.concatenate([sums, jnp.zeros(sums.shape, f32)], 0)
+    sums[...] = na[...] + nb[...]
 
     def step(i):
         half = i % 2
         spot = jnp.where(i < 2, 1 - core, core)
         at = block(2 * half + spot)
         grad = dot_nt(dm_ref[at, :], w_ref[:, :cols])
-        keep[2 * RB : 2 * RB + 1] += jnp.sum(grad * unit_ref[at, :], 0, keepdims=True)
-        keep[2 * RB + 1 : 2 * RB + 2] += jnp.sum(grad, 0, keepdims=True)
+        sums[0:1] += jnp.sum(grad * unit_ref[at, :], 0, keepdims=True)
+        sums[1:2] += jnp.sum(grad, 0, keepdims=True)
         keep[block(half), :] = grad
-
-        @pl.when(i < 2)
-        def _():
-            send[block(half), :] = grad.astype(bf16)
+        for k, out in enumerate((s0, s1)):
+
+            @pl.when(i == k)
+            def _():
+                out[...] = grad.astype(bf16)
 
     loop(4, step)
-    send[2 * RB :] = keep[2 * RB :].astype(bf16)
-
-
-def to_rows_kernel(info, keep, received, mine, sent):
-    own = info[1]
-    for out, half in ((mine, own), (sent, 1 - own)):
-        at = block(half)
-        out[:RB] = (keep[at, :] + received[at, :].astype(f32)).astype(out.dtype)
-        if out.shape[0] > RB:
-            out[RB:] = (keep[2 * RB :] + received[2 * RB :].astype(f32)).astype(out.dtype)
+
+
+def to_rows_kernel(info, keep, r0, r1, mine, sent):
+    low = info[1] == 0
+    first = keep[:RB] + r0[...].astype(f32)
+    second = keep[RB:] + r1[...].astype(f32)
+    mine[...] = jnp.where(low, first, second)
+    sent[...] = jnp.where(low, second, first).astype(bf16)
 
 
 def output_rows_kernel(info, ka, kb, ra, rb, mine, sent):
@@ -455,24 +479,27 @@
     out[...] = (resid + mine[...] + received[...].astype(f32)).astype(bf16)
 
 
-def qkv_grad_kernel(info, a1_ref, dm_ref, aba, abb, ca, cb, out, fw, bw):
+def qkv_grad_kernel(info, a1_ref, dm_ref, aba, abb, ca, cb, sums, out, fw, bw, turn):
+    cols, width = dm_ref.shape[1], sums.shape[1]
+    turn[...] = jnp.zeros(turn.shape, f32)
+    turn[: sums.shape[0]] = sums[...]
+
     def step(j):
         at = block(j)
         grad = dot_tn(a1_ref[:, at], dm_ref[...])
         proj = dot_tn(aba[:, at], ca[...]) + dot_tn(abb[:, at], cb[...])
-        out[at, :] = jnp.concatenate([grad, proj], 1).astype(out.dtype)
+        out[at, : out.shape[1] - LANES] = jnp.concatenate([grad, proj], 1).astype(out.dtype)
+        out[at, out.shape[1] - LANES :] = turn[:, at].T.astype(out.dtype)
 
     loop(out.shape[0] // RB, step)
     starts(info, out, fw, bw)
 
 
-def norm_one_kernel(info, x_ref, own, received, dra, drb, norm_ref, out, sums):
+def norm_one_kernel(info, x_ref, own, received, dra, drb, norm_ref, out):
     unit, scale = norm_stats(x_ref[block(info[2]), :].astype(f32))
-    grad = own[:RB] + received[:RB].astype(f32)
+    grad = own[...] + received[...].astype(f32)
     dr = jnp.where(info[1] == 0, dra[...], drb[...])
     out[...] = dr + norm_back(unit, scale, norm_ref[0:1], grad)
-    total = own[RB:] + received[RB:].astype(f32)
-    sums[...] = total[:8]
 
 
 def first_kernel(heads, info, src, d0, d1, d2, d3, out):
@@ -505,6 +532,8 @@
     grad = a[...].astype(f32) + b[...].astype(f32)
     grad += full[block(info[4], rows), :].astype(f32)
     cols = ins[0].shape[1]
+    if turned:
+        grad = grad[:, : cols + ins[3].shape[0]]
     second = grad[:, cols:]
     if turned:
         second = jnp.concatenate([second, jnp.zeros((LANES - rows, second.shape[1]), f32)], 0).T[:, :rows]
@@ -514,11 +543,18 @@
             ref[...] = value
 
 
-def norm_adam_kernel(info, sums, received, w, m, s, w_out, m_out, s_out):
-    total = sums[...] + received[...]
-    cols = w.shape[1]
-    shift = total.shape[1] - info[3] * cols
-    grad = pltpu.roll(total, shift, 1)[:4, :cols]
+def norm_sum_kernel(info, full, a, b, out, turn):
+    rows, width = a.shape
+    at = slice(width - LANES, width)
+    grad = a[:, at].astype(f32) + b[:, at].astype(f32) + full[block(info[4], rows), at].astype(f32)
+    turn[...] = jnp.zeros(turn.shape, f32)
+    turn[:rows] = grad
+    out[...] = turn[...].T[:8]
+
+
+def norm_adam_kernel(sums, received, w, m, s, w_out, m_out, s_out):
+    rows, cols = w.shape
+    grad = (sums[...] + received[...])[:rows, :cols]
     new = adamw(w[...], m[...], s[...], grad, RATES["norm"], 0.0)
     for ref, value in zip((w_out, m_out, s_out), new):
         ref[...] = value
@@ -534,6 +570,10 @@
 
 def swap_x(value):
     return lax.ppermute(value, "mp", [(i, i ^ 2) for i in range(4)])
+
+
+def both_cores(value):
+    return lax.all_gather(value, "mp", axis_index_groups=[[0, 1], [2, 3]], axis=0, tiled=True)
 
 
 FORWARD = [(RING[i], RING[(i + 1) % 8]) for i in range(8)]
@@ -615,7 +655,7 @@
         return tuple(new[:3]), tuple(new[3:])
     grad = lax.psum_scatter(full.astype(f32), "dp", scatter_dimension=0, tiled=True)
     cols = firsts[0].shape[1]
-    other = grad[:, cols:]
+    other = grad[:, cols : cols + seconds[0].shape[0 if turned else 1]]
     return (
         adamw(*firsts, grad[:, :cols], RATES[first], 0.1),
         adamw(*seconds, other.T if turned else other, RATES[second], 0.1),
@@ -670,6 +710,7 @@
                 pltpu.VMEM((LANES, LANES), f32),
                 pltpu.SemaphoreType.DMA((2,)),
             ],
+            vmem=60,
             far=True,
         )
         proj_t, fc_low, down_t = call(
@@ -685,6 +726,7 @@
                 pltpu.VMEM((cw, LANES), f32),
                 pltpu.SemaphoreType.DMA((3,)),
             ],
+            vmem=56,
             far=True,
         )
     else:
@@ -709,7 +751,7 @@
         ring_two = jnp.concatenate([fc_low, proj_t, proj_x], 1)
     two, three = Gather(ring_two), Gather(down_t)
     two.step()
-    first_t = first_values.T
+    first_t = after(first_values.T, unit_one)
     first_x, first_c = swap_x(first_t), swap_core(first_t)
     one.a, one.b = fence(one.a, one.b)
     one.step()
@@ -751,15 +793,27 @@
         )
 
     ctx_a, lse_a = attend(0, mixed)
-    xa, ca = swap_x(ctx_a), swap_core(ctx_a)
-    ctx_b, lse_b = attend(1, after(mixed, ctx_a))
-    xb, cb = swap_x(ctx_b), swap_core(ctx_b)
-    xca, xcb = swap_core(xa), swap_core(xb)
+    two.a, two.b, three.a, three.b, ctx_a = fence(two.a, two.b, three.a, three.b, ctx_a)
     two.step()
     three.step()
+    xa = swap_x(ctx_a)
+    ctx_b, lse_b = attend(1, after(mixed, ctx_a))
+    two.a, two.b, three.a, three.b, xa, ctx_b = fence(two.a, two.b, three.a, three.b, xa, ctx_b)
     two.step()
     three.step()
-    start, xca, xcb, two_last, three.a, three.b = fence(two.start, xca, xcb, two.a, three.a, three.b)
+    xb = swap_x(ctx_b)
+    (grad_out,) = call(
+        fetch_kernel,
+        "fetch",
+        (),
+        [after(grad_out, ctx_b)],
+        [(grad_out.shape, bf16)],
+        scratch=[pltpu.SemaphoreType.DMA],
+        vmem=4,
+        far=True,
+    )
+    start, xb, two_last, three.a, three.b, grad_out = fence(two.start, xb, two.a, three.a, three.b, grad_out)
+    ca, xca, cb, xcb = swap_core(ctx_a), swap_core(xa), swap_core(ctx_b), swap_core(xb)
     three.step()
     context, lse = (ctx_a, ctx_b), (lse_a, lse_b)
     wf, own_w, across_w = call(
@@ -837,12 +891,7 @@
     mlp_sum = Scatter("mlp", info, mlp_grad, mlp_fw, mlp_bw)
     mlp_sum.step()
     mine_b = add(1, after(dkeep_b, mlp_grad), *received_b)
-    ysend_a, ykeep_a = mlp_out(0, mine_b)
-    ysend_b, ykeep_b = mlp_out(1, ysend_a)
-    yreceived_a, yreceived_b = swap_core(ysend_a), swap_core(ysend_b)
-    across_a, mine_b, ykeep_b = fence(across_a, mine_b, ykeep_b)
     across_b = swap_x(mine_b)
-
     def norm_two(part, mine, across):
         return call(
             functools.partial(norm_two_kernel, part),
@@ -852,103 +901,110 @@
             [((RB, width), f32)] + [((RB // 2, width), bf16)] * 2,
         )
 
-    def attend_back(part, own, partner, before):
-        outs = [((half, width), bf16)]
-        if part:
-            outs += [((count, cols), bf16), ((cw, count), bf16)]
-        else:
-            outs += [((half, cw), f32)] * 3
+    def attend_back(stage, base, blocks, given, part, before, outs):
         return call(
-            functools.partial(attend_back_kernel, heads, part * half, bool(part)),
-            f"attend_back{part}",
+            functools.partial(attend_back_kernel, heads, base, blocks, stage),
+            f"attend_back{stage}",
             (info, src),
-            [mixed, values, *own, *partner, own_w, lse[part], *before],
+            [mixed, values, *given, own_w, lse[part], *before],
             outs,
             vmem=24,
         )
 
     dr_a, *ab_a = norm_two(0, after(mine_a, mine_b), across_a)
-
+    partner = [swap_core(v) for v in ab_a]
+    ab_one, dq_a, dk, dv = attend_back(
+        0, 0, 2, [*ab_a, *partner], 0, [], [((half, width), bf16)] + [((half, cw), f32)] * 3
+    )
+    mlp_sum.a, mlp_sum.b, dq_a = fence(mlp_sum.a, mlp_sum.b, dq_a)
+    mlp_sum.step()
+    ysend_a, ykeep_a = mlp_out(0, dq_a)
+    ysend_b, ykeep_b = mlp_out(1, ysend_a)
+    yreceived_a, yreceived_b = swap_core(ysend_a), swap_core(ysend_b)
     rows_mine, rows_sent = call(
         output_rows_kernel,
         "output_rows",
         (info,),
-        [after(ykeep_a, dr_a), ykeep_b, yreceived_a, yreceived_b],
+        [ykeep_a, ykeep_b, yreceived_a, yreceived_b],
         [((RB, width), f32), ((RB, width), bf16)],
     )
-    partner = [swap_core(v) for v in ab_a]
-    mlp_sum.a, mlp_sum.b, rows_sent, *partner = fence(mlp_sum.a, mlp_sum.b, rows_sent, *partner)
-    ab_one, dq, dk, dv = attend_back(0, ab_a, partner, [])
+    dr_b, *ab_b = norm_two(1, after(mine_b, ysend_b), across_b)
+    partner = [swap_core(v) for v in ab_b]
+    rows_received = swap_x(after(rows_sent, dr_b))
+    top = half + RB
+    ab_two, dq_b, dk, dv = attend_back(
+        1, half, 1, [*ab_b, *partner], 1, [dk, dv], [((half, width), bf16), ((RB, cw), f32)] + [((top, cw), f32)] * 2
+    )
+    mlp_sum.a, mlp_sum.b, dq_b = fence(mlp_sum.a, mlp_sum.b, dq_b)
     mlp_sum.step()
-    dr_b, *ab_b = norm_two(1, after(mine_b, dq), across_b)
-    rows_received = swap_x(after(rows_sent, dr_b))
-    ab_two, dmixed, dreused = attend_back(1, ab_b, [swap_core(v) for v in ab_b], [dq, dk, dv])
-    mlp_sum.a, mlp_sum.b, dmixed, rows_received = fence(mlp_sum.a, mlp_sum.b, dmixed, rows_received)
-    mlp_sum.step()
-
+    dmixed, dreused = attend_back(
+        2,
+        top,
+        1,
+        [ab_two],
+        1,
+        [after(dk, mlp_sum.last) if ring else dk, dv, dq_a, dq_b],
+        [((count, cols), bf16), ((cw, count), bf16)],
+    )
+
+    *isend, ikeep, sums = call(
+        input_kernel,
+        "input",
+        (info,),
+        [dmixed, qkv_full, unit_one, nacc_a, nacc_b],
+        [((RB, width), bf16)] * 2 + [((half, width), f32), ((8, width), f32)],
+    )
     qkv_grad, qkv_fw, qkv_bw = call(
         qkv_grad_kernel,
         "qkv_grad",
         (info,),
-        [a1, after(dmixed, mlp_sum.last) if ring else dmixed, ab_one, ab_two, context[0], context[1]],
-        [((width, cols + cw), bf16 if ring else f32)] + piece(cols + cw),
+        [a1, dmixed, ab_one, ab_two, context[0], context[1], sums],
+        [((width, cols + cw + LANES), bf16 if ring else f32)] + piece(cols + cw + LANES),
+        scratch=[pltpu.VMEM((LANES, width), f32)],
     )
     qkv_sum = Scatter("qkv", info, qkv_grad, qkv_fw, qkv_bw)
+    mlp_sum.a, mlp_sum.b, qkv_sum.a, qkv_sum.b, rows_received = fence(
+        mlp_sum.a, mlp_sum.b, qkv_sum.a, qkv_sum.b, rows_received
+    )
+    mlp_sum.step()
     qkv_sum.step()
-    isend, ikeep = call(
-        input_kernel,
-        "input",
+    gathered = [swap_core(v) for v in isend]
+    mine, sent = call(
+        to_rows_kernel, "to_rows", (info,), [ikeep, *gathered], [((RB, width), f32), ((RB, width), bf16)]
+    )
+    across, dx = swap_x(sent), swap_x(dreused)
+    qkv_sum.a, qkv_sum.b, sent = fence(qkv_sum.a, qkv_sum.b, sent)
+    qkv_sum.step()
+    (block_out,) = call(
+        output_kernel,
+        "output",
         (info,),
-        [after(dmixed, qkv_fw), qkv_full, unit_one, nacc_a, nacc_b],
-        [((half + 16, width), bf16), ((half + 16, width), f32)],
-    )
-    mine, sent = call(
-        to_rows_kernel,
-        "to_rows",
-        (info,),
-        [ikeep, swap_core(isend)],
-        [((RB + 16, width), f32), ((RB + 16, width), bf16)],
-    )
-    across = swap_x(sent)
-    mlp_sum.a, mlp_sum.b, qkv_sum.a, qkv_sum.b = fence(mlp_sum.a, mlp_sum.b, qkv_sum.a, qkv_sum.b)
+        [resid[0], resid[1], rows_mine, rows_received],
+        [((RB, width), bf16)],
+    )
+    qkv_sum.a, qkv_sum.b, mlp_sum.a, block_out = fence(qkv_sum.a, qkv_sum.b, mlp_sum.a, block_out)
     qkv_sum.step()
-    mlp_sum.step()
-    qkv_sum.a, qkv_sum.b = fence(qkv_sum.a, qkv_sum.b)
+    fc_new, down_new = update(
+        ("fc", "down"),
+        info,
+        mlp_grad,
+        mlp_sum.ends(),
+        [fc_weight, fc_moment, fc_second],
+        [down_weight.T, down_moment.T, down_second.T],
+        False,
+    )
+    qkv_sum.a, qkv_sum.b, across, dx, *fc_new = fence(qkv_sum.a, qkv_sum.b, across, dx, *fc_new)
+    down_new = tuple(v.T for v in down_new)
     qkv_sum.step()
-    dx, dc = swap_x(dreused), swap_core(dreused)
-    qkv_sum.a, qkv_sum.b, across = fence(qkv_sum.a, qkv_sum.b, across)
-    qkv_sum.step()
-    input_grad, sums = call(
+    (input_grad,) = call(
         norm_one_kernel,
         "norm_one",
         (info,),
         [tokens, mine, across, dr_a, dr_b, norms],
-        [((RB, width), f32), ((8, width), f32)],
-    )
-    (block_out,) = call(
-        output_kernel,
-        "output",
-        (info,),
-        [resid[0], resid[1], after(rows_mine, input_grad), rows_received],
-        [((RB, width), bf16)],
-    )
-    dxc = swap_core(dx)
-    mlp_ends = mlp_sum.ends()
-    if ring:
-        hop = lambda value, bit: lax.ppermute(value, "dp", [(i, i ^ bit) for i in range(n)])
-        for bit in (1, 2):
-            (sums,) = call(sum_kernel, f"sum{bit}", (), [sums, hop(sums, bit)], [(sums.shape, f32)])
-        received = hop(sums, 4)
-    fc_new, down_new = update(
-        ("fc", "down"),
-        info,
-        mlp_grad,
-        mlp_ends,
-        [fc_weight, fc_moment, fc_second],
-        [down_weight.T, down_moment.T, down_second.T],
-        False,
-    )
-    down_new = tuple(v.T for v in down_new)
+        [((RB, width), f32)],
+    )
+    dx, dreused = fence(dx, dreused)
+    dc, dxc = swap_core(dreused), swap_core(dx)
     (first_grad,) = call(
         functools.partial(first_kernel, heads),
         "first",
@@ -956,12 +1012,24 @@
         [dreused, dc, dx, dxc],
         [((cw, count), f32)],
     )
+    qkv_sum.a, input_grad, first_grad = fence(qkv_sum.a, input_grad, first_grad)
+    if ring:
+        (sums,) = call(
+            norm_sum_kernel,
+            "norm_sum",
+            (info,),
+            [qkv_grad, *qkv_sum.ends()],
+            [((8, LANES), f32)],
+            scratch=[pltpu.VMEM((LANES, LANES), f32)],
+        )
+        (sums,) = call(sum_kernel, "sum", (), [sums, swap_core(sums)], [(sums.shape, f32)])
+        received = swap_x(sums)
     qkv_new, proj_new = update(
         ("qkv", "proj"),
         info,
         qkv_grad,
         qkv_sum.ends(),
-        [after(qkv_weight, first_grad), qkv_moment, qkv_second],
+        [qkv_weight, qkv_moment, qkv_second],
         [proj_weight, proj_moment, proj_second],
         True,
     )
@@ -969,12 +1037,12 @@
         norm_new = call(
             norm_adam_kernel,
             "adam_norm",
-            (info,),
+            (),
             [sums, received, norm_params, norm_moment, norm_second],
             [(norm_params.shape, f32)] * 3,
         )
     else:
-        own = lax.psum_scatter(sums, "dp", scatter_dimension=1, tiled=True)[:4]
+        own = lax.psum_scatter(lax.psum(sums, "mp"), "dp", scatter_dimension=1, tiled=True)[:4]
         norm_new = adamw(norm_params, norm_moment, norm_second, own, RATES["norm"], 0.0)
     return (block_out, input_grad, first_grad.T, *qkv_new, *proj_new, *fc_new, *down_new, *norm_new)
 

time: 174 us -> 154 us (0.89)
  waiting for transfers between devices: 56.9 us -> 44.5 us
  starting transfers between devices: 56.7 us -> 50.6 us
  local copies, waits for them, and re-layouts: 7.21 us -> 1.51 us
  Pallas kernels: 51.3 us -> 55.5 us
    ppermute x15, waiting for transfers between devices: 16.1 us -> 8.32 us  [behind(): return lax.ppermute(value, 'dp', BACKWARD)]
    unnamed x50 -> x48, local copies, waits for them, and re-layouts: 7.21 us -> 1.51 us
    ppermute x3 -> x0, waiting for transfers between devices: 5.16 us -> none  [local(): lax.ppermute(value, 'dp', [(i, i ^ bit) for i in range(n)])]
    pallas_call x41 -> x43, Pallas kernels: 51.3 us -> 55.5 us  [call(): pl.pallas_call(kernel, in_specs=[smem] * len(scalars) + [given] * len(ins...]
    ppermute x9 -> x10, starting transfers between devices: 11.9 us -> 8.23 us  [swap_x(): return lax.ppermute(value, 'mp', [(i, i ^ 2) for i in range(4)])]
    ppermute x15, starting transfers between devices: 8.14 us -> 11.3 us  [behind(): return lax.ppermute(value, 'dp', BACKWARD)]
    ppermute x20, starting transfers between devices: 29 us -> 25.9 us  [ahead(): return lax.ppermute(value, 'dp', FORWARD)]
    ppermute x3 -> x0, starting transfers between devices: 3.01 us -> none  [local(): lax.ppermute(value, 'dp', [(i, i ^ bit) for i in range(n)])]
  transfers between devices with their start and end apart: 68 -> 68, of which waited for: 25 -> 30; matrix products, arithmetic and copies ran while one was open for 0% -> 0% of each run, Pallas kernels for 24% -> 33%
where the time goes in v3:
time: 154 us; the launch traced here: 153 us
  Pallas kernels  55.5 us (36%)
  starting transfers between devices  50.6 us (33%)
  waiting for transfers between devices  44.5 us (29%)
    pallas_call x43, Pallas kernels, call(): pl.pallas_call(kernel, in_specs=[smem] * len(scalars) + [given] * len(ins...  55.5 us
    ppermute x20, starting transfers between devices, ahead(): return lax.ppermute(value, 'dp', FORWARD)  25.9 us
    ppermute x20, waiting for transfers between devices, ahead(): return lax.ppermute(value, 'dp', FORWARD)  23.8 us
    ppermute x15, starting transfers between devices, behind(): return lax.ppermute(value, 'dp', BACKWARD)  11.3 us
    ppermute x10, waiting for transfers between devices, swap_x(): return lax.ppermute(value, 'mp', [(i, i ^ 2) for i in range(4)])  10 us
    ppermute x15, waiting for transfers between devices, behind(): return lax.ppermute(value, 'dp', BACKWARD)  8.32 us
    ppermute x10, starting transfers between devices, swap_x(): return lax.ppermute(value, 'mp', [(i, i ^ 2) for i in range(4)])  8.23 us
    ppermute x23, starting transfers between devices, swap_core(): return lax.ppermute(value, 'mp', [(i, i ^ 1) for i in range(4)])  5.1 us
  transfers between devices with their start and end apart: 68, of which 30 were waited for; matrix products, arithmetic and copies ran while one was open for 0% of the time, Pallas kernels for 33%

profile of v3, /device:TPU:0, one launch (start us, length us, event | category | flops | bytes accessed | tf_op | source)
XLA Modules:
  0.0 153.3 jit_solution(15714893747761889607)
XLA Ops:
  0.7 1.8 %prep_one.1.refs_1_ = bf16[96,640]{1,0:T(8,128)(2,1)} custom-call(f32[96,576]{1,0:T(8,128)} %refs_3_.3, f32[4,96]{1,0:T(4,128)} %w.1), custom_call_target="tpu_custom_call" | custom-call | flops 1 | bytes 1 | tf_op jit(solution)/shard_map/prep_one/pallas_call | solution.py:65
  2.4 3.1 %collective-permute-start = (bf16[96,640]{1,0:T(8,128)(2,1)}, bf16[96,640]{1,0:T(8,128)(2,1)S(1)}, u32[]{:S(2)}, u32[]{:S(2)}) collective-permute-start(bf16[96,640]{1,0:T(8,128)(2,1)} %prep_one.1.refs_1_), channel_id=1, source_target_pairs={{0,8},{8,16},{16,24},{24,28},{28,20},{20,12},{12,4},{4,0},{1,9},{9... | collective-permute-start | bytes 368648 | tf_op jit(solution)/shard_map/ppermute | solution.py:584
  5.5 1.9 %prep_two.1 = (bf16[96,192]{1,0:T(8,128)(2,1)}, bf16[96,768]{1,0:T(8,128)(2,1)}, bf16[96,768]{1,0:T(8,128)(2,1)}) custom-call(f32[192,96]{1,0:T(8,128)} %refs_6_.1, f32[96,768]{1,0:T(8,128)} %refs_3_.2, f32[96,768]{1,0:T(8,128)} %bitcast.8), custom_call_target="tpu_custom_call" | custom-call | flops 1 | bytes 1 | tf_op jit(solution)/shard_map/prep_two/pallas_call | solution.py:65
  7.4 1.6 %collective-permute-done.refs_2_ = bf16[96,640]{1,0:T(8,128)(2,1)S(1)} collective-permute-done((bf16[96,640]{1,0:T(8,128)(2,1)}, bf16[96,640]{1,0:T(8,128)(2,1)S(1)}, u32[]{:S(2)}, u32[]{:S(2)}) %collective-permute-start) | collective-permute-done | bytes 122912 | tf_op jit(solution)/shard_map/ppermute | solution.py:584
  9.0 1.6 %collective-permute-done.1.refs_6_ = bf16[96,640]{1,0:T(8,128)(2,1)S(1)} collective-permute-done((bf16[96,640]{1,0:T(8,128)(2,1)}, bf16[96,640]{1,0:T(8,128)(2,1)S(1)}, u32[]{:S(2)}, u32[]{:S(2)}) %collective-permute-start.1) | collective-permute-done | bytes 122912 | tf_op jit(solution)/shard_map/ppermute | solution.py:588
  10.6 1.6 %collective-permute-start.2 = (bf16[96,640]{1,0:T(8,128)(2,1)S(1)}, bf16[96,640]{1,0:T(8,128)(2,1)S(1)}, u32[]{:S(2)}, u32[]{:S(2)}) collective-permute-start(bf16[96,640]{1,0:T(8,128)(2,1)S(1)} %collective-permute-done.refs_2_), channel_id=1, source_target_pairs={{0,8},{8,16},{16,24},{24,28},{28,20},{20,12},{12,4},{4,0},{1,9},{9... | collective-permute-start | bytes 368648 | tf_op jit(solution)/shard_map/ppermute | solution.py:584
  12.6 1.5 collective-permute-start.4
  14.1 1.4 copy-done
  17.1 1.5 collective-permute-start.10
  18.6 1.6 %collective-permute-start.5 = (bf16[96,640]{1,0:T(8,128)(2,1)S(1)}, bf16[96,640]{1,0:T(8,128)(2,1)S(1)}, u32[]{:S(2)}, u32[]{:S(2)}) collective-permute-start(bf16[96,640]{1,0:T(8,128)(2,1)S(1)} %collective-permute-done.2.refs_3_), channel_id=1, source_target_pairs={{0,8},{8,16},{16,24},{24,28},{28,20},{20,12},{12,4},{4,0},{1,9},{9... | collective-permute-start | bytes 368648 | tf_op jit(solution)/shard_map/ppermute | solution.py:584
  20.7 1.6 %collective-permute-start.8 = (bf16[96,1152]{1,0:T(8,128)(2,1)S(1)}, bf16[96,1152]{1,0:T(8,128)(2,1)S(1)}, u32[]{:S(2)}, u32[]{:S(2)}) collective-permute-start(bf16[96,1152]{1,0:T(8,128)(2,1)S(1)} %join.1.refs_0_), channel_id=1, source_target_pairs={{0,8},{8,16},{16,24},{24,28},{28,20},{20,12},{12,4},{4,0},{1,9},{9... | collective-permute-start | bytes 663560 | tf_op jit(solution)/shard_map/ppermute | solution.py:584
  22.8 1.0 collective-permute-done.5.refs_4_
  23.7 1.3 collective-permute-done.6.refs_8_
  25.0 1.5 collective-permute-start.7
  26.7 1.6 %collective-permute-done.9.refs_5_ = bf16[96,1152]{1,0:T(8,128)(2,1)S(1)} collective-permute-done((bf16[96,1152]{1,0:T(8,128)(2,1)S(1)}, bf16[96,1152]{1,0:T(8,128)(2,1)S(1)}, u32[]{:S(2)}, u32[]{:S(2)}) %collective-permute-start.9) | collective-permute-done | bytes 221216 | tf_op jit(solution)/shard_map/ppermute | solution.py:588
  28.2 1.7 %collective-permute-done.7.refs_5_ = bf16[96,640]{1,0:T(8,128)(2,1)S(1)} collective-permute-done((bf16[96,640]{1,0:T(8,128)(2,1)S(1)}, bf16[96,640]{1,0:T(8,128)(2,1)S(1)}, u32[]{:S(2)}, u32[]{:S(2)}) %collective-permute-start.7) | collective-permute-done | bytes 122912 | tf_op jit(solution)/shard_map/ppermute | solution.py:584
  29.9 1.6 %collective-permute-start.13 = (bf16[96,1152]{1,0:T(8,128)(2,1)S(1)}, bf16[96,1152]{1,0:T(8,128)(2,1)S(1)}, u32[]{:S(2)}, u32[]{:S(2)}) collective-permute-start(bf16[96,1152]{1,0:T(8,128)(2,1)S(1)} %collective-permute-done.8.refs_1_), channel_id=1, source_target_pairs={{0,8},{8,16},{16,24},{24,28},{28,20},{20,12},{12,4},{4,0},{1,9},{9... | collective-permute-start | bytes 663560 | tf_op jit(solution)/shard_map/ppermute | solution.py:584
  32.0 1.5 collective-permute-start.15
  34.0 2.4 %qkv.1 = (bf16[1024,768]{1,0:T(8,128)(2,1)S(1)}, bf16[1024,576]{1,0:T(8,128)(2,1)S(1)}, bf16[192,1024]{1,0:T(8,128)(2,1)S(1)}, bf16[768,640]{1,0:T(8,128)(2,1)S(1)}, f32[8,768]{1,0:T(8,128)S(1)}) custom-call(f32[1024,768]{1,0:T(8,128)S(1)} %unit.1.refs_0_.refs_2_, bf16[96,640]{1,0:T(8,128)(2,1)S(1)} %copy-done.6, ...), custom_call_target="tpu_custom_call" | custom-call | flops 1 | bytes 1 | tf_op jit(solution)/shard_map/qkv/pallas_call | solution.py:65
  37.2 1.8 %attend0.1 = (bf16[512,192]{1,0:T(8,128)(2,1)S(1)}, f32[8,512]{1,0:T(8,128)S(1)}) custom-call(bf16[1024,576]{1,0:T(8,128)(2,1)S(1)} %get-tuple-element.250.m_ref.refs_1_, bf16[192,1024]{1,0:T(8,128)(2,1)S(1)} %values.1.v_ref.refs_2_), custom_call_target="tpu_custom_call" | custom-call | flops 1 | bytes 1 | tf_op jit(solution)/shard_map/attend0/pallas_call | solution.py:65
  39.0 1.9 %collective-permute-done.15.refs_1_ = bf16[96,768]{1,0:T(8,128)(2,1)S(1)} collective-permute-done((bf16[96,768]{1,0:T(8,128)(2,1)S(1)}, bf16[96,768]{1,0:T(8,128)(2,1)S(1)}, u32[]{:S(2)}, u32[]{:S(2)}) %collective-permute-start.15) | collective-permute-done | bytes 147488 | tf_op jit(solution)/shard_map/ppermute | solution.py:584
  40.9 1.3 collective-permute-done.16.refs_5_
  42.3 1.7 %collective-permute-start.18 = (bf16[96,1152]{1,0:T(8,128)(2,1)S(1)}, bf16[96,1152]{1,0:T(8,128)(2,1)S(1)}, u32[]{:S(2)}, u32[]{:S(2)}) collective-permute-start(bf16[96,1152]{1,0:T(8,128)(2,1)S(1)} %collective-permute-done.13.refs_2_), channel_id=1, source_target_pairs={{0,8},{8,16},{16,24},{24,28},{28,20},{20,12},{12,4},{4,0},{1,9},{9... | collective-permute-start | bytes 663560 | tf_op jit(solution)/shard_map/ppermute | solution.py:584
  44.7 1.5 collective-permute-start.20
  46.8 3.9 %attend1.1 = (bf16[512,192]{1,0:T(8,128)(2,1)S(1)}, f32[8,512]{1,0:T(8,128)S(1)}) custom-call(bf16[1024,576]{1,0:T(8,128)(2,1)S(1)} %get-tuple-element.250.m_ref.refs_1_, bf16[192,1024]{1,0:T(8,128)(2,1)S(1)} %values.1.v_ref.refs_2_), custom_call_target="tpu_custom_call" | custom-call | flops 1 | bytes 1 | tf_op jit(solution)/shard_map/attend1/pallas_call | solution.py:65
  50.7 1.5 collective-permute-done.20.refs_2_
  52.2 1.4 collective-permute-done.21.refs_6_
  53.6 1.0 collective-permute-start.25
  55.5 1.4 collective-permute-start.27
  56.9 5.4 %collective-permute-done.26.refs_3_ = bf16[96,768]{1,0:T(8,128)(2,1)S(1)} collective-permute-done((bf16[96,768]{1,0:T(8,128)(2,1)S(1)}, bf16[96,768]{1,0:T(8,128)(2,1)S(1)}, u32[]{:S(2)}, u32[]{:S(2)}) %collective-permute-start.26) | collective-permute-done | bytes 147488 | tf_op jit(solution)/shard_map/ppermute | solution.py:584
  64.0 1.1 collective-permute-start.32
  65.2 3.4 %mlp0.1 = (f32[512,768]{1,0:T(8,128)S(1)}, f32[512,768]{1,0:T(8,128)S(1)}, bf16[512,768]{1,0:T(8,128)(2,1)S(1)}, bf16[512,768]{1,0:T(8,128)(2,1)S(1)}, f32[512,768]{1,0:T(8,128)S(1)}) custom-call(bf16[1024,768]{1,0:T(8,128)(2,1)S(1)} %copy-done.1, f32[8,768]{1,0:T(8,128)S(1)} %get-tuple-element.265.norm_ref.refs_4_.refs_5_, ...), custom_call_target="tpu_custom_call" | custom-call | flops 1 | bytes 1 | tf_op jit(solution)/shard_map/mlp0/pallas_call | solution.py:65
  68.6 3.4 %mlp1.1 = (f32[512,768]{1,0:T(8,128)S(1)}, f32[512,768]{1,0:T(8,128)S(1)}, bf16[512,768]{1,0:T(8,128)(2,1)S(1)}, bf16[512,768]{1,0:T(8,128)(2,1)S(1)}, f32[512,768]{1,0:T(8,128)S(1)}) custom-call(bf16[1024,768]{1,0:T(8,128)(2,1)S(1)} %copy-done.1, f32[8,768]{1,0:T(8,128)S(1)} %get-tuple-element.265.norm_ref.refs_4_.refs_5_, ...), custom_call_target="tpu_custom_call" | custom-call | flops 1 | bytes 1 | tf_op jit(solution)/shard_map/mlp1/pallas_call | solution.py:65
  72.1 1.9 %mlp_back0.1 = (bf16[512,768]{1,0:T(8,128)(2,1)S(1)}, bf16[128,768]{1,0:T(8,128)(2,1)S(1)}, bf16[128,768]{1,0:T(8,128)(2,1)S(1)}, f32[256,768]{1,0:T(8,128)S(1)}, f32[8,768]{1,0:T(8,128)S(1)}) custom-call(bf16[1024,768]{1,0:T(8,128)(2,1)S(1)} %fetch.1.refs_0_.refs_4_.refs_3_, f32[512,768]{1,0:T(8,128)S(1)} %get-tuple-element.271.refs_1_, ...), custom_call_target="tpu_custom_call" | custom-call | flops 1 | bytes 1 | tf_op jit(solution)/shard_map/mlp_back0/pallas_call | solution.py:65
  74.6 1.9 %mlp_back1.1 = (bf16[512,768]{1,0:T(8,128)(2,1)S(1)}, bf16[128,768]{1,0:T(8,128)(2,1)S(1)}, bf16[128,768]{1,0:T(8,128)(2,1)S(1)}, f32[256,768]{1,0:T(8,128)S(1)}, f32[8,768]{1,0:T(8,128)S(1)}) custom-call(bf16[1024,768]{1,0:T(8,128)(2,1)S(1)} %fetch.1.refs_0_.refs_4_.refs_3_, f32[512,768]{1,0:T(8,128)S(1)} %get-tuple-element.277.refs_1_, ...), custom_call_target="tpu_custom_call" | custom-call | flops 1 | bytes 1 | tf_op jit(solution)/shard_map/mlp_back1/pallas_call | solution.py:65
  77.6 3.1 %mlp_grad.1 = (bf16[768,1536]{1,0:T(8,128)(2,1)S(1)}, bf16[96,1536]{1,0:T(8,128)(2,1)S(1)}, bf16[96,1536]{1,0:T(8,128)(2,1)S(1)}) custom-call(bf16[512,768]{1,0:T(8,128)(2,1)S(1)} %get-tuple-element.286.refs_0_, bf16[512,768]{1,0:T(8,128)(2,1)S(1)} %get-tuple-element.287.refs_1_, bf16[512,768]{1,0:T(8,128)(2,1)S(1)} %get-tuple-element.275.refs_2_, ...), custom_call_target="tpu_custom_call" | custom-call | flops 1 | bytes 1 | tf_op jit(solution)/shard_map/mlp_grad/pallas_call | solution.py:65
  81.6 1.2 collective-permute-start.38
  82.9 5.0 %collective-permute-done.39.refs_2_ = bf16[256,768]{1,0:T(8,128)(2,1)S(1)} collective-permute-done((bf16[256,768]{1,0:T(8,128)(2,1)S(1)}, bf16[256,768]{1,0:T(8,128)(2,1)S(1)}, u32[]{:S(2)}, u32[]{:S(2)}) %collective-permute-start.39) | collective-permute-done | bytes 393248 | tf_op jit(solution)/shard_map/ppermute | solution.py:572
  90.2 3.8 %attend_back0.1 = (bf16[512,768]{1,0:T(8,128)(2,1)S(1)}, f32[512,192]{1,0:T(8,128)S(1)}, f32[512,192]{1,0:T(8,128)S(1)}, f32[512,192]{1,0:T(8,128)S(1)}) custom-call(s32[12]{0:T(128)S(1)} %copy-done.20, bf16[1024,576]{1,0:T(8,128)(2,1)S(1)} %get-tuple-element.250.m_ref.refs_1_, bf16[192,1024]{1,0:T(8,128)(2,1)S(1)} %values.1.v_ref.refs_2_, ...), custom_call_target="tpu_custom_call" | custom-call | flops 1 | bytes 1 | tf_op jit(solution)/shard_map/attend_back0/pallas_call | solution.py:65
  96.4 1.0 collective-permute-start.45
  97.4 1.1 collective-permute-start.46
  98.5 1.7 %collective-permute-done.42.refs_2_ = bf16[256,768]{1,0:T(8,128)(2,1)S(1)} collective-permute-done((bf16[256,768]{1,0:T(8,128)(2,1)S(1)}, bf16[256,768]{1,0:T(8,128)(2,1)S(1)}, u32[]{:S(2)}, u32[]{:S(2)}) %collective-permute-start.42) | collective-permute-done | bytes 393248 | tf_op jit(solution)/shard_map/ppermute | solution.py:572
  102.5 3.5 %attend_back1.1 = (bf16[512,768]{1,0:T(8,128)(2,1)S(1)}, f32[256,192]{1,0:T(8,128)S(1)}, f32[768,192]{1,0:T(8,128)S(1)}, f32[768,192]{1,0:T(8,128)S(1)}) custom-call(s32[12]{0:T(128)S(1)} %copy-done.20, bf16[1024,576]{1,0:T(8,128)(2,1)S(1)} %get-tuple-element.250.m_ref.refs_1_, bf16[192,1024]{1,0:T(8,128)(2,1)S(1)} %values.1.v_ref.refs_2_, ...), custom_call_target="tpu_custom_call" | custom-call | flops 1 | bytes 1 | tf_op jit(solution)/shard_map/attend_back1/pallas_call | solution.py:65
  106.5 1.1 collective-permute-start.48
  108.5 4.0 %attend_back2.1 = (bf16[1024,576]{1,0:T(8,128)(2,1)S(1)}, bf16[192,1024]{1,0:T(8,128)(2,1)S(1)}) custom-call(s32[12]{0:T(128)S(1)} %copy-done.20, bf16[1024,576]{1,0:T(8,128)(2,1)S(1)} %get-tuple-element.250.m_ref.refs_1_, bf16[192,1024]{1,0:T(8,128)(2,1)S(1)} %values.1.v_ref.refs_2_, bf16[512,768]{1,0:T(8,128)(2,1)S(1)} %get-tuple-element.311.refs_3_, ...), custom_call_target="tpu_custom_call" | custom-call | flops 1 | bytes 1 | tf_op jit(solution)/shard_map/attend_back2/pallas_call | solution.py:65
  112.6 2.2 %input.1 = (bf16[256,768]{1,0:T(8,128)(2,1)S(1)}, bf16[256,768]{1,0:T(8,128)(2,1)S(1)}, f32[512,768]{1,0:T(8,128)S(1)}, f32[8,768]{1,0:T(8,128)S(1)}) custom-call(bf16[1024,576]{1,0:T(8,128)(2,1)S(1)} %get-tuple-element.324.refs_0_.refs_1_, bf16[768,640]{1,0:T(8,128)(2,1)S(1)} %get-tuple-element.326.refs_1_, f32[1024,768]{1,0:T(8,128)S(1)} %unit.1.refs_0_.refs_2_, ...), custom_call_target="tpu_custom_call" | custom-call | flops 1 | bytes 1 | tf_op jit(solution)/shard_map/input/pallas_call | solution.py:65
  115.3 2.7 %qkv_grad.1 = (bf16[768,896]{1,0:T(8,128)(2,1)S(1)}, bf16[96,896]{1,0:T(8,128)(2,1)S(1)}, bf16[96,896]{1,0:T(8,128)(2,1)S(1)}) custom-call(bf16[1024,768]{1,0:T(8,128)(2,1)S(1)} %get-tuple-element.228.refs_0_, bf16[1024,576]{1,0:T(8,128)(2,1)S(1)} %get-tuple-element.324.refs_0_.refs_1_, bf16[512,768]{1,0:T(8,128)(2,1)S(1)} %get-tuple-element.325.refs_2_, ...), custom_call_target="tpu_custom_call" | custom-call | flops 1 | bytes 1 | tf_op jit(solution)/shard_map/qkv_grad/pallas_call | solution.py:65
  119.0 1.2 collective-permute-start.53
  121.1 1.0 collective-permute-start.62
  122.4 1.1 collective-permute-start.61
  123.5 1.9 %collective-permute-done.52.refs_1_ = bf16[96,896]{1,0:T(8,128)(2,1)S(1)} collective-permute-done((bf16[96,896]{1,0:T(8,128)(2,1)S(1)}, bf16[96,896]{1,0:T(8,128)(2,1)S(1)}, u32[]{:S(2)}, u32[]{:S(2)}) %collective-permute-start.52) | collective-permute-done | bytes 172064 | tf_op jit(solution)/shard_map/ppermute | solution.py:584
  126.4 1.2 collective-permute-start.57
  128.4 3.2 %collective-permute-done.58.refs_1_ = bf16[96,1536]{1,0:T(8,128)(2,1)S(1)} collective-permute-done((bf16[96,1536]{1,0:T(8,128)(2,1)S(1)}, bf16[96,1536]{1,0:T(8,128)(2,1)S(1)}, u32[]{:S(2)}, u32[]{:S(2)}) %collective-permute-start.58) | collective-permute-done | bytes 294944 | tf_op jit(solution)/shard_map/ppermute | solution.py:584
  131.6 2.8 %collective-permute-done.56.refs_1_ = bf16[96,896]{1,0:T(8,128)(2,1)S(1)} collective-permute-done((bf16[96,896]{1,0:T(8,128)(2,1)S(1)}, bf16[96,896]{1,0:T(8,128)(2,1)S(1)}, u32[]{:S(2)}, u32[]{:S(2)}) %collective-permute-start.56) | collective-permute-done | bytes 172064 | tf_op jit(solution)/shard_map/ppermute | solution.py:584
  135.5 1.2 collective-permute-start.60
  136.7 1.6 %adam_fc.1 = (f32[96,768]{1,0:T(8,128)}, f32[96,768]{1,0:T(8,128)}, f32[96,768]{1,0:T(8,128)}, f32[96,768]{1,0:T(8,128)}, f32[96,768]{1,0:T(8,128)}, /*index=5*/f32[96,768]{1,0:T(8,128)}) custom-call(bf16[768,1536]{1,0:T(8,128)(2,1)S(1)} %get-tuple-element.289.refs_0_, bf16[96,1536]{1,0:T(8,128)(2,1)S(1)} %collective-permute-done.58.refs_1_, ...), custom_call_target="tpu_custom_call" | custom-call | flops 1 | bytes 1 | tf_op jit(solution)/shard_map/adam_fc/pallas_call | solution.py:65
  138.3 1.5 collective-permute-done.61.refs_2_
  142.3 1.5 norm_one.1
  143.8 1.6 %first.1 = f32[192,1024]{1,0:T(8,128)} custom-call(s32[12]{0:T(128)S(1)} %copy-done.20, bf16[192,1024]{1,0:T(8,128)(2,1)S(1)} %get-tuple-element.368.refs_1_, bf16[192,1024]{1,0:T(8,128)(2,1)S(1)} %collective-permute-done.64.refs_2_, bf16[192,1024]{1,0:T(8,128)(2,1)S(1)} %collective-permute-done.62.refs_3_, bf16[192,1024]{1,0:T(8,128)(2,1)S(1)} %collective-permute-done.65.refs_4_), custom_call_target="tpu_custom_call" | custom-call | flops 1 | bytes 1 | tf_op jit(solution)/shard_map/first/pallas_call | solution.py:65
  145.4 2.4 %collective-permute-done.63.refs_1_ = bf16[96,896]{1,0:T(8,128)(2,1)S(1)} collective-permute-done((bf16[96,896]{1,0:T(8,128)(2,1)S(1)}, bf16[96,896]{1,0:T(8,128)(2,1)S(1)}, u32[]{:S(2)}, u32[]{:S(2)}) %collective-permute-start.63) | collective-permute-done | bytes 172064 | tf_op jit(solution)/shard_map/ppermute | solution.py:584
  147.9 1.2 collective-permute-done.66.b
  149.1 1.0 collective-permute-start.67
  150.1 1.3 adam_qkv.1
  151.4 1.3 collective-permute-done.67.received
  (163 shorter events, 28.8 us)
Async XLA Ops:
  2.4 6.6 %collective-permute-start = (bf16[96,640]{1,0:T(8,128)(2,1)}, bf16[96,640]{1,0:T(8,128)(2,1)S(1)}, u32[]{:S(2)}, u32[]{:S(2)}) collective-permute-start(bf16[96,640]{1,0:T(8,128)(2,1)} %prep_one.1.refs_1_), channel_id=1, source_target_pairs={{0,8},{8,16},{16,24},{24,28},{28,20},{20,12},{12,4},{4,0},{1,9},{9... | collective-permute-start | bytes 368648 | tf_op jit(solution)/shard_map/ppermute | solution.py:584
  5.5 5.1 %collective-permute-start.1 = (bf16[96,640]{1,0:T(8,128)(2,1)}, bf16[96,640]{1,0:T(8,128)(2,1)S(1)}, u32[]{:S(2)}, u32[]{:S(2)}) collective-permute-start(bf16[96,640]{1,0:T(8,128)(2,1)} %prep_one.1.refs_1_), channel_id=1, source_target_pairs={{8,0},{16,8},{24,16},{28,24},{20,28},{12,20},{4,12},{0,4},{9,1},{1... | collective-permute-start | bytes 368648 | tf_op jit(solution)/shard_map/ppermute | solution.py:588
  10.6 6.3 %collective-permute-start.2 = (bf16[96,640]{1,0:T(8,128)(2,1)S(1)}, bf16[96,640]{1,0:T(8,128)(2,1)S(1)}, u32[]{:S(2)}, u32[]{:S(2)}) collective-permute-start(bf16[96,640]{1,0:T(8,128)(2,1)S(1)} %collective-permute-done.refs_2_), channel_id=1, source_target_pairs={{0,8},{8,16},{16,24},{24,28},{28,20},{20,12},{12,4},{4,0},{1,9},{9... | collective-permute-start | bytes 368648 | tf_op jit(solution)/shard_map/ppermute | solution.py:584
  12.2 4.9 %collective-permute-start.3 = (bf16[96,640]{1,0:T(8,128)(2,1)S(1)}, bf16[96,640]{1,0:T(8,128)(2,1)S(1)}, u32[]{:S(2)}, u32[]{:S(2)}) collective-permute-start(bf16[96,640]{1,0:T(8,128)(2,1)S(1)} %collective-permute-done.1.refs_6_), channel_id=1, source_target_pairs={{8,0},{16,8},{24,16},{28,24},{20,28},{12,20},{4,12},{0,4},{9,1},{1... | collective-permute-start | bytes 368648 | tf_op jit(solution)/shard_map/ppermute | solution.py:588
  12.6 4.3 %collective-permute-start.4 = (bf16[96,192]{1,0:T(8,128)(2,1)}, bf16[96,192]{1,0:T(8,128)(2,1)S(1)}, u32[]{:S(2)}, u32[]{:S(2)}) collective-permute-start(bf16[96,192]{1,0:T(8,128)(2,1)} %get-tuple-element.212.own), channel_id=1, source_target_pairs={{0,2},{1,3},{2,0},{3,1},{4,6},{5,7},{6,4},{7,5},{8,10},{9,11},{10,... | collective-permute-start | bytes 110600 | tf_op jit(solution)/shard_map/ppermute | solution.py:572
  17.1 12.8 %collective-permute-start.10 = (bf16[192,1024]{1,0:T(8,128)(2,1)S(1)}, bf16[192,1024]{1,0:T(8,128)(2,1)S(1)}, u32[]{:S(2)}, u32[]{:S(2)}) collective-permute-start(bf16[192,1024]{1,0:T(8,128)(2,1)S(1)} %bitcast.10), channel_id=1, source_target_pairs={{0,2},{1,3},{2,0},{3,1},{4,6},{5,7},{6,4},{7,5},{8,10},{9,11},{10,... | collective-permute-start | bytes 1179656 | tf_op jit(solution)/shard_map/ppermute | solution.py:572
  18.6 5.2 %collective-permute-start.5 = (bf16[96,640]{1,0:T(8,128)(2,1)S(1)}, bf16[96,640]{1,0:T(8,128)(2,1)S(1)}, u32[]{:S(2)}, u32[]{:S(2)}) collective-permute-start(bf16[96,640]{1,0:T(8,128)(2,1)S(1)} %collective-permute-done.2.refs_3_), channel_id=1, source_target_pairs={{0,8},{8,16},{16,24},{24,28},{28,20},{20,12},{12,4},{4,0},{1,9},{9... | collective-permute-start | bytes 368648 | tf_op jit(solution)/shard_map/ppermute | solution.py:584
  20.1 4.9 %collective-permute-start.6 = (bf16[96,640]{1,0:T(8,128)(2,1)S(1)}, bf16[96,640]{1,0:T(8,128)(2,1)S(1)}, u32[]{:S(2)}, u32[]{:S(2)}) collective-permute-start(bf16[96,640]{1,0:T(8,128)(2,1)S(1)} %collective-permute-done.3.refs_7_), channel_id=1, source_target_pairs={{8,0},{16,8},{24,16},{28,24},{20,28},{12,20},{4,12},{0,4},{9,1},{1... | collective-permute-start | bytes 368648 | tf_op jit(solution)/shard_map/ppermute | solution.py:588
  20.7 6.0 %collective-permute-start.8 = (bf16[96,1152]{1,0:T(8,128)(2,1)S(1)}, bf16[96,1152]{1,0:T(8,128)(2,1)S(1)}, u32[]{:S(2)}, u32[]{:S(2)}) collective-permute-start(bf16[96,1152]{1,0:T(8,128)(2,1)S(1)} %join.1.refs_0_), channel_id=1, source_target_pairs={{0,8},{8,16},{16,24},{24,28},{28,20},{20,12},{12,4},{4,0},{1,9},{9... | collective-permute-start | bytes 663560 | tf_op jit(solution)/shard_map/ppermute | solution.py:584
  22.3 5.9 %collective-permute-start.9 = (bf16[96,1152]{1,0:T(8,128)(2,1)S(1)}, bf16[96,1152]{1,0:T(8,128)(2,1)S(1)}, u32[]{:S(2)}, u32[]{:S(2)}) collective-permute-start(bf16[96,1152]{1,0:T(8,128)(2,1)S(1)} %join.1.refs_0_), channel_id=1, source_target_pairs={{8,0},{16,8},{24,16},{28,24},{20,28},{12,20},{4,12},{0,4},{9,1},{1... | collective-permute-start | bytes 663560 | tf_op jit(solution)/shard_map/ppermute | solution.py:588
  23.7 9.8 %collective-permute-start.11 = (bf16[192,1024]{1,0:T(8,128)(2,1)S(1)}, bf16[192,1024]{1,0:T(8,128)(2,1)S(1)}, u32[]{:S(2)}, u32[]{:S(2)}) collective-permute-start(bf16[192,1024]{1,0:T(8,128)(2,1)S(1)} %bitcast.11), channel_id=1, source_target_pairs={{0,1},{1,0},{2,3},{3,2},{4,5},{5,4},{6,7},{7,6},{8,9},{9,8},{10,11... | collective-permute-start | bytes 1179656 | tf_op jit(solution)/shard_map/ppermute | solution.py:568
  25.0 4.9 %collective-permute-start.7 = (bf16[96,640]{1,0:T(8,128)(2,1)S(1)}, bf16[96,640]{1,0:T(8,128)(2,1)S(1)}, u32[]{:S(2)}, u32[]{:S(2)}) collective-permute-start(bf16[96,640]{1,0:T(8,128)(2,1)S(1)} %collective-permute-done.5.refs_4_), channel_id=1, source_target_pairs={{0,8},{8,16},{16,24},{24,28},{28,20},{20,12},{12,4},{4,0},{1,9},{9... | collective-permute-start | bytes 368648 | tf_op jit(solution)/shard_map/ppermute | solution.py:584
  29.9 6.5 %collective-permute-start.12 = (bf16[192,1024]{1,0:T(8,128)(2,1)S(1)}, bf16[192,1024]{1,0:T(8,128)(2,1)S(1)}, u32[]{:S(2)}, u32[]{:S(2)}) collective-permute-start(bf16[192,1024]{1,0:T(8,128)(2,1)S(1)} %collective-permute-done.10.refs_4_), channel_id=1, source_target_pairs={{0,1},{1,0},{2,3},{3,2},{4,5},{5,4},{6,7},{7,6},{8,9},{9,8},{10,11... | collective-permute-start | bytes 1179656 | tf_op jit(solution)/shard_map/ppermute | solution.py:568
  29.9 12.3 %collective-permute-start.13 = (bf16[96,1152]{1,0:T(8,128)(2,1)S(1)}, bf16[96,1152]{1,0:T(8,128)(2,1)S(1)}, u32[]{:S(2)}, u32[]{:S(2)}) collective-permute-start(bf16[96,1152]{1,0:T(8,128)(2,1)S(1)} %collective-permute-done.8.refs_1_), channel_id=1, source_target_pairs={{0,8},{8,16},{16,24},{24,28},{28,20},{20,12},{12,4},{4,0},{1,9},{9... | collective-permute-start | bytes 663560 | tf_op jit(solution)/shard_map/ppermute | solution.py:584
  31.5 10.8 %collective-permute-start.14 = (bf16[96,1152]{1,0:T(8,128)(2,1)S(1)}, bf16[96,1152]{1,0:T(8,128)(2,1)S(1)}, u32[]{:S(2)}, u32[]{:S(2)}) collective-permute-start(bf16[96,1152]{1,0:T(8,128)(2,1)S(1)} %collective-permute-done.9.refs_5_), channel_id=1, source_target_pairs={{8,0},{16,8},{24,16},{28,24},{20,28},{12,20},{4,12},{0,4},{9,1},{1... | collective-permute-start | bytes 663560 | tf_op jit(solution)/shard_map/ppermute | solution.py:588
  32.0 8.9 %collective-permute-start.15 = (bf16[96,768]{1,0:T(8,128)(2,1)S(1)}, bf16[96,768]{1,0:T(8,128)(2,1)S(1)}, u32[]{:S(2)}, u32[]{:S(2)}) collective-permute-start(bf16[96,768]{1,0:T(8,128)(2,1)S(1)} %copy-done.15), channel_id=1, source_target_pairs={{0,8},{8,16},{16,24},{24,28},{28,20},{20,12},{12,4},{4,0},{1,9},{9... | collective-permute-start | bytes 442376 | tf_op jit(solution)/shard_map/ppermute | solution.py:584
  33.5 8.7 %collective-permute-start.16 = (bf16[96,768]{1,0:T(8,128)(2,1)S(1)}, bf16[96,768]{1,0:T(8,128)(2,1)S(1)}, u32[]{:S(2)}, u32[]{:S(2)}) collective-permute-start(bf16[96,768]{1,0:T(8,128)(2,1)S(1)} %copy-done.15), channel_id=1, source_target_pairs={{8,0},{16,8},{24,16},{28,24},{20,28},{12,20},{4,12},{0,4},{9,1},{1... | collective-permute-start | bytes 442376 | tf_op jit(solution)/shard_map/ppermute | solution.py:588
  42.3 11.3 %collective-permute-start.18 = (bf16[96,1152]{1,0:T(8,128)(2,1)S(1)}, bf16[96,1152]{1,0:T(8,128)(2,1)S(1)}, u32[]{:S(2)}, u32[]{:S(2)}) collective-permute-start(bf16[96,1152]{1,0:T(8,128)(2,1)S(1)} %collective-permute-done.13.refs_2_), channel_id=1, source_target_pairs={{0,8},{8,16},{16,24},{24,28},{28,20},{20,12},{12,4},{4,0},{1,9},{9... | collective-permute-start | bytes 663560 | tf_op jit(solution)/shard_map/ppermute | solution.py:584
  44.0 9.6 %collective-permute-start.19 = (bf16[96,1152]{1,0:T(8,128)(2,1)S(1)}, bf16[96,1152]{1,0:T(8,128)(2,1)S(1)}, u32[]{:S(2)}, u32[]{:S(2)}) collective-permute-start(bf16[96,1152]{1,0:T(8,128)(2,1)S(1)} %collective-permute-done.14.refs_6_), channel_id=1, source_target_pairs={{8,0},{16,8},{24,16},{28,24},{20,28},{12,20},{4,12},{0,4},{9,1},{1... | collective-permute-start | bytes 663560 | tf_op jit(solution)/shard_map/ppermute | solution.py:588
  44.3 9.3 %collective-permute-start.22 = (bf16[512,192]{1,0:T(8,128)(2,1)S(1)}, bf16[512,192]{1,0:T(8,128)(2,1)S(1)}, u32[]{:S(2)}, u32[]{:S(2)}) collective-permute-start(bf16[512,192]{1,0:T(8,128)(2,1)S(1)} %get-tuple-element.241.c0.refs_4_), channel_id=1, source_target_pairs={{0,2},{1,3},{2,0},{3,1},{4,6},{5,7},{6,4},{7,5},{8,10},{9,11},{10,... | collective-permute-start | bytes 589832 | tf_op jit(solution)/shard_map/ppermute | solution.py:572
  44.7 7.5 %collective-permute-start.20 = (bf16[96,768]{1,0:T(8,128)(2,1)S(1)}, bf16[96,768]{1,0:T(8,128)(2,1)S(1)}, u32[]{:S(2)}, u32[]{:S(2)}) collective-permute-start(bf16[96,768]{1,0:T(8,128)(2,1)S(1)} %collective-permute-done.15.refs_1_), channel_id=1, source_target_pairs={{0,8},{8,16},{16,24},{24,28},{28,20},{20,12},{12,4},{4,0},{1,9},{9... | collective-permute-start | bytes 442376 | tf_op jit(solution)/shard_map/ppermute | solution.py:584
  46.2 7.3 %collective-permute-start.21 = (bf16[96,768]{1,0:T(8,128)(2,1)S(1)}, bf16[96,768]{1,0:T(8,128)(2,1)S(1)}, u32[]{:S(2)}, u32[]{:S(2)}) collective-permute-start(bf16[96,768]{1,0:T(8,128)(2,1)S(1)} %collective-permute-done.16.refs_5_), channel_id=1, source_target_pairs={{8,0},{16,8},{24,16},{28,24},{20,28},{12,20},{4,12},{0,4},{9,1},{1... | collective-permute-start | bytes 442376 | tf_op jit(solution)/shard_map/ppermute | solution.py:588
  53.6 8.9 %collective-permute-start.25 = (bf16[96,1152]{1,0:T(8,128)(2,1)S(1)}, bf16[96,1152]{1,0:T(8,128)(2,1)S(1)}, u32[]{:S(2)}, u32[]{:S(2)}) collective-permute-start(bf16[96,1152]{1,0:T(8,128)(2,1)S(1)} %collective-permute-done.18.refs_3_), channel_id=1, source_target_pairs={{0,8},{8,16},{16,24},{24,28},{28,20},{20,12},{12,4},{4,0},{1,9},{9... | collective-permute-start | bytes 663560 | tf_op jit(solution)/shard_map/ppermute | solution.py:584
  54.6 7.8 %collective-permute-start.24 = (bf16[512,192]{1,0:T(8,128)(2,1)S(1)}, bf16[512,192]{1,0:T(8,128)(2,1)S(1)}, u32[]{:S(2)}, u32[]{:S(2)}) collective-permute-start(bf16[512,192]{1,0:T(8,128)(2,1)S(1)} %get-tuple-element.253.c0.refs_5_), channel_id=1, source_target_pairs={{0,2},{1,3},{2,0},{3,1},{4,6},{5,7},{6,4},{7,5},{8,10},{9,11},{10,... | collective-permute-start | bytes 589832 | tf_op jit(solution)/shard_map/ppermute | solution.py:572
  54.9 7.4 %collective-permute-start.26 = (bf16[96,768]{1,0:T(8,128)(2,1)S(1)}, bf16[96,768]{1,0:T(8,128)(2,1)S(1)}, u32[]{:S(2)}, u32[]{:S(2)}) collective-permute-start(bf16[96,768]{1,0:T(8,128)(2,1)S(1)} %collective-permute-done.20.refs_2_), channel_id=1, source_target_pairs={{0,8},{8,16},{16,24},{24,28},{28,20},{20,12},{12,4},{4,0},{1,9},{9... | collective-permute-start | bytes 442376 | tf_op jit(solution)/shard_map/ppermute | solution.py:584
  55.5 6.9 %collective-permute-start.27 = (bf16[96,768]{1,0:T(8,128)(2,1)S(1)}, bf16[96,768]{1,0:T(8,128)(2,1)S(1)}, u32[]{:S(2)}, u32[]{:S(2)}) collective-permute-start(bf16[96,768]{1,0:T(8,128)(2,1)S(1)} %collective-permute-done.21.refs_6_), channel_id=1, source_target_pairs={{8,0},{16,8},{24,16},{28,24},{20,28},{12,20},{4,12},{0,4},{9,1},{1... | collective-permute-start | bytes 442376 | tf_op jit(solution)/shard_map/ppermute | solution.py:588
  56.9 7.1 %collective-permute-start.17 = (bf16[512,192]{1,0:T(8,128)(2,1)S(1)}, bf16[512,192]{1,0:T(8,128)(2,1)S(1)}, u32[]{:S(2)}, u32[]{:S(2)}) collective-permute-start(bf16[512,192]{1,0:T(8,128)(2,1)S(1)} %get-tuple-element.241.c0.refs_4_), channel_id=1, source_target_pairs={{0,1},{1,0},{2,3},{3,2},{4,5},{5,4},{6,7},{7,6},{8,9},{9,8},{10,11... | collective-permute-start | bytes 589832 | tf_op jit(solution)/shard_map/ppermute | solution.py:568
  62.3 1.7 %collective-permute-start.23 = (bf16[512,192]{1,0:T(8,128)(2,1)S(1)}, bf16[512,192]{1,0:T(8,128)(2,1)S(1)}, u32[]{:S(2)}, u32[]{:S(2)}) collective-permute-start(bf16[512,192]{1,0:T(8,128)(2,1)S(1)} %collective-permute-done.22.c2), channel_id=1, source_target_pairs={{0,1},{1,0},{2,3},{3,2},{4,5},{5,4},{6,7},{7,6},{8,9},{9,8},{10,11... | collective-permute-start | bytes 589832 | tf_op jit(solution)/shard_map/ppermute | solution.py:568
  62.9 2.3 %collective-permute-start.29 = (bf16[192,768]{1,0:T(8,128)(2,1)S(1)}, bf16[192,768]{1,0:T(8,128)(2,1)S(1)}, u32[]{:S(2)}, u32[]{:S(2)}) collective-permute-start(bf16[192,768]{1,0:T(8,128)(2,1)S(1)} %get-tuple-element.262.w2), channel_id=1, source_target_pairs={{0,1},{1,0},{2,3},{3,2},{4,5},{5,4},{6,7},{7,6},{8,9},{9,8},{10,11... | collective-permute-start | bytes 884744 | tf_op jit(solution)/shard_map/ppermute | solution.py:568
  63.4 1.7 %collective-permute-start.28 = (bf16[192,768]{1,0:T(8,128)(2,1)S(1)}, bf16[192,768]{1,0:T(8,128)(2,1)S(1)}, u32[]{:S(2)}, u32[]{:S(2)}) collective-permute-start(bf16[192,768]{1,0:T(8,128)(2,1)S(1)} %get-tuple-element.261.w0.refs_7_.refs_4_), channel_id=1, source_target_pairs={{0,1},{1,0},{2,3},{3,2},{4,5},{5,4},{6,7},{7,6},{8,9},{9,8},{10,11... | collective-permute-start | bytes 884744 | tf_op jit(solution)/shard_map/ppermute | solution.py:568
  63.5 5.1 %collective-permute-start.30 = (bf16[512,192]{1,0:T(8,128)(2,1)S(1)}, bf16[512,192]{1,0:T(8,128)(2,1)S(1)}, u32[]{:S(2)}, u32[]{:S(2)}) collective-permute-start(bf16[512,192]{1,0:T(8,128)(2,1)S(1)} %get-tuple-element.253.c0.refs_5_), channel_id=1, source_target_pairs={{0,1},{1,0},{2,3},{3,2},{4,5},{5,4},{6,7},{7,6},{8,9},{9,8},{10,11... | collective-permute-start | bytes 589832 | tf_op jit(solution)/shard_map/ppermute | solution.py:568
  63.9 4.6 %collective-permute-start.31 = (bf16[512,192]{1,0:T(8,128)(2,1)S(1)}, bf16[512,192]{1,0:T(8,128)(2,1)S(1)}, u32[]{:S(2)}, u32[]{:S(2)}) collective-permute-start(bf16[512,192]{1,0:T(8,128)(2,1)S(1)} %collective-permute-done.24.c2), channel_id=1, source_target_pairs={{0,1},{1,0},{2,3},{3,2},{4,5},{5,4},{6,7},{7,6},{8,9},{9,8},{10,11... | collective-permute-start | bytes 589832 | tf_op jit(solution)/shard_map/ppermute | solution.py:568
  64.0 7.9 %collective-permute-start.32 = (bf16[96,768]{1,0:T(8,128)(2,1)S(1)}, bf16[96,768]{1,0:T(8,128)(2,1)S(1)}, u32[]{:S(2)}, u32[]{:S(2)}) collective-permute-start(bf16[96,768]{1,0:T(8,128)(2,1)S(1)} %collective-permute-done.26.refs_3_), channel_id=1, source_target_pairs={{0,8},{8,16},{16,24},{24,28},{28,20},{20,12},{12,4},{4,0},{1,9},{9... | collective-permute-start | bytes 442376 | tf_op jit(solution)/shard_map/ppermute | solution.py:584
  74.0 2.5 %collective-permute-start.33 = (bf16[128,768]{1,0:T(8,128)(2,1)S(1)}, bf16[128,768]{1,0:T(8,128)(2,1)S(1)}, u32[]{:S(2)}, u32[]{:S(2)}) collective-permute-start(bf16[128,768]{1,0:T(8,128)(2,1)S(1)} %get-tuple-element.284), channel_id=1, source_target_pairs={{0,1},{1,0},{2,3},{3,2},{4,5},{5,4},{6,7},{7,6},{8,9},{9,8},{10,11... | collective-permute-start | bytes 589832 | tf_op jit(solution)/shard_map/ppermute | solution.py:568
  74.3 2.2 %collective-permute-start.34 = (bf16[128,768]{1,0:T(8,128)(2,1)S(1)}, bf16[128,768]{1,0:T(8,128)(2,1)S(1)}, u32[]{:S(2)}, u32[]{:S(2)}) collective-permute-start(bf16[128,768]{1,0:T(8,128)(2,1)S(1)} %get-tuple-element.285), channel_id=1, source_target_pairs={{0,1},{1,0},{2,3},{3,2},{4,5},{5,4},{6,7},{7,6},{8,9},{9,8},{10,11... | collective-permute-start | bytes 589832 | tf_op jit(solution)/shard_map/ppermute | solution.py:568
  76.6 11.3 %collective-permute-start.39 = (bf16[256,768]{1,0:T(8,128)(2,1)S(1)}, bf16[256,768]{1,0:T(8,128)(2,1)S(1)}, u32[]{:S(2)}, u32[]{:S(2)}) collective-permute-start(bf16[256,768]{1,0:T(8,128)(2,1)S(1)} %add0.1.refs_1_), channel_id=1, source_target_pairs={{0,2},{1,3},{2,0},{3,1},{4,6},{5,7},{6,4},{7,5},{8,10},{9,11},{10,... | collective-permute-start | bytes 1179656 | tf_op jit(solution)/shard_map/ppermute | solution.py:572
  77.1 5.7 %collective-permute-start.35 = (bf16[128,768]{1,0:T(8,128)(2,1)S(1)}, bf16[128,768]{1,0:T(8,128)(2,1)S(1)}, u32[]{:S(2)}, u32[]{:S(2)}) collective-permute-start(bf16[128,768]{1,0:T(8,128)(2,1)S(1)} %get-tuple-element.291), channel_id=1, source_target_pairs={{0,1},{1,0},{2,3},{3,2},{4,5},{5,4},{6,7},{7,6},{8,9},{9,8},{10,11... | collective-permute-start | bytes 589832 | tf_op jit(solution)/shard_map/ppermute | solution.py:568
  77.1 5.7 %collective-permute-start.36 = (bf16[128,768]{1,0:T(8,128)(2,1)S(1)}, bf16[128,768]{1,0:T(8,128)(2,1)S(1)}, u32[]{:S(2)}, u32[]{:S(2)}) collective-permute-start(bf16[128,768]{1,0:T(8,128)(2,1)S(1)} %get-tuple-element.292), channel_id=1, source_target_pairs={{0,1},{1,0},{2,3},{3,2},{4,5},{5,4},{6,7},{7,6},{8,9},{9,8},{10,11... | collective-permute-start | bytes 589832 | tf_op jit(solution)/shard_map/ppermute | solution.py:568
  80.7 13.3 %collective-permute-start.37 = (bf16[96,1536]{1,0:T(8,128)(2,1)S(1)}, bf16[96,1536]{1,0:T(8,128)(2,1)S(1)}, u32[]{:S(2)}, u32[]{:S(2)}) collective-permute-start(bf16[96,1536]{1,0:T(8,128)(2,1)S(1)} %get-tuple-element.293), channel_id=1, source_target_pairs={{0,8},{8,16},{16,24},{24,28},{28,20},{20,12},{12,4},{4,0},{1,9},{9... | collective-permute-start | bytes 884744 | tf_op jit(solution)/shard_map/ppermute | solution.py:584
  81.6 12.4 %collective-permute-start.38 = (bf16[96,1536]{1,0:T(8,128)(2,1)S(1)}, bf16[96,1536]{1,0:T(8,128)(2,1)S(1)}, u32[]{:S(2)}, u32[]{:S(2)}) collective-permute-start(bf16[96,1536]{1,0:T(8,128)(2,1)S(1)} %get-tuple-element.294), channel_id=1, source_target_pairs={{8,0},{16,8},{24,16},{28,24},{20,28},{12,20},{4,12},{0,4},{9,1},{1... | collective-permute-start | bytes 884744 | tf_op jit(solution)/shard_map/ppermute | solution.py:588
  88.5 1.7 %collective-permute-start.41 = (bf16[128,768]{1,0:T(8,128)(2,1)S(1)}, bf16[128,768]{1,0:T(8,128)(2,1)S(1)}, u32[]{:S(2)}, u32[]{:S(2)}) collective-permute-start(bf16[128,768]{1,0:T(8,128)(2,1)S(1)} %get-tuple-element.297.refs_4_), channel_id=1, source_target_pairs={{0,1},{1,0},{2,3},{3,2},{4,5},{5,4},{6,7},{7,6},{8,9},{9,8},{10,11... | collective-permute-start | bytes 589832 | tf_op jit(solution)/shard_map/ppermute | solution.py:568
  89.0 11.1 %collective-permute-start.42 = (bf16[256,768]{1,0:T(8,128)(2,1)S(1)}, bf16[256,768]{1,0:T(8,128)(2,1)S(1)}, u32[]{:S(2)}, u32[]{:S(2)}) collective-permute-start(bf16[256,768]{1,0:T(8,128)(2,1)S(1)} %add1.1.refs_1_), channel_id=1, source_target_pairs={{0,2},{1,3},{2,0},{3,1},{4,6},{5,7},{6,4},{7,5},{8,10},{9,11},{10,... | collective-permute-start | bytes 1179656 | tf_op jit(solution)/shard_map/ppermute | solution.py:572
  95.6 5.1 %collective-permute-start.50 = (bf16[256,768]{1,0:T(8,128)(2,1)S(1)}, bf16[256,768]{1,0:T(8,128)(2,1)S(1)}, u32[]{:S(2)}, u32[]{:S(2)}) collective-permute-start(bf16[256,768]{1,0:T(8,128)(2,1)S(1)} %get-tuple-element.304), channel_id=1, source_target_pairs={{0,1},{1,0},{2,3},{3,2},{4,5},{5,4},{6,7},{7,6},{8,9},{9,8},{10,11... | collective-permute-start | bytes 1179656 | tf_op jit(solution)/shard_map/ppermute | solution.py:568
  95.9 5.3 %collective-permute-start.49 = (bf16[256,768]{1,0:T(8,128)(2,1)S(1)}, bf16[256,768]{1,0:T(8,128)(2,1)S(1)}, u32[]{:S(2)}, u32[]{:S(2)}) collective-permute-start(bf16[256,768]{1,0:T(8,128)(2,1)S(1)} %get-tuple-element.302), channel_id=1, source_target_pairs={{0,1},{1,0},{2,3},{3,2},{4,5},{5,4},{6,7},{7,6},{8,9},{9,8},{10,11... | collective-permute-start | bytes 1179656 | tf_op jit(solution)/shard_map/ppermute | solution.py:568
  96.4 9.6 %collective-permute-start.45 = (bf16[96,1536]{1,0:T(8,128)(2,1)S(1)}, bf16[96,1536]{1,0:T(8,128)(2,1)S(1)}, u32[]{:S(2)}, u32[]{:S(2)}) collective-permute-start(bf16[96,1536]{1,0:T(8,128)(2,1)S(1)} %get-tuple-element.315), channel_id=1, source_target_pairs={{0,8},{8,16},{16,24},{24,28},{28,20},{20,12},{12,4},{4,0},{1,9},{9... | collective-permute-start | bytes 884744 | tf_op jit(solution)/shard_map/ppermute | solution.py:584
  97.4 8.9 %collective-permute-start.46 = (bf16[96,1536]{1,0:T(8,128)(2,1)S(1)}, bf16[96,1536]{1,0:T(8,128)(2,1)S(1)}, u32[]{:S(2)}, u32[]{:S(2)}) collective-permute-start(bf16[96,1536]{1,0:T(8,128)(2,1)S(1)} %get-tuple-element.316), channel_id=1, source_target_pairs={{8,0},{16,8},{24,16},{28,24},{20,28},{12,20},{4,12},{0,4},{9,1},{1... | collective-permute-start | bytes 884744 | tf_op jit(solution)/shard_map/ppermute | solution.py:588
  101.5 16.5 %collective-permute-start.51 = (bf16[256,768]{1,0:T(8,128)(2,1)S(1)}, bf16[256,768]{1,0:T(8,128)(2,1)S(1)}, u32[]{:S(2)}, u32[]{:S(2)}) collective-permute-start(bf16[256,768]{1,0:T(8,128)(2,1)S(1)} %get-tuple-element.338), channel_id=1, source_target_pairs={{0,2},{1,3},{2,0},{3,1},{4,6},{5,7},{6,4},{7,5},{8,10},{9,11},{10,... | collective-permute-start | bytes 1179656 | tf_op jit(solution)/shard_map/ppermute | solution.py:572
  106.5 11.6 %collective-permute-start.48 = (bf16[96,1536]{1,0:T(8,128)(2,1)S(1)}, bf16[96,1536]{1,0:T(8,128)(2,1)S(1)}, u32[]{:S(2)}, u32[]{:S(2)}) collective-permute-start(bf16[96,1536]{1,0:T(8,128)(2,1)S(1)} %get-tuple-element.331), channel_id=1, source_target_pairs={{8,0},{16,8},{24,16},{28,24},{20,28},{12,20},{4,12},{0,4},{9,1},{1... | collective-permute-start | bytes 884744 | tf_op jit(solution)/shard_map/ppermute | solution.py:588
  107.6 10.5 %collective-permute-start.47 = (bf16[96,1536]{1,0:T(8,128)(2,1)S(1)}, bf16[96,1536]{1,0:T(8,128)(2,1)S(1)}, u32[]{:S(2)}, u32[]{:S(2)}) collective-permute-start(bf16[96,1536]{1,0:T(8,128)(2,1)S(1)} %get-tuple-element.320), channel_id=1, source_target_pairs={{0,8},{8,16},{16,24},{24,28},{28,20},{20,12},{12,4},{4,0},{1,9},{9... | collective-permute-start | bytes 884744 | tf_op jit(solution)/shard_map/ppermute | solution.py:584
  114.8 6.4 %collective-permute-start.54 = (bf16[256,768]{1,0:T(8,128)(2,1)S(1)}, bf16[256,768]{1,0:T(8,128)(2,1)S(1)}, u32[]{:S(2)}, u32[]{:S(2)}) collective-permute-start(bf16[256,768]{1,0:T(8,128)(2,1)S(1)} %get-tuple-element.342), channel_id=1, source_target_pairs={{0,1},{1,0},{2,3},{3,2},{4,5},{5,4},{6,7},{7,6},{8,9},{9,8},{10,11... | collective-permute-start | bytes 1179656 | tf_op jit(solution)/shard_map/ppermute | solution.py:568
  114.8 7.3 %collective-permute-start.55 = (bf16[256,768]{1,0:T(8,128)(2,1)S(1)}, bf16[256,768]{1,0:T(8,128)(2,1)S(1)}, u32[]{:S(2)}, u32[]{:S(2)}) collective-permute-start(bf16[256,768]{1,0:T(8,128)(2,1)S(1)} %get-tuple-element.343), channel_id=1, source_target_pairs={{0,1},{1,0},{2,3},{3,2},{4,5},{5,4},{6,7},{7,6},{8,9},{9,8},{10,11... | collective-permute-start | bytes 1179656 | tf_op jit(solution)/shard_map/ppermute | solution.py:568
  118.0 7.3 %collective-permute-start.52 = (bf16[96,896]{1,0:T(8,128)(2,1)S(1)}, bf16[96,896]{1,0:T(8,128)(2,1)S(1)}, u32[]{:S(2)}, u32[]{:S(2)}) collective-permute-start(bf16[96,896]{1,0:T(8,128)(2,1)S(1)} %get-tuple-element.339), channel_id=1, source_target_pairs={{0,8},{8,16},{16,24},{24,28},{28,20},{20,12},{12,4},{4,0},{1,9},{9... | collective-permute-start | bytes 516104 | tf_op jit(solution)/shard_map/ppermute | solution.py:584
  119.0 6.4 %collective-permute-start.53 = (bf16[96,896]{1,0:T(8,128)(2,1)S(1)}, bf16[96,896]{1,0:T(8,128)(2,1)S(1)}, u32[]{:S(2)}, u32[]{:S(2)}) collective-permute-start(bf16[96,896]{1,0:T(8,128)(2,1)S(1)} %get-tuple-element.340), channel_id=1, source_target_pairs={{8,0},{16,8},{24,16},{28,24},{20,28},{12,20},{4,12},{0,4},{9,1},{1... | collective-permute-start | bytes 516104 | tf_op jit(solution)/shard_map/ppermute | solution.py:588
  120.2 11.4 %collective-permute-start.58 = (bf16[96,1536]{1,0:T(8,128)(2,1)S(1)}, bf16[96,1536]{1,0:T(8,128)(2,1)S(1)}, u32[]{:S(2)}, u32[]{:S(2)}) collective-permute-start(bf16[96,1536]{1,0:T(8,128)(2,1)S(1)} %mlp_hop1.1), channel_id=1, source_target_pairs={{0,8},{8,16},{16,24},{24,28},{28,20},{20,12},{12,4},{4,0},{1,9},{9... | collective-permute-start | bytes 884744 | tf_op jit(solution)/shard_map/ppermute | solution.py:584
  121.1 17.2 %collective-permute-start.62 = (bf16[192,1024]{1,0:T(8,128)(2,1)S(1)}, bf16[192,1024]{1,0:T(8,128)(2,1)S(1)}, u32[]{:S(2)}, u32[]{:S(2)}) collective-permute-start(bf16[192,1024]{1,0:T(8,128)(2,1)S(1)} %get-tuple-element.368.refs_1_), channel_id=1, source_target_pairs={{0,2},{1,3},{2,0},{3,1},{4,6},{5,7},{6,4},{7,5},{8,10},{9,11},{10,... | collective-permute-start | bytes 1179656 | tf_op jit(solution)/shard_map/ppermute | solution.py:572
  122.4 17.5 %collective-permute-start.61 = (bf16[256,768]{1,0:T(8,128)(2,1)S(1)}, bf16[256,768]{1,0:T(8,128)(2,1)S(1)}, u32[]{:S(2)}, u32[]{:S(2)}) collective-permute-start(bf16[256,768]{1,0:T(8,128)(2,1)S(1)} %get-tuple-element.344), channel_id=1, source_target_pairs={{0,2},{1,3},{2,0},{3,1},{4,6},{5,7},{6,4},{7,5},{8,10},{9,11},{10,... | collective-permute-start | bytes 1179656 | tf_op jit(solution)/shard_map/ppermute | solution.py:572
  125.4 9.0 %collective-permute-start.56 = (bf16[96,896]{1,0:T(8,128)(2,1)S(1)}, bf16[96,896]{1,0:T(8,128)(2,1)S(1)}, u32[]{:S(2)}, u32[]{:S(2)}) collective-permute-start(bf16[96,896]{1,0:T(8,128)(2,1)S(1)} %get-tuple-element.347), channel_id=1, source_target_pairs={{0,8},{8,16},{16,24},{24,28},{28,20},{20,12},{12,4},{4,0},{1,9},{9... | collective-permute-start | bytes 516104 | tf_op jit(solution)/shard_map/ppermute | solution.py:584
  126.4 8.1 %collective-permute-start.57 = (bf16[96,896]{1,0:T(8,128)(2,1)S(1)}, bf16[96,896]{1,0:T(8,128)(2,1)S(1)}, u32[]{:S(2)}, u32[]{:S(2)}) collective-permute-start(bf16[96,896]{1,0:T(8,128)(2,1)S(1)} %get-tuple-element.348), channel_id=1, source_target_pairs={{8,0},{16,8},{24,16},{28,24},{20,28},{12,20},{4,12},{0,4},{9,1},{1... | collective-permute-start | bytes 516104 | tf_op jit(solution)/shard_map/ppermute | solution.py:588
  134.6 5.6 %collective-permute-start.59 = (bf16[96,896]{1,0:T(8,128)(2,1)S(1)}, bf16[96,896]{1,0:T(8,128)(2,1)S(1)}, u32[]{:S(2)}, u32[]{:S(2)}) collective-permute-start(bf16[96,896]{1,0:T(8,128)(2,1)S(1)} %get-tuple-element.355), channel_id=1, source_target_pairs={{0,8},{8,16},{16,24},{24,28},{28,20},{20,12},{12,4},{4,0},{1,9},{9... | collective-permute-start | bytes 516104 | tf_op jit(solution)/shard_map/ppermute | solution.py:584
  135.5 5.4 %collective-permute-start.60 = (bf16[96,896]{1,0:T(8,128)(2,1)S(1)}, bf16[96,896]{1,0:T(8,128)(2,1)S(1)}, u32[]{:S(2)}, u32[]{:S(2)}) collective-permute-start(bf16[96,896]{1,0:T(8,128)(2,1)S(1)} %get-tuple-element.356), channel_id=1, source_target_pairs={{8,0},{16,8},{24,16},{28,24},{20,28},{12,20},{4,12},{0,4},{9,1},{1... | collective-permute-start | bytes 516104 | tf_op jit(solution)/shard_map/ppermute | solution.py:588
  140.9 2.9 %collective-permute-start.64 = (bf16[192,1024]{1,0:T(8,128)(2,1)S(1)}, bf16[192,1024]{1,0:T(8,128)(2,1)S(1)}, u32[]{:S(2)}, u32[]{:S(2)}) collective-permute-start(bf16[192,1024]{1,0:T(8,128)(2,1)S(1)} %get-tuple-element.368.refs_1_), channel_id=1, source_target_pairs={{0,1},{1,0},{2,3},{3,2},{4,5},{5,4},{6,7},{7,6},{8,9},{9,8},{10,11... | collective-permute-start | bytes 1179656 | tf_op jit(solution)/shard_map/ppermute | solution.py:568
  140.9 2.9 %collective-permute-start.65 = (bf16[192,1024]{1,0:T(8,128)(2,1)S(1)}, bf16[192,1024]{1,0:T(8,128)(2,1)S(1)}, u32[]{:S(2)}, u32[]{:S(2)}) collective-permute-start(bf16[192,1024]{1,0:T(8,128)(2,1)S(1)} %collective-permute-done.62.refs_3_), channel_id=1, source_target_pairs={{0,1},{1,0},{2,3},{3,2},{4,5},{5,4},{6,7},{7,6},{8,9},{9,8},{10,11... | collective-permute-start | bytes 1179656 | tf_op jit(solution)/shard_map/ppermute | solution.py:568
  141.5 6.3 %collective-permute-start.63 = (bf16[96,896]{1,0:T(8,128)(2,1)S(1)}, bf16[96,896]{1,0:T(8,128)(2,1)S(1)}, u32[]{:S(2)}, u32[]{:S(2)}) collective-permute-start(bf16[96,896]{1,0:T(8,128)(2,1)S(1)} %qkv_hop1.1), channel_id=1, source_target_pairs={{0,8},{8,16},{16,24},{24,28},{28,20},{20,12},{12,4},{4,0},{1,9},{9... | collective-permute-start | bytes 516104 | tf_op jit(solution)/shard_map/ppermute | solution.py:584
  149.1 3.6 %collective-permute-start.67 = (f32[8,128]{1,0:T(8,128)S(1)}, f32[8,128]{1,0:T(8,128)S(1)}, u32[]{:S(2)}, u32[]{:S(2)}) collective-permute-start(f32[8,128]{1,0:T(8,128)S(1)} %sum.1.sums), channel_id=1, source_target_pairs={{0,2},{1,3},{2,0},{3,1},{4,6},{5,7},{6,4},{7,5},{8,10},{9,11},{10,... | collective-permute-start | bytes 12296 | tf_op jit(solution)/shard_map/ppermute | solution.py:572
  (28 other events, 191.4 us)
